TPU v7x, 256 devices: a whole 4x4x8 slice. The times are simulated.
256 devices in a mesh: grid: 64 (over x_hi, y, z), vis: 4 (over x_lo, core).
Axes of the slice: x: 4 (x_hi: 2, x_lo: 2; x = x_hi * 2 + x_lo), y: 4, z: 8, core: 2. Of those that a mesh axis runs over, the one named last changes fastest.
Arguments:
- vis_coords: float32 [64, 256, 2, 512], P('grid', 'vis'), may hold values from 0 to 64
- vis_values: float32 [64, 256, 2, 512], P('grid', 'vis'), may hold values from -6 to 6
- tile_index: int32 [64, 256], P('grid', 'vis'), may hold values from 0 to 63
Outputs:
- facets: float32 [64, 2, 1024, 1024], P('grid', None, 'vis')
Inputs may be any that keep to these rules, and one draw needn't show every extreme that they name: `tile_index`: tile a * 8 + e covers subgrid rows from a * 64 and columns from e * 64.
All inputs are finite; a program needn't handle non-finite values.
Results may differ from a plain program's by a relative error of at most 0.014.
Values may be sent and summed in bfloat16 or wider, within the bound.
No kernel may reach another device: no remote copies, remote signals or barrier semaphores. Data moves between devices by JAX's collectives and lax.ppermute only.
A program may use at most 64 MiB of HBM per device.

v0:
```python
import functools
import math

import jax
import jax.numpy as jnp
import ml_dtypes
import numpy as np
from jax import lax
from jax.experimental import pallas as pl
from jax.experimental.pallas import tpu as pltpu
from jax.sharding import PartitionSpec as P

SUB = 512
FAC = 1024
CONTRIB = 64
TILE = 64
BLK = 512
BLOCKS = 64
NBLK = 8
LANES = 128
QUARTER = 16
ROWS = NBLK * QUARTER
ROWS_OUT = FAC // 4
WIDTH = 2 * SUB
UNITARY = 1.0 / math.sqrt(SUB)
BF16 = jnp.bfloat16
F32 = jnp.float32


def angles(first, second, length):
    return (first[:, None] * second[None, :] % length) * (2.0 * math.pi / length)


def as_bf16(table):
    return np.ascontiguousarray(table.astype(np.float32)).astype(ml_dtypes.bfloat16)


@functools.lru_cache(maxsize=None)
def tables():
    spectrum = np.arange(SUB)
    turn = angles(spectrum, spectrum, SUB).reshape(NBLK, TILE, NBLK, CONTRIB)
    cos, sin = np.cos(turn), np.sin(turn)
    columns = np.empty((NBLK, 2, TILE, NBLK, 2, CONTRIB))
    columns[:, 0, :, :, 0] = cos
    columns[:, 1, :, :, 0] = sin
    columns[:, 0, :, :, 1] = -sin
    columns[:, 1, :, :, 1] = cos
    columns = as_bf16(columns.reshape(WIDTH, WIDTH))
    turn = angles(spectrum, spectrum, SUB)
    rows = np.concatenate([np.cos(turn), np.sin(turn)], 1)
    rows = rows.reshape(NBLK, 2, 2, QUARTER, WIDTH).transpose(2, 1, 0, 3, 4)
    rows = as_bf16(rows.reshape(SUB, WIDTH))
    turn = angles(np.arange(FAC), spectrum, FAC).reshape(4, ROWS_OUT, NBLK, 4, QUARTER)
    parts = np.stack([np.cos(turn), np.sin(turn)], 2)
    left = np.empty((4, ROWS_OUT, 4, 2, NBLK, QUARTER))
    for g in range(4):
        for j in range(4):
            left[g, :, j] = parts[g, :, :, :, g ^ j]
    left = as_bf16(left.reshape(4, ROWS_OUT, WIDTH))
    turn = angles(spectrum, np.arange(FAC), FAC).reshape(NBLK, CONTRIB, FAC)
    cos, sin = np.cos(turn), np.sin(turn)
    right = np.empty((NBLK, 2, CONTRIB, 2, FAC))
    right[:, 0, :, 0] = cos
    right[:, 1, :, 0] = -sin
    right[:, 0, :, 1] = sin
    right[:, 1, :, 1] = cos
    right = right.reshape(WIDTH, 4, FAC // 2).transpose(1, 0, 2)
    right = as_bf16(right)
    sines = np.sin(math.pi * (np.arange(FAC) + 0.5) / FAC)
    taper = 0.25 + 0.75 * sines * sines
    taper_rows = np.broadcast_to(taper.reshape(4, ROWS_OUT, 1), (4, ROWS_OUT, LANES)).astype(np.float32)
    taper_cols = (taper / math.sqrt(SUB)).reshape(2, 1, FAC // 2).astype(np.float32)
    pixel = np.arange(TILE)
    bell = (1.0 - 2.0 * (pixel % 2)) * np.exp(-(pixel * pixel) / 256.0)
    bell = (bell[:, None] * np.concatenate([bell, bell])[None, :]).astype(np.float32)
    return columns, rows, left, right, np.ascontiguousarray(taper_rows), taper_cols, bell


SINE = [math.pi ** (2 * k + 1) * (-1) ** k / math.factorial(2 * k + 1) for k in range(7)]


def gridding_kernel(
    tile_ref, place_ref, coords_hbm, values_hbm, columns_hbm, rows_hbm, bell_ref,
    send_ref, send_x_ref, keep_ref, keep_x_ref,
    coords, values, whole, offset, step8, slope, height, u_buf, v_buf, acc, grid16, stacked, columns, rows, sems,
):
    in_coords = pltpu.make_async_copy(coords_hbm, coords, sems.at[0])
    in_values = pltpu.make_async_copy(values_hbm, values, sems.at[1])
    in_columns = pltpu.make_async_copy(columns_hbm, columns, sems.at[2])
    in_rows = pltpu.make_async_copy(rows_hbm, rows, sems.at[3])
    in_coords.start()
    in_values.start()
    in_columns.start()
    in_rows.start()
    acc[...] = jnp.zeros_like(acc)
    u_buf[...] = jnp.zeros_like(u_buf)
    v_buf[...] = jnp.zeros_like(v_buf)
    in_coords.wait()
    in_values.wait()

    @pl.loop(0, BLOCKS * 8 // 64)
    def _(chunk):
        at = pl.ds(pl.multiple_of(chunk * 64, 64), 64)
        c = coords[at, :]
        r = jnp.round(c)
        f = c - r
        f = jnp.where(jnp.abs(f) < 1e-20, 1e-20, f)
        square = f * f
        sine = jnp.full_like(f, SINE[6])
        for k in range(5, -1, -1):
            sine = sine * square + SINE[k]
        half = r * 0.5
        odd = half - jnp.floor(half)
        sine = sine * f * ((1.0 - 4.0 * odd) * (1.0 / math.pi))
        whole[at, :] = r
        offset[at, :] = f
        step8[at, :] = jnp.exp(c * (1.0 / 16.0))
        slope[at, :] = c * (1.0 / 128.0)
        height[at, :] = sine * jnp.exp(c * c * (-1.0 / 256.0))

    row_of = lax.broadcasted_iota(jnp.int32, (8, LANES), 0).astype(F32)

    def spread(ref, row):
        return jnp.broadcast_to(ref[pl.ds(row, 1), :], (8, LANES))

    def generate(b, slot):
        for t in range(4):
            lanes = slice(t * LANES, (t + 1) * LANES)
            for axis in range(2):
                row = b * 8 + t * 2 + axis
                base = row_of - spread(whole, row)
                f = spread(offset, row)
                ratio = spread(step8, row)
                w = spread(height, row) * jnp.exp(row_of * spread(slope, row))
                if axis == 0:
                    found = []
                    for a in range(8):
                        inverse = pl.reciprocal((base + 8.0 * a) - f, approx=True)
                        found.append(w * inverse)
                        w = w * ratio
                    u_buf[slot, :, lanes] = jnp.concatenate(found, 0).astype(BF16)
                else:
                    w_real = w * spread(values, b * 8 + t * 2)
                    w_imag = w * spread(values, b * 8 + t * 2 + 1)
                    real, imag = [], []
                    for a in range(8):
                        inverse = pl.reciprocal((base + 8.0 * a) - f, approx=True)
                        real.append(w_real * inverse)
                        imag.append(w_imag * inverse)
                        w_real = w_real * ratio
                        w_imag = w_imag * ratio
                    v_buf[slot, :TILE, lanes] = jnp.concatenate(real, 0).astype(BF16)
                    v_buf[slot, TILE:, lanes] = jnp.concatenate(imag, 0).astype(BF16)

    def deposit(b, slot):
        patch = lax.dot_general(
            u_buf[slot], v_buf[slot], (((1,), (1,)), ((), ())), preferred_element_type=F32
        )
        tile = tile_ref[b]
        at = (
            pl.ds(pl.multiple_of((tile // NBLK) * TILE, TILE), TILE),
            pl.ds(pl.multiple_of((tile % NBLK) * LANES, LANES), LANES),
        )
        acc[at] = acc[at] + patch

    @pl.loop(0, BLOCKS // 2)
    def _(pair):
        deposit(jnp.maximum(pair * 2 - 1, 0), 1)
        generate(pair * 2, 0)
        deposit(pair * 2, 0)
        generate(pair * 2 + 1, 1)

    deposit(BLOCKS - 1, 1)

    bell = bell_ref[...]

    @pl.loop(0, NBLK)
    def _(a):
        at = pl.ds(pl.multiple_of(a * TILE, TILE), TILE)
        for e in range(NBLK):
            lanes = slice(e * LANES, (e + 1) * LANES)
            grid16[at, lanes] = (acc[at, lanes] * bell).astype(BF16)

    in_columns.wait()
    in_rows.wait()
    sign = jnp.where(lax.broadcasted_iota(jnp.int32, (1, LANES), 1) < CONTRIB, 1.0, -1.0)

    @pl.loop(0, WIDTH // 256)
    def _(n):
        at = pl.ds(pl.multiple_of(n * 256, 256), 256)
        images = jnp.dot(grid16[...], columns[:, at], preferred_element_type=F32) * UNITARY
        stacked[:SUB, at] = images.astype(BF16)
        turned = jnp.concatenate(
            [pltpu.roll(images[:, :LANES], CONTRIB, 1) * sign, pltpu.roll(images[:, LANES:], CONTRIB, 1) * sign], 1
        )
        stacked[SUB:, at] = turned.astype(BF16)

    core = place_ref[0] % 2
    side = place_ref[0] // 2
    for half, outs in ((1 - core, (send_ref, send_x_ref)), (core, (keep_ref, keep_x_ref))):
        left = rows[pl.ds(pl.multiple_of(half * 2 * ROWS, 2 * ROWS), 2 * ROWS), :]

        @pl.loop(0, WIDTH // 256)
        def _(n):
            at = pl.ds(pl.multiple_of(n * 256, 256), 256)
            spectra = jnp.dot(left, stacked[:, at], preferred_element_type=F32) * UNITARY
            spectra = spectra.astype(BF16)
            for i in range(2):
                lanes = slice(i * LANES, (i + 1) * LANES)

                @pl.when(side == 0)
                def _():
                    outs[0][n * 2 + i] = spectra[:ROWS, lanes]
                    outs[1][n * 2 + i] = spectra[ROWS:, lanes]

                @pl.when(side == 1)
                def _():
                    outs[1][n * 2 + i] = spectra[:ROWS, lanes]
                    outs[0][n * 2 + i] = spectra[ROWS:, lanes]


def gridding(tile_ids, place, coords, values, columns, rows, bell):
    any_space = pl.BlockSpec(memory_space=pl.ANY)
    scalar = pl.BlockSpec(memory_space=pltpu.SMEM)
    vector = pl.BlockSpec(memory_space=pltpu.VMEM)
    quarter = jax.ShapeDtypeStruct((NBLK, ROWS, LANES), BF16)
    plane = pltpu.VMEM((BLOCKS * 8, LANES), F32)
    return pl.pallas_call(
        gridding_kernel,
        out_shape=[quarter] * 4,
        in_specs=[scalar, scalar, any_space, any_space, any_space, any_space, vector],
        out_specs=[vector] * 4,
        scratch_shapes=[
            plane, plane, plane, plane, plane, plane, plane,
            pltpu.VMEM((2, TILE, BLK), BF16),
            pltpu.VMEM((2, 2 * TILE, BLK), BF16),
            pltpu.VMEM((SUB, WIDTH), F32),
            pltpu.VMEM((SUB, WIDTH), BF16),
            pltpu.VMEM((WIDTH, WIDTH), BF16),
            pltpu.VMEM((WIDTH, WIDTH), BF16),
            pltpu.VMEM((SUB, WIDTH), BF16),
            pltpu.SemaphoreType.DMA((4,)),
        ],
        compiler_params=pltpu.CompilerParams(vmem_limit_bytes=63 * 1024 * 1024),
        name="gridding",
    )(tile_ids, place, coords, values, columns, rows, bell)


def facet_kernel(place_ref, own, by_core, by_x, by_both, left, right, taper_rows, taper_cols, out_ref, stacked, mixture):
    @pl.when(pl.program_id(0) == 0)
    def _():
        sign = jnp.where(lax.broadcasted_iota(jnp.int32, (1, LANES), 1) < CONTRIB, -1.0, 1.0)
        for j, part in enumerate((own, by_core, by_x, by_both)):
            for sb in range(NBLK):
                lanes = slice(sb * LANES, (sb + 1) * LANES)
                block = part[sb]
                stacked[2 * j * ROWS : (2 * j + 1) * ROWS, lanes] = block
                turned = pltpu.roll(block.astype(F32), CONTRIB, 1) * sign
                stacked[(2 * j + 1) * ROWS : (2 * j + 2) * ROWS, lanes] = turned.astype(BF16)

        @pl.loop(0, WIDTH // 256)
        def _(n):
            at = pl.ds(pl.multiple_of(n * 256, 256), 256)
            mixed = jnp.dot(left[0], stacked[:, at], preferred_element_type=F32) * UNITARY
            mixture[:, at] = mixed.astype(BF16)

    image = jnp.dot(mixture[...], right[0], preferred_element_type=F32)
    weight = taper_rows[0]
    for i in range(FAC // 2 // LANES):
        lanes = slice(i * LANES, (i + 1) * LANES)
        out_ref[0, :, lanes] = image[:, lanes] * (weight * taper_cols[0, :, lanes])


def facet(place, quarters, left, right, taper_rows, taper_cols):
    quarter = pl.BlockSpec((NBLK, ROWS, LANES), lambda n, place: (0, 0, 0))
    return pl.pallas_call(
        facet_kernel,
        out_shape=jax.ShapeDtypeStruct((2, ROWS_OUT, FAC), F32),
        grid_spec=pltpu.PrefetchScalarGridSpec(
            num_scalar_prefetch=1,
            grid=(4,),
            in_specs=[
                quarter, quarter, quarter, quarter,
                pl.BlockSpec((1, ROWS_OUT, WIDTH), lambda n, place: (place[0], 0, 0)),
                pl.BlockSpec((1, WIDTH, FAC // 2), lambda n, place: (n, 0, 0)),
                pl.BlockSpec((1, ROWS_OUT, LANES), lambda n, place: (place[0], 0, 0)),
                pl.BlockSpec((1, 1, FAC // 2), lambda n, place: (n % 2, 0, 0)),
            ],
            out_specs=pl.BlockSpec((1, ROWS_OUT, FAC // 2), lambda n, place: (n // 2, 0, n % 2)),
            scratch_shapes=[
                pltpu.VMEM((WIDTH, WIDTH), BF16),
                pltpu.VMEM((ROWS_OUT, WIDTH), BF16),
            ],
        ),
        compiler_params=pltpu.CompilerParams(vmem_limit_bytes=63 * 1024 * 1024),
        name="facet",
    )(place, *quarters, left, right, taper_rows, taper_cols)


def by_visibility_row(array):
    return array.reshape(BLOCKS, 2, BLK // LANES, LANES).transpose(0, 2, 1, 3).reshape(BLOCKS * 8, LANES)


def shards(vis_coords, vis_values, tile_index):
    columns, rows, left, right, taper_rows, taper_cols, bell = (jnp.asarray(table) for table in tables())
    place = lax.axis_index("vis").astype(jnp.int32).reshape(1)

    def swap(array, bit):
        return lax.ppermute(array, "vis", [(i, i ^ bit) for i in range(4)])

    send, send_x, keep, keep_x = gridding(
        tile_index[0], place, by_visibility_row(vis_coords), by_visibility_row(vis_values), columns, rows, bell
    )
    got_x = swap(send_x, 1)
    got = swap(send, 1)
    give = (keep_x.astype(F32) + got_x.astype(F32)).astype(BF16)
    arrived = swap(give, 2)
    total = (keep.astype(F32) + got.astype(F32) + arrived.astype(F32)).astype(BF16)
    outgoing = total.reshape(NBLK * NBLK, QUARTER, LANES)
    own = lax.all_to_all(outgoing, "grid", split_axis=0, concat_axis=0, tiled=True)
    own = own.reshape(NBLK, ROWS, LANES)
    by_x = swap(own, 2)
    by_core = swap(own, 1)
    by_both = swap(by_x, 1)
    return facet(place, (own, by_core, by_x, by_both), left, right, taper_rows, taper_cols)[None]


def solution(mesh):
    placed = (P("grid", "vis", None, None), P("grid", "vis", None, None), P("grid", "vis"))
    return jax.shard_map(
        shards, mesh=mesh, in_specs=placed, out_specs=P("grid", None, "vis", None), check_vma=False
    )
```

profile of v0, /device:TPU:1, one launch (start us, length us, event | category | flops | bytes accessed | tf_op | source)
XLA Modules:
  0.0 75.9 jit_solution(17115704312633060091)
XLA Ops:
  0.0 18.1 %gridding.1 = (bf16[8,128,128]{2,1,0:T(8,128)(2,1)}, bf16[8,128,128]{2,1,0:T(8,128)(2,1)}, bf16[8,128,128]{2,1,0:T(8,128)(2,1)}, bf16[8,128,128]{2,1,0:T(8,128)(2,1)}) custom-call(s32[64]{0:T(128)} %bitcast.21, s32[1]{0:T(128)} %bitcast.place_ref, f32[512,128]{1,0:T(8,128)} %bitcast.19, f32[512,128]{1,0:T(8,128)} %bitcast.20, ...), custom_call_target="tpu_custom_call" | custom-call | tf_op jit(solution)/shard_map/gridding/pallas_call | solution.py:228
  18.1 3.3 %collective-permute-start.1 = (bf16[8,128,128]{2,1,0:T(8,128)(2,1)}, bf16[8,128,128]{2,1,0:T(8,128)(2,1)S(1)}, u32[]{:S(2)}, u32[]{:S(2)}) collective-permute-start(bf16[8,128,128]{2,1,0:T(8,128)(2,1)} %get-tuple-element.12), channel_id=1, source_target_pairs={{0,1},{1,0},{2,3},{3,2},{4,5},{5,4},{6,7},{7,6},{8,9},{9,8},{10,11... | collective-permute-start | bytes 786440 | tf_op jit(solution)/shard_map/ppermute | solution.py:309
  21.5 0.1 collective-permute-start
  21.6 1.3 %collective-permute-done.1 = bf16[8,128,128]{2,1,0:T(8,128)(2,1)S(1)} collective-permute-done((bf16[8,128,128]{2,1,0:T(8,128)(2,1)}, bf16[8,128,128]{2,1,0:T(8,128)(2,1)S(1)}, u32[]{:S(2)}, u32[]{:S(2)}) %collective-permute-start.1) | collective-permute-done | bytes 262176 | tf_op jit(solution)/shard_map/ppermute | solution.py:309
  22.8 1.0 %add_convert_fusion.1 = bf16[8,128,128]{2,1,0:T(8,128)(2,1)S(1)} fusion(bf16[8,128,128]{2,1,0:T(8,128)(2,1)S(1)} %collective-permute-done.1, bf16[8,128,128]{2,1,0:T(8,128)(2,1)} %get-tuple-element.11), kind=kLoop, calls=%fused_computation.1 | loop fusion | flops 524288 | bytes 786432 | tf_op jit(solution)/shard_map/convert_element_type | solution.py:316
  23.9 0.1 collective-permute-start.2
  24.0 0.0 collective-permute-done
  24.0 7.5 %collective-permute-done.2 = bf16[8,128,128]{2,1,0:T(8,128)(2,1)S(1)} collective-permute-done((bf16[8,128,128]{2,1,0:T(8,128)(2,1)S(1)}, bf16[8,128,128]{2,1,0:T(8,128)(2,1)S(1)}, u32[]{:S(2)}, u32[]{:S(2)}) %collective-permute-start.2) | collective-permute-done | bytes 262176 | tf_op jit(solution)/shard_map/ppermute | solution.py:309
  31.5 1.1 %add_convert_fusion = bf16[8,128,128]{2,1,0:T(8,128)(2,1)S(1)} fusion(bf16[8,128,128]{2,1,0:T(8,128)(2,1)S(1)} %collective-permute-done.2, bf16[8,128,128]{2,1,0:T(8,128)(2,1)S(1)} %collective-permute-done, bf16[8,128,128]{2,1,0:T(8,128)(2,1)} %get-tuple-element.9), kind=kLoop, calls=%fused_computation | loop fusion | flops 786432 | bytes 1048576 | tf_op jit(solution)/shard_map/convert_element_type | solution.py:318
  32.5 24.8 %all_to_all.5 = bf16[64,16,128]{2,1,0:T(8,128)(2,1)S(1)} all-to-all(bf16[64,16,128]{2,1,0:T(8,128)(2,1)S(1)} %bitcast.18), channel_id=1, replica_groups=mesh['grid'=64,'vis'=4] {'grid'}, dimensions={0} | all-to-all | bytes 524288 | tf_op jit(solution)/shard_map/all_to_all | solution.py:320
  57.4 0.0 copy-start
  57.4 0.3 collective-permute-start.4
  57.7 3.8 %collective-permute-start.3 = (bf16[8,128,128]{2,1,0:T(8,128)(2,1)S(1)}, bf16[8,128,128]{2,1,0:T(8,128)(2,1)S(1)}, u32[]{:S(2)}, u32[]{:S(2)}) collective-permute-start(bf16[8,128,128]{2,1,0:T(8,128)(2,1)S(1)} %bitcast.16), channel_id=1, source_target_pairs={{0,1},{1,0},{2,3},{3,2},{4,5},{5,4},{6,7},{7,6},{8,9},{9,8},{10,11... | collective-permute-start | bytes 786440 | tf_op jit(solution)/shard_map/ppermute | solution.py:309
  61.5 1.1 %collective-permute-done.4.by_x = bf16[8,128,128]{2,1,0:T(8,128)(2,1)S(1)} collective-permute-done((bf16[8,128,128]{2,1,0:T(8,128)(2,1)S(1)}, bf16[8,128,128]{2,1,0:T(8,128)(2,1)S(1)}, u32[]{:S(2)}, u32[]{:S(2)}) %collective-permute-start.4) | collective-permute-done | bytes 262176 | tf_op jit(solution)/shard_map/ppermute | solution.py:309
  62.6 0.0 copy-start.1
  62.6 4.7 %collective-permute-start.5 = (bf16[8,128,128]{2,1,0:T(8,128)(2,1)S(1)}, bf16[8,128,128]{2,1,0:T(8,128)(2,1)}, u32[]{:S(2)}, u32[]{:S(2)}) collective-permute-start(bf16[8,128,128]{2,1,0:T(8,128)(2,1)S(1)} %collective-permute-done.4.by_x), channel_id=1, source_target_pairs={{0,1},{1,0},{2,3},{3,2},{4,5},{5,4},{6,7},{7,6},{8,9},{9,8},{10,11... | collective-permute-start | bytes 786440 | tf_op jit(solution)/shard_map/ppermute | solution.py:309
  67.3 0.0 collective-permute-done.3.by_core
  67.3 0.0 copy-start.2
  67.3 1.3 %collective-permute-done.5.by_both = bf16[8,128,128]{2,1,0:T(8,128)(2,1)} collective-permute-done((bf16[8,128,128]{2,1,0:T(8,128)(2,1)S(1)}, bf16[8,128,128]{2,1,0:T(8,128)(2,1)}, u32[]{:S(2)}, u32[]{:S(2)}) %collective-permute-start.5) | collective-permute-done | bytes 262176 | tf_op jit(solution)/shard_map/ppermute | solution.py:309
  68.6 0.0 copy-done
  68.6 0.0 copy-done.1
  68.6 0.0 copy-done.2
  68.6 7.3 %facet.1 = f32[2,256,1024]{2,1,0:T(8,128)} custom-call(s32[1]{0:T(128)} %bitcast.place_ref, bf16[8,128,128]{2,1,0:T(8,128)(2,1)} %bitcast.17, bf16[8,128,128]{2,1,0:T(8,128)(2,1)} %copy-done.2, bf16[8,128,128]{2,1,0:T(8,128)(2,1)} %copy-done.1, bf16[8,128,128]{2,1,0:T(8,128)(2,1)} %collective-permute-done.5.by_both, ...), custom_call_target="tpu_custom_call" | custom-call | tf_op jit(solution)/shard_map/facet/pallas_call | solution.py:276
Async XLA Ops:
  18.1 4.7 %collective-permute-start.1 = (bf16[8,128,128]{2,1,0:T(8,128)(2,1)}, bf16[8,128,128]{2,1,0:T(8,128)(2,1)S(1)}, u32[]{:S(2)}, u32[]{:S(2)}) collective-permute-start(bf16[8,128,128]{2,1,0:T(8,128)(2,1)} %get-tuple-element.12), channel_id=1, source_target_pairs={{0,1},{1,0},{2,3},{3,2},{4,5},{5,4},{6,7},{7,6},{8,9},{9,8},{10,11... | collective-permute-start | bytes 786440 | tf_op jit(solution)/shard_map/ppermute | solution.py:309
  21.5 2.5 %collective-permute-start = (bf16[8,128,128]{2,1,0:T(8,128)(2,1)}, bf16[8,128,128]{2,1,0:T(8,128)(2,1)S(1)}, u32[]{:S(2)}, u32[]{:S(2)}) collective-permute-start(bf16[8,128,128]{2,1,0:T(8,128)(2,1)} %get-tuple-element.10), channel_id=1, source_target_pairs={{0,1},{1,0},{2,3},{3,2},{4,5},{5,4},{6,7},{7,6},{8,9},{9,8},{10,11... | collective-permute-start | bytes 786440 | tf_op jit(solution)/shard_map/ppermute | solution.py:309
  23.9 7.6 %collective-permute-start.2 = (bf16[8,128,128]{2,1,0:T(8,128)(2,1)S(1)}, bf16[8,128,128]{2,1,0:T(8,128)(2,1)S(1)}, u32[]{:S(2)}, u32[]{:S(2)}) collective-permute-start(bf16[8,128,128]{2,1,0:T(8,128)(2,1)S(1)} %add_convert_fusion.1), channel_id=1, source_target_pairs={{0,2},{1,3},{2,0},{3,1},{4,6},{5,7},{6,4},{7,5},{8,10},{9,11},{10,... | collective-permute-start | bytes 786440 | tf_op jit(solution)/shard_map/ppermute | solution.py:309
  57.4 11.2 %copy-start = (bf16[64,16,128]{2,1,0:T(8,128)(2,1)}, bf16[64,16,128]{2,1,0:T(8,128)(2,1)S(1)}, u32[]{:S(2)}) copy-start(bf16[64,16,128]{2,1,0:T(8,128)(2,1)S(1)} %all_to_all.5) | copy-start | bytes 786436
  57.4 5.2 %collective-permute-start.4 = (bf16[8,128,128]{2,1,0:T(8,128)(2,1)S(1)}, bf16[8,128,128]{2,1,0:T(8,128)(2,1)S(1)}, u32[]{:S(2)}, u32[]{:S(2)}) collective-permute-start(bf16[8,128,128]{2,1,0:T(8,128)(2,1)S(1)} %bitcast.15), channel_id=1, source_target_pairs={{0,2},{1,3},{2,0},{3,1},{4,6},{5,7},{6,4},{7,5},{8,10},{9,11},{10,... | collective-permute-start | bytes 786440 | tf_op jit(solution)/shard_map/ppermute | solution.py:309
  57.7 9.6 %collective-permute-start.3 = (bf16[8,128,128]{2,1,0:T(8,128)(2,1)S(1)}, bf16[8,128,128]{2,1,0:T(8,128)(2,1)S(1)}, u32[]{:S(2)}, u32[]{:S(2)}) collective-permute-start(bf16[8,128,128]{2,1,0:T(8,128)(2,1)S(1)} %bitcast.16), channel_id=1, source_target_pairs={{0,1},{1,0},{2,3},{3,2},{4,5},{5,4},{6,7},{7,6},{8,9},{9,8},{10,11... | collective-permute-start | bytes 786440 | tf_op jit(solution)/shard_map/ppermute | solution.py:309
  62.6 6.0 %copy-start.1 = (bf16[8,128,128]{2,1,0:T(8,128)(2,1)}, bf16[8,128,128]{2,1,0:T(8,128)(2,1)S(1)}, u32[]{:S(2)}) copy-start(bf16[8,128,128]{2,1,0:T(8,128)(2,1)S(1)} %collective-permute-done.4.by_x) | copy-start | bytes 786436
  62.6 6.0 %collective-permute-start.5 = (bf16[8,128,128]{2,1,0:T(8,128)(2,1)S(1)}, bf16[8,128,128]{2,1,0:T(8,128)(2,1)}, u32[]{:S(2)}, u32[]{:S(2)}) collective-permute-start(bf16[8,128,128]{2,1,0:T(8,128)(2,1)S(1)} %collective-permute-done.4.by_x), channel_id=1, source_target_pairs={{0,1},{1,0},{2,3},{3,2},{4,5},{5,4},{6,7},{7,6},{8,9},{9,8},{10,11... | collective-permute-start | bytes 786440 | tf_op jit(solution)/shard_map/ppermute | solution.py:309
  67.3 1.3 %copy-start.2 = (bf16[8,128,128]{2,1,0:T(8,128)(2,1)}, bf16[8,128,128]{2,1,0:T(8,128)(2,1)S(1)}, u32[]{:S(2)}) copy-start(bf16[8,128,128]{2,1,0:T(8,128)(2,1)S(1)} %collective-permute-done.3.by_core) | copy-start | bytes 786436
where the time goes:
time: 76.2 us; the launch traced here: 75.9 us
  Pallas kernels  25.5 us (33%)
  blocking collectives  24.8 us (33%)
  starting transfers between devices  12.3 us (16%)
  waiting for transfers between devices  11.2 us (15%)
  other arithmetic  2.08 us (3%)
    all_to_all x1, blocking collectives, shards(): lax.all_to_all(outgoing, 'grid', split_axis=0, concat_axis=0, tiled=True)  24.8 us
    pallas_call x1, Pallas kernels, gridding(): pl.pallas_call(gridding_kernel, out_shape=[quarter] * 4, in_specs=[scalar...  18.1 us
    ppermute x6, starting transfers between devices, swap(): return lax.ppermute(array, 'vis', [(i, i ^ bit) for i in range(4)])  12.3 us
    ppermute x6, waiting for transfers between devices, swap(): return lax.ppermute(array, 'vis', [(i, i ^ bit) for i in range(4)])  11.2 us
    pallas_call x1, Pallas kernels, facet(): pl.pallas_call(facet_kernel, out_shape=jax.ShapeDtypeStruct((2, ROWS_OUT,...  7.32 us
  transfers between devices with their start and end apart: 6, of which 4 were waited for; matrix products, arithmetic and copies ran while one was open for 1% of the time, Pallas kernels for 0%

commit v1 on v0

v1 whole, which is shorter than its diff:
```python
import functools
import math

import jax
import jax.numpy as jnp
import ml_dtypes
import numpy as np
from jax import lax
from jax.experimental import pallas as pl
from jax.experimental.pallas import tpu as pltpu
from jax.sharding import PartitionSpec as P

SUB = 512
FAC = 1024
CONTRIB = 64
TILE = 64
BLK = 512
BLOCKS = 64
GROUP = 8
NBLK = 8
LANES = 128
QUARTER = 16
ROWS = NBLK * QUARTER
ROWS_OUT = FAC // 4
WIDTH = 2 * SUB
UNITARY = 1.0 / math.sqrt(SUB)
BF16 = jnp.bfloat16
F32 = jnp.float32


def angles(first, second, length):
    return (first[:, None] * second[None, :] % length) * (2.0 * math.pi / length)


def as_bf16(table):
    return np.ascontiguousarray(table.astype(np.float32)).astype(ml_dtypes.bfloat16)


@functools.lru_cache(maxsize=None)
def tables():
    spectrum = np.arange(SUB)
    turn = angles(spectrum, spectrum, SUB).reshape(NBLK, TILE, NBLK, CONTRIB)
    cos, sin = np.cos(turn), np.sin(turn)
    columns = np.empty((NBLK, 2, TILE, NBLK, 2, CONTRIB))
    columns[:, 0, :, :, 0] = cos
    columns[:, 1, :, :, 0] = sin
    columns[:, 0, :, :, 1] = -sin
    columns[:, 1, :, :, 1] = cos
    columns = as_bf16(columns.reshape(WIDTH, WIDTH))
    turn = angles(spectrum, spectrum, SUB)
    rows = np.concatenate([np.cos(turn), np.sin(turn)], 1)
    rows = rows.reshape(NBLK, 4, QUARTER, WIDTH).transpose(1, 0, 2, 3)
    rows = as_bf16(rows.reshape(SUB, WIDTH))
    turn = angles(np.arange(FAC), spectrum, FAC).reshape(4, ROWS_OUT, NBLK, 4, QUARTER)
    left = np.empty((4, 2, ROWS_OUT, 4, NBLK, QUARTER))
    for g in range(4):
        for j in range(4):
            left[g, 0, :, j] = np.cos(turn[g, :, :, g ^ j])
            left[g, 1, :, j] = np.sin(turn[g, :, :, g ^ j])
    left = as_bf16(left.reshape(4, 2 * ROWS_OUT, SUB))
    turn = angles(spectrum, np.arange(FAC), FAC).reshape(NBLK, CONTRIB, FAC)
    cos, sin = np.cos(turn), np.sin(turn)
    right = np.empty((NBLK, 2, CONTRIB, 2, FAC))
    right[:, 0, :, 0] = cos
    right[:, 1, :, 0] = -sin
    right[:, 0, :, 1] = sin
    right[:, 1, :, 1] = cos
    right = right.reshape(WIDTH, CHUNKS, 2 * FAC // CHUNKS).transpose(1, 0, 2)
    right = as_bf16(right)
    sines = np.sin(math.pi * (np.arange(FAC) + 0.5) / FAC)
    taper = 0.25 + 0.75 * sines * sines
    taper_rows = np.broadcast_to(taper.reshape(4, ROWS_OUT, 1), (4, ROWS_OUT, LANES)).astype(np.float32)
    taper_cols = (taper / math.sqrt(SUB)).reshape(1, FAC).astype(np.float32)
    pixel = np.arange(TILE)
    bell = (1.0 - 2.0 * (pixel % 2)) * np.exp(-(pixel * pixel) / 256.0)
    bell = (bell[:, None] * np.concatenate([bell, bell])[None, :]).astype(np.float32)
    return columns, rows, left, right, np.ascontiguousarray(taper_rows), taper_cols, bell


SINE = [math.pi ** (2 * k + 1) * (-1) ** k / math.factorial(2 * k + 1) for k in range(7)]


def gridding_kernel(
    place_ref, tiles_hbm, coords_hbm, values_hbm, columns_hbm, rows_hbm, bell_hbm, left_hbm, taper_rows_hbm, taper_cols_hbm,
    keep_ref, send_ref, keep_x_ref, send_x_ref, left_ref, taper_rows_ref, taper_cols_ref,
    tile_ref, coords, values, whole, offset, step8, slope, height, u_buf, v_buf, acc, grid16, stacked, columns, rows, bell_ref,
    sems,
):
    place = place_ref[0]
    first = [(coords_hbm, coords), (values_hbm, values), (tiles_hbm, tile_ref)]
    later = [(columns_hbm, columns), (bell_hbm, bell_ref)]
    for i in range(4):
        quarter = pl.ds(pl.multiple_of((place ^ i) * ROWS, ROWS), ROWS)
        later.append((rows_hbm.at[quarter], rows.at[i * ROWS : (i + 1) * ROWS]))
    last = [(left_hbm.at[place], left_ref), (taper_rows_hbm.at[place], taper_rows_ref), (taper_cols_hbm, taper_cols_ref)]
    copies = [pltpu.make_async_copy(*ends, sems.at[i]) for i, ends in enumerate(first + later + last)]
    for copy in copies:
        copy.start()
    acc[...] = jnp.zeros_like(acc)
    for copy in copies[: len(first)]:
        copy.wait()

    @pl.loop(0, BLOCKS * 8 // 64)
    def _(chunk):
        at = pl.ds(pl.multiple_of(chunk * 64, 64), 64)
        c = coords[at, :]
        r = jnp.round(c)
        f = c - r
        f = jnp.where(jnp.abs(f) < 1e-20, 1e-20, f)
        square = f * f
        sine = jnp.full_like(f, SINE[6])
        for k in range(5, -1, -1):
            sine = sine * square + SINE[k]
        half = r * 0.5
        odd = half - jnp.floor(half)
        sine = sine * f * ((1.0 - 4.0 * odd) * (1.0 / math.pi))
        whole[at, :] = r
        offset[at, :] = f
        step8[at, :] = jnp.exp(c * (1.0 / 16.0))
        slope[at, :] = c * (1.0 / 128.0)
        height[at, :] = sine * jnp.exp(c * c * (-1.0 / 256.0))

    row_of = lax.broadcasted_iota(jnp.int32, (8, LANES), 0).astype(F32)

    def spread(ref, row):
        return jnp.broadcast_to(ref[pl.ds(row, 1), :], (8, LANES))

    def generate(b, slot):
        for t in range(4):
            lanes = slice(t * LANES, (t + 1) * LANES)
            for axis in range(2):
                row = b * 8 + t * 2 + axis
                base = row_of - spread(whole, row)
                f = spread(offset, row)
                ratio = spread(step8, row)
                w = spread(height, row) * jnp.exp(row_of * spread(slope, row))
                if axis == 0:
                    found = []
                    for a in range(8):
                        inverse = pl.reciprocal((base + 8.0 * a) - f, approx=True)
                        found.append(w * inverse)
                        w = w * ratio
                    u_buf[slot, :, lanes] = jnp.concatenate(found, 0).astype(BF16)
                else:
                    w_real = w * spread(values, b * 8 + t * 2)
                    w_imag = w * spread(values, b * 8 + t * 2 + 1)
                    real, imag = [], []
                    for a in range(8):
                        inverse = pl.reciprocal((base + 8.0 * a) - f, approx=True)
                        real.append(w_real * inverse)
                        imag.append(w_imag * inverse)
                        w_real = w_real * ratio
                        w_imag = w_imag * ratio
                    v_buf[slot, :TILE, lanes] = jnp.concatenate(real, 0).astype(BF16)
                    v_buf[slot, TILE:, lanes] = jnp.concatenate(imag, 0).astype(BF16)

    def patch_of(slot):
        return lax.dot_general(
            u_buf[slot], v_buf[slot], (((1,), (1,)), ((), ())), preferred_element_type=F32
        )

    def deposit(b, patch):
        tile = tile_ref[0, b]
        at = (
            pl.ds(pl.multiple_of((tile // NBLK) * TILE, TILE), TILE),
            pl.ds(pl.multiple_of((tile % NBLK) * LANES, LANES), LANES),
        )
        acc[at] = acc[at] + patch

    @pl.loop(0, BLOCKS // GROUP)
    def _(group):
        held = None
        for i in range(GROUP):
            generate(group * GROUP + i, i)
            patch = patch_of(i)
            if held is not None:
                deposit(group * GROUP + i - 1, held)
            held = patch
        deposit(group * GROUP + GROUP - 1, held)

    for copy in copies[len(first) :]:
        copy.wait()
    bell = bell_ref[...]

    @pl.loop(0, NBLK)
    def _(a):
        at = pl.ds(pl.multiple_of(a * TILE, TILE), TILE)
        for e in range(NBLK):
            lanes = slice(e * LANES, (e + 1) * LANES)
            grid16[at, lanes] = (acc[at, lanes] * bell).astype(BF16)

    sign = jnp.where(lax.broadcasted_iota(jnp.int32, (1, LANES), 1) < CONTRIB, 1.0, -1.0)

    @pl.loop(0, WIDTH // 256)
    def _(n):
        at = pl.ds(pl.multiple_of(n * 256, 256), 256)
        images = jnp.dot(grid16[...], columns[:, at], preferred_element_type=F32) * UNITARY
        stacked[:SUB, at] = images.astype(BF16)
        turned = jnp.concatenate(
            [pltpu.roll(images[:, :LANES], CONTRIB, 1) * sign, pltpu.roll(images[:, LANES:], CONTRIB, 1) * sign], 1
        )
        stacked[SUB:, at] = turned.astype(BF16)

    @pl.loop(0, WIDTH // 256)
    def _(n):
        at = pl.ds(pl.multiple_of(n * 256, 256), 256)
        spectra = jnp.dot(rows[...], stacked[:, at], preferred_element_type=F32) * UNITARY
        spectra = spectra.astype(BF16)
        for quarter, out in enumerate((keep_ref, send_ref, keep_x_ref, send_x_ref)):
            for i in range(2):
                out[n * 2 + i] = spectra[quarter * ROWS : (quarter + 1) * ROWS, i * LANES : (i + 1) * LANES]


def gridding(place, arrays):
    hbm = pl.BlockSpec(memory_space=pltpu.HBM)
    vector = pl.BlockSpec(memory_space=pltpu.VMEM)
    quarter = jax.ShapeDtypeStruct((NBLK, ROWS, LANES), BF16)
    plane = pltpu.VMEM((BLOCKS * 8, LANES), F32)
    return pl.pallas_call(
        gridding_kernel,
        out_shape=[quarter] * 4
        + [
            jax.ShapeDtypeStruct((2 * ROWS_OUT, SUB), BF16),
            jax.ShapeDtypeStruct((ROWS_OUT, LANES), F32),
            jax.ShapeDtypeStruct((1, FAC), F32),
        ],
        in_specs=[pl.BlockSpec(memory_space=pltpu.SMEM)] + [hbm] * len(arrays),
        out_specs=[vector] * 7,
        scratch_shapes=[
            pltpu.SMEM((1, BLOCKS), jnp.int32),
            plane, plane, plane, plane, plane, plane, plane,
            pltpu.VMEM((GROUP, TILE, BLK), BF16),
            pltpu.VMEM((GROUP, 2 * TILE, BLK), BF16),
            pltpu.VMEM((SUB, WIDTH), F32),
            pltpu.VMEM((SUB, WIDTH), BF16),
            pltpu.VMEM((WIDTH, WIDTH), BF16),
            pltpu.VMEM((WIDTH, WIDTH), BF16),
            pltpu.VMEM((SUB, WIDTH), BF16),
            pltpu.VMEM((TILE, LANES), F32),
            pltpu.SemaphoreType.DMA((12,)),
        ],
        compiler_params=pltpu.CompilerParams(vmem_limit_bytes=24 * 1024 * 1024),
        name="gridding",
    )(place, *(stay(array) for array in arrays))


def stay(array):
    return pltpu.with_memory_space_constraint(array, pltpu.HBM)


CHUNKS = 8


def facet_kernel(own, by_core, by_x, by_both, left, taper_rows, taper_cols, right_hbm, out_hbm, right, mixture, image, sems):
    for chunk in range(CHUNKS):
        pltpu.make_async_copy(right_hbm.at[chunk], right.at[chunk], sems.at[chunk]).start()
    sign = jnp.where(lax.broadcasted_iota(jnp.int32, (1, LANES), 1) < CONTRIB, -UNITARY, UNITARY)

    @pl.loop(0, NBLK // 2)
    def _(n):
        right_side = jnp.concatenate(
            [jnp.concatenate([part[2 * n], part[2 * n + 1]], 1) for part in (own, by_core, by_x, by_both)], 0
        )
        both = jnp.dot(left[...], right_side, preferred_element_type=F32)
        mixed = [
            both[:ROWS_OUT, lanes] * UNITARY + pltpu.roll(both[ROWS_OUT:, lanes], CONTRIB, 1) * sign
            for lanes in (slice(0, LANES), slice(LANES, 2 * LANES))
        ]
        at = pl.ds(pl.multiple_of(n * 2 * LANES, 2 * LANES), 2 * LANES)
        mixture[:, at] = jnp.concatenate(mixed, 1).astype(BF16)

    width = 2 * FAC // CHUNKS

    def departure(chunk):
        first = pl.multiple_of(chunk % (CHUNKS // 2) * width, width)
        into = out_hbm.at[chunk // (CHUNKS // 2), :, pl.ds(first, width)]
        return pltpu.make_async_copy(image.at[chunk], into, sems.at[CHUNKS + chunk])

    @pl.loop(0, CHUNKS)
    def _(chunk):
        pltpu.make_async_copy(right_hbm.at[chunk], right.at[chunk], sems.at[chunk]).wait()
        pixels = jnp.dot(mixture[...], right[chunk], preferred_element_type=F32)
        for i in range(width // LANES):
            first = pl.multiple_of(chunk % (CHUNKS // 2) * width + i * LANES, LANES)
            weight = taper_rows[...] * taper_cols[:, pl.ds(first, LANES)]
            image[chunk, :, i * LANES : (i + 1) * LANES] = pixels[:, i * LANES : (i + 1) * LANES] * weight
        departure(chunk).start()

    for chunk in range(CHUNKS):
        departure(chunk).wait()


def facet(quarters, left, taper_rows, taper_cols, right):
    vector = pl.BlockSpec(memory_space=pltpu.VMEM)
    hbm = pl.BlockSpec(memory_space=pltpu.HBM)
    return pl.pallas_call(
        facet_kernel,
        out_shape=jax.ShapeDtypeStruct((2, ROWS_OUT, FAC), F32),
        in_specs=[vector] * 7 + [hbm],
        out_specs=hbm,
        scratch_shapes=[
            pltpu.VMEM((CHUNKS, WIDTH, 2 * FAC // CHUNKS), BF16),
            pltpu.VMEM((ROWS_OUT, WIDTH), BF16),
            pltpu.VMEM((CHUNKS, ROWS_OUT, 2 * FAC // CHUNKS), F32),
            pltpu.SemaphoreType.DMA((2 * CHUNKS,)),
        ],
        compiler_params=pltpu.CompilerParams(vmem_limit_bytes=24 * 1024 * 1024),
        name="facet",
    )(*quarters, left, taper_rows, taper_cols, stay(right))


def by_visibility_row(array):
    return array.reshape(BLOCKS, 2, BLK // LANES, LANES).transpose(0, 2, 1, 3).reshape(BLOCKS * 8, LANES)


def shards(vis_coords, vis_values, tile_index):
    columns, rows, left, right, taper_rows, taper_cols, bell = (jnp.asarray(table) for table in tables())
    place = lax.axis_index("vis").astype(jnp.int32).reshape(1)

    def swap(array, bit):
        return lax.ppermute(array, "vis", [(i, i ^ bit) for i in range(4)])

    keep, send, keep_x, send_x, left, taper_rows, taper_cols = gridding(
        place,
        [
            tile_index, by_visibility_row(vis_coords), by_visibility_row(vis_values),
            columns, rows, bell, left, taper_rows, taper_cols,
        ],
    )
    got_x = swap(send_x, 1)
    got = swap(send, 1)
    give = (keep_x.astype(F32) + got_x.astype(F32)).astype(BF16)
    arrived = swap(give, 2)
    total = (keep.astype(F32) + got.astype(F32) + arrived.astype(F32)).astype(BF16)
    outgoing = total.reshape(NBLK * NBLK, QUARTER, LANES)
    own = lax.all_to_all(outgoing, "grid", split_axis=0, concat_axis=0, tiled=True)
    own = own.reshape(NBLK, ROWS, LANES)
    by_x = swap(own, 2)
    by_core = swap(own, 1)
    by_both = swap(by_x, 1)
    return facet((own, by_core, by_x, by_both), left, taper_rows, taper_cols, right)[None]


def solution(mesh):
    placed = (P("grid", "vis", None, None), P("grid", "vis", None, None), P("grid", "vis"))
    return jax.shard_map(
        shards, mesh=mesh, in_specs=placed, out_specs=P("grid", None, "vis", None), check_vma=False
    )
```

time: 76.2 us -> 65.7 us (0.86)
  Pallas kernels: 25.5 us -> 17.5 us
  other arithmetic: 2.08 us -> 0.18 us
    pallas_call x1, Pallas kernels: 18.1 us -> 12.7 us  [gridding(): pl.pallas_call(gridding_kernel, out_shape=[quarter] * 4 + [jax.ShapeDtype...]
    pallas_call x1, Pallas kernels: 7.32 us -> 4.79 us  [facet(): pl.pallas_call(facet_kernel, out_shape=jax.ShapeDtypeStruct((2, ROWS_OUT,...]
    convert_element_type x1, other arithmetic: 1.02 us -> 0.07 us  [shards(): give = (keep_x.astype(F32) + got_x.astype(F32)).astype(BF16)]
    convert_element_type x1, other arithmetic: 1.06 us -> 0.11 us  [shards(): (keep.astype(F32) + got.astype(F32) + arrived.astype(F32)).astype(BF16)]
  transfers between devices with their start and end apart: 6 -> 6, of which waited for: 4 -> 5; matrix products, arithmetic and copies ran while one was open for 1% -> 0% of each run, Pallas kernels for 0% -> 0%
where the time goes in v1:
time: 65.7 us; the launch traced here: 65.6 us
  blocking collectives  24.8 us (38%)
  Pallas kernels  17.5 us (27%)
  starting transfers between devices  12.3 us (19%)
  waiting for transfers between devices  10.9 us (17%)
    all_to_all x1, blocking collectives, shards(): lax.all_to_all(outgoing, 'grid', split_axis=0, concat_axis=0, tiled=True)  24.8 us
    pallas_call x1, Pallas kernels, gridding(): pl.pallas_call(gridding_kernel, out_shape=[quarter] * 4 + [jax.ShapeDtype...  12.7 us
    ppermute x6, starting transfers between devices, swap(): return lax.ppermute(array, 'vis', [(i, i ^ bit) for i in range(4)])  12.3 us
    ppermute x6, waiting for transfers between devices, swap(): return lax.ppermute(array, 'vis', [(i, i ^ bit) for i in range(4)])  10.9 us
    pallas_call x1, Pallas kernels, facet(): pl.pallas_call(facet_kernel, out_shape=jax.ShapeDtypeStruct((2, ROWS_OUT,...  4.79 us
  transfers between devices with their start and end apart: 6, of which 5 were waited for; matrix products, arithmetic and copies ran while one was open for 0% of the time, Pallas kernels for 0%

profile of v1, /device:TPU:1, one launch (start us, length us, event | category | flops | bytes accessed | tf_op | source)
XLA Modules:
  0.0 65.6 jit_solution(15924967659298989040)
XLA Ops:
  0.0 12.7 %gridding.1 = (bf16[8,128,128]{2,1,0:T(8,128)(2,1)S(1)}, bf16[8,128,128]{2,1,0:T(8,128)(2,1)S(1)}, bf16[8,128,128]{2,1,0:T(8,128)(2,1)S(1)}, bf16[8,128,128]{2,1...) custom-call(s32[1]{0:T(128)} %bitcast.place_ref, ...), custom_call_target="tpu_custom_call" | custom-call | tf_op jit(solution)/shard_map/gridding/pallas_call | solution.py:219
  12.7 3.3 %collective-permute-start.1 = (bf16[8,128,128]{2,1,0:T(8,128)(2,1)S(1)}, bf16[8,128,128]{2,1,0:T(8,128)(2,1)S(1)}, u32[]{:S(2)}, u32[]{:S(2)}) collective-permute-start(bf16[8,128,128]{2,1,0:T(8,128)(2,1)S(1)} %get-tuple-element.15), channel_id=1, source_target_pairs={{0,1},{1,0},{2,3},{3,2},{4,5},{5,4},{6,7},{7,6},{8,9},{9,8},{10,11... | collective-permute-start | bytes 786440 | tf_op jit(solution)/shard_map/ppermute | solution.py:321
  16.0 0.1 collective-permute-start
  16.1 1.1 %collective-permute-done.1 = bf16[8,128,128]{2,1,0:T(8,128)(2,1)S(1)} collective-permute-done((bf16[8,128,128]{2,1,0:T(8,128)(2,1)S(1)}, bf16[8,128,128]{2,1,0:T(8,128)(2,1)S(1)}, u32[]{:S(2)}, u32[]{:S(2)}) %collective-permute-start.1) | collective-permute-done | bytes 262176 | tf_op jit(solution)/shard_map/ppermute | solution.py:321
  17.2 0.1 add_convert_fusion.1
  17.2 0.1 collective-permute-start.2
  17.3 0.2 collective-permute-done
  17.5 7.3 %collective-permute-done.2 = bf16[8,128,128]{2,1,0:T(8,128)(2,1)S(1)} collective-permute-done((bf16[8,128,128]{2,1,0:T(8,128)(2,1)S(1)}, bf16[8,128,128]{2,1,0:T(8,128)(2,1)S(1)}, u32[]{:S(2)}, u32[]{:S(2)}) %collective-permute-start.2) | collective-permute-done | bytes 262176 | tf_op jit(solution)/shard_map/ppermute | solution.py:321
  24.8 0.1 add_convert_fusion
  25.0 24.8 %all_to_all.5 = bf16[64,16,128]{2,1,0:T(8,128)(2,1)S(1)} all-to-all(bf16[64,16,128]{2,1,0:T(8,128)(2,1)S(1)} %bitcast.17), channel_id=1, replica_groups=mesh['grid'=64,'vis'=4] {'grid'}, dimensions={0} | all-to-all | bytes 524288 | tf_op jit(solution)/shard_map/all_to_all | solution.py:336
  49.8 0.3 collective-permute-start.4
  50.1 3.8 %collective-permute-start.3 = (bf16[8,128,128]{2,1,0:T(8,128)(2,1)S(1)}, bf16[8,128,128]{2,1,0:T(8,128)(2,1)S(1)}, u32[]{:S(2)}, u32[]{:S(2)}) collective-permute-start(bf16[8,128,128]{2,1,0:T(8,128)(2,1)S(1)} %bitcast.15), channel_id=1, source_target_pairs={{0,1},{1,0},{2,3},{3,2},{4,5},{5,4},{6,7},{7,6},{8,9},{9,8},{10,11... | collective-permute-start | bytes 786440 | tf_op jit(solution)/shard_map/ppermute | solution.py:321
  53.9 1.1 %collective-permute-done.4.by_x = bf16[8,128,128]{2,1,0:T(8,128)(2,1)S(1)} collective-permute-done((bf16[8,128,128]{2,1,0:T(8,128)(2,1)S(1)}, bf16[8,128,128]{2,1,0:T(8,128)(2,1)S(1)}, u32[]{:S(2)}, u32[]{:S(2)}) %collective-permute-start.4) | collective-permute-done | bytes 262176 | tf_op jit(solution)/shard_map/ppermute | solution.py:321
  55.0 4.7 %collective-permute-start.5 = (bf16[8,128,128]{2,1,0:T(8,128)(2,1)S(1)}, bf16[8,128,128]{2,1,0:T(8,128)(2,1)S(1)}, u32[]{:S(2)}, u32[]{:S(2)}) collective-permute-start(bf16[8,128,128]{2,1,0:T(8,128)(2,1)S(1)} %collective-permute-done.4.by_x), channel_id=1, source_target_pairs={{0,1},{1,0},{2,3},{3,2},{4,5},{5,4},{6,7},{7,6},{8,9},{9,8},{10,11... | collective-permute-start | bytes 786440 | tf_op jit(solution)/shard_map/ppermute | solution.py:321
  59.7 0.0 collective-permute-done.3.by_core
  59.7 1.2 %collective-permute-done.5.by_both = bf16[8,128,128]{2,1,0:T(8,128)(2,1)S(1)} collective-permute-done((bf16[8,128,128]{2,1,0:T(8,128)(2,1)S(1)}, bf16[8,128,128]{2,1,0:T(8,128)(2,1)S(1)}, u32[]{:S(2)}, u32[]{:S(2)}) %collective-permute-start.5) | collective-permute-done | bytes 262176 | tf_op jit(solution)/shard_map/ppermute | solution.py:321
  60.8 4.8 %facet.1 = f32[2,256,1024]{2,1,0:T(8,128)} custom-call(bf16[8,128,128]{2,1,0:T(8,128)(2,1)S(1)} %bitcast.16, bf16[8,128,128]{2,1,0:T(8,128)(2,1)S(1)} %collective-permute-done.3.by_core, bf16[8,128,128]{2,1,0:T(8,128)(2,1)S(1)} %collective-permute-done.4.by_x, bf16[8,128,128]{2,1,0:T(8,128)(2,1)S(1)} %collective-permute-done.5.by_both, ...), custom_call_target="tpu_custom_call" | custom-call | tf_op jit(solution)/shard_map/facet/pallas_call | solution.py:296
Async XLA Ops:
  12.7 4.5 %collective-permute-start.1 = (bf16[8,128,128]{2,1,0:T(8,128)(2,1)S(1)}, bf16[8,128,128]{2,1,0:T(8,128)(2,1)S(1)}, u32[]{:S(2)}, u32[]{:S(2)}) collective-permute-start(bf16[8,128,128]{2,1,0:T(8,128)(2,1)S(1)} %get-tuple-element.15), channel_id=1, source_target_pairs={{0,1},{1,0},{2,3},{3,2},{4,5},{5,4},{6,7},{7,6},{8,9},{9,8},{10,11... | collective-permute-start | bytes 786440 | tf_op jit(solution)/shard_map/ppermute | solution.py:321
  16.0 1.5 %collective-permute-start = (bf16[8,128,128]{2,1,0:T(8,128)(2,1)S(1)}, bf16[8,128,128]{2,1,0:T(8,128)(2,1)S(1)}, u32[]{:S(2)}, u32[]{:S(2)}) collective-permute-start(bf16[8,128,128]{2,1,0:T(8,128)(2,1)S(1)} %get-tuple-element.13), channel_id=1, source_target_pairs={{0,1},{1,0},{2,3},{3,2},{4,5},{5,4},{6,7},{7,6},{8,9},{9,8},{10,11... | collective-permute-start | bytes 786440 | tf_op jit(solution)/shard_map/ppermute | solution.py:321
  17.2 7.6 %collective-permute-start.2 = (bf16[8,128,128]{2,1,0:T(8,128)(2,1)S(1)}, bf16[8,128,128]{2,1,0:T(8,128)(2,1)S(1)}, u32[]{:S(2)}, u32[]{:S(2)}) collective-permute-start(bf16[8,128,128]{2,1,0:T(8,128)(2,1)S(1)} %add_convert_fusion.1), channel_id=1, source_target_pairs={{0,2},{1,3},{2,0},{3,1},{4,6},{5,7},{6,4},{7,5},{8,10},{9,11},{10,... | collective-permute-start | bytes 786440 | tf_op jit(solution)/shard_map/ppermute | solution.py:321
  49.8 5.2 %collective-permute-start.4 = (bf16[8,128,128]{2,1,0:T(8,128)(2,1)S(1)}, bf16[8,128,128]{2,1,0:T(8,128)(2,1)S(1)}, u32[]{:S(2)}, u32[]{:S(2)}) collective-permute-start(bf16[8,128,128]{2,1,0:T(8,128)(2,1)S(1)} %bitcast.14), channel_id=1, source_target_pairs={{0,2},{1,3},{2,0},{3,1},{4,6},{5,7},{6,4},{7,5},{8,10},{9,11},{10,... | collective-permute-start | bytes 786440 | tf_op jit(solution)/shard_map/ppermute | solution.py:321
  50.1 9.6 %collective-permute-start.3 = (bf16[8,128,128]{2,1,0:T(8,128)(2,1)S(1)}, bf16[8,128,128]{2,1,0:T(8,128)(2,1)S(1)}, u32[]{:S(2)}, u32[]{:S(2)}) collective-permute-start(bf16[8,128,128]{2,1,0:T(8,128)(2,1)S(1)} %bitcast.15), channel_id=1, source_target_pairs={{0,1},{1,0},{2,3},{3,2},{4,5},{5,4},{6,7},{7,6},{8,9},{9,8},{10,11... | collective-permute-start | bytes 786440 | tf_op jit(solution)/shard_map/ppermute | solution.py:321
  55.0 5.8 %collective-permute-start.5 = (bf16[8,128,128]{2,1,0:T(8,128)(2,1)S(1)}, bf16[8,128,128]{2,1,0:T(8,128)(2,1)S(1)}, u32[]{:S(2)}, u32[]{:S(2)}) collective-permute-start(bf16[8,128,128]{2,1,0:T(8,128)(2,1)S(1)} %collective-permute-done.4.by_x), channel_id=1, source_target_pairs={{0,1},{1,0},{2,3},{3,2},{4,5},{5,4},{6,7},{7,6},{8,9},{9,8},{10,11... | collective-permute-start | bytes 786440 | tf_op jit(solution)/shard_map/ppermute | solution.py:321

commit v2 on v1

--- a/solution.py
+++ b/solution.py
@@ -21,6 +21,7 @@
 LANES = 128
 QUARTER = 16
 ROWS = NBLK * QUARTER
+HALF = 2 * ROWS
 ROWS_OUT = FAC // 4
 WIDTH = 2 * SUB
 UNITARY = 1.0 / math.sqrt(SUB)
@@ -49,7 +50,7 @@
     columns = as_bf16(columns.reshape(WIDTH, WIDTH))
     turn = angles(spectrum, spectrum, SUB)
     rows = np.concatenate([np.cos(turn), np.sin(turn)], 1)
-    rows = rows.reshape(NBLK, 4, QUARTER, WIDTH).transpose(1, 0, 2, 3)
+    rows = rows.reshape(NBLK, 2, 2, QUARTER, WIDTH).transpose(2, 0, 1, 3, 4)
     rows = as_bf16(rows.reshape(SUB, WIDTH))
     turn = angles(np.arange(FAC), spectrum, FAC).reshape(4, ROWS_OUT, NBLK, 4, QUARTER)
     left = np.empty((4, 2, ROWS_OUT, 4, NBLK, QUARTER))
@@ -82,16 +83,16 @@
 
 def gridding_kernel(
     place_ref, tiles_hbm, coords_hbm, values_hbm, columns_hbm, rows_hbm, bell_hbm, left_hbm, taper_rows_hbm, taper_cols_hbm,
-    keep_ref, send_ref, keep_x_ref, send_x_ref, left_ref, taper_rows_ref, taper_cols_ref,
+    keep_ref, send_ref, left_ref, taper_rows_ref, taper_cols_ref,
     tile_ref, coords, values, whole, offset, step8, slope, height, u_buf, v_buf, acc, grid16, stacked, columns, rows, bell_ref,
     sems,
 ):
     place = place_ref[0]
     first = [(coords_hbm, coords), (values_hbm, values), (tiles_hbm, tile_ref)]
     later = [(columns_hbm, columns), (bell_hbm, bell_ref)]
-    for i in range(4):
-        quarter = pl.ds(pl.multiple_of((place ^ i) * ROWS, ROWS), ROWS)
-        later.append((rows_hbm.at[quarter], rows.at[i * ROWS : (i + 1) * ROWS]))
+    for i in range(2):
+        half = pl.ds(pl.multiple_of((place % 2 ^ i) * HALF, HALF), HALF)
+        later.append((rows_hbm.at[half], rows.at[i * HALF : (i + 1) * HALF]))
     last = [(left_hbm.at[place], left_ref), (taper_rows_hbm.at[place], taper_rows_ref), (taper_cols_hbm, taper_cols_ref)]
     copies = [pltpu.make_async_copy(*ends, sems.at[i]) for i, ends in enumerate(first + later + last)]
     for copy in copies:
@@ -206,26 +207,26 @@
         at = pl.ds(pl.multiple_of(n * 256, 256), 256)
         spectra = jnp.dot(rows[...], stacked[:, at], preferred_element_type=F32) * UNITARY
         spectra = spectra.astype(BF16)
-        for quarter, out in enumerate((keep_ref, send_ref, keep_x_ref, send_x_ref)):
+        for half, out in enumerate((keep_ref, send_ref)):
             for i in range(2):
-                out[n * 2 + i] = spectra[quarter * ROWS : (quarter + 1) * ROWS, i * LANES : (i + 1) * LANES]
+                out[n * 2 + i] = spectra[half * HALF : (half + 1) * HALF, i * LANES : (i + 1) * LANES]
 
 
 def gridding(place, arrays):
     hbm = pl.BlockSpec(memory_space=pltpu.HBM)
     vector = pl.BlockSpec(memory_space=pltpu.VMEM)
-    quarter = jax.ShapeDtypeStruct((NBLK, ROWS, LANES), BF16)
+    half = jax.ShapeDtypeStruct((NBLK, HALF, LANES), BF16)
     plane = pltpu.VMEM((BLOCKS * 8, LANES), F32)
     return pl.pallas_call(
         gridding_kernel,
-        out_shape=[quarter] * 4
+        out_shape=[half] * 2
         + [
             jax.ShapeDtypeStruct((2 * ROWS_OUT, SUB), BF16),
             jax.ShapeDtypeStruct((ROWS_OUT, LANES), F32),
             jax.ShapeDtypeStruct((1, FAC), F32),
         ],
         in_specs=[pl.BlockSpec(memory_space=pltpu.SMEM)] + [hbm] * len(arrays),
-        out_specs=[vector] * 7,
+        out_specs=[vector] * 5,
         scratch_shapes=[
             pltpu.SMEM((1, BLOCKS), jnp.int32),
             plane, plane, plane, plane, plane, plane, plane,
@@ -237,7 +238,7 @@
             pltpu.VMEM((WIDTH, WIDTH), BF16),
             pltpu.VMEM((SUB, WIDTH), BF16),
             pltpu.VMEM((TILE, LANES), F32),
-            pltpu.SemaphoreType.DMA((12,)),
+            pltpu.SemaphoreType.DMA((10,)),
         ],
         compiler_params=pltpu.CompilerParams(vmem_limit_bytes=24 * 1024 * 1024),
         name="gridding",
@@ -248,26 +249,53 @@
     return pltpu.with_memory_space_constraint(array, pltpu.HBM)
 
 
+def pair_sum_kernel(arrived, *halves):
+    count = NBLK * NBLK // 2
+    for i, half in enumerate(halves):
+
+        @pl.loop(0, count // 8)
+        def _(n):
+            pairs = arrived[pl.ds(i * count + n * 8, 8)].astype(F32)
+            half[pl.ds(n * 8, 8)] = (pairs[:, 0] + pairs[:, 1]).astype(BF16)
+
+
+def pair_sum(arrived):
+    vector = pl.BlockSpec(memory_space=pltpu.VMEM)
+    half = jax.ShapeDtypeStruct((NBLK * NBLK // 2, QUARTER, LANES), BF16)
+    return pl.pallas_call(
+        pair_sum_kernel,
+        out_shape=[half] * 2,
+        in_specs=[vector],
+        out_specs=[vector] * 2,
+        compiler_params=pltpu.CompilerParams(vmem_limit_bytes=24 * 1024 * 1024),
+        name="pair_sum",
+    )(arrived)
+
+
 CHUNKS = 8
 
 
-def facet_kernel(own, by_core, by_x, by_both, left, taper_rows, taper_cols, right_hbm, out_hbm, right, mixture, image, sems):
+def facet_kernel(*refs):
+    parts = refs[:8]
+    left, taper_rows, taper_cols, right_hbm, out_hbm, right, mixture, image, sems = refs[8:]
     for chunk in range(CHUNKS):
         pltpu.make_async_copy(right_hbm.at[chunk], right.at[chunk], sems.at[chunk]).start()
     sign = jnp.where(lax.broadcasted_iota(jnp.int32, (1, LANES), 1) < CONTRIB, -UNITARY, UNITARY)
 
-    @pl.loop(0, NBLK // 2)
-    def _(n):
-        right_side = jnp.concatenate(
-            [jnp.concatenate([part[2 * n], part[2 * n + 1]], 1) for part in (own, by_core, by_x, by_both)], 0
-        )
-        both = jnp.dot(left[...], right_side, preferred_element_type=F32)
-        mixed = [
-            both[:ROWS_OUT, lanes] * UNITARY + pltpu.roll(both[ROWS_OUT:, lanes], CONTRIB, 1) * sign
-            for lanes in (slice(0, LANES), slice(LANES, 2 * LANES))
-        ]
-        at = pl.ds(pl.multiple_of(n * 2 * LANES, 2 * LANES), 2 * LANES)
-        mixture[:, at] = jnp.concatenate(mixed, 1).astype(BF16)
+    for half in range(2):
+
+        @pl.loop(0, NBLK // 4)
+        def _(n):
+            right_side = jnp.concatenate(
+                [jnp.concatenate([part[2 * n], part[2 * n + 1]], 1) for part in parts[half::2]], 0
+            )
+            both = jnp.dot(left[...], right_side, preferred_element_type=F32)
+            mixed = [
+                both[:ROWS_OUT, lanes] * UNITARY + pltpu.roll(both[ROWS_OUT:, lanes], CONTRIB, 1) * sign
+                for lanes in (slice(0, LANES), slice(LANES, 2 * LANES))
+            ]
+            first = pl.multiple_of((half * 2 + n) * 2 * LANES, 2 * LANES)
+            mixture[:, pl.ds(first, 2 * LANES)] = jnp.concatenate(mixed, 1).astype(BF16)
 
     width = 2 * FAC // CHUNKS
 
@@ -296,7 +324,7 @@
     return pl.pallas_call(
         facet_kernel,
         out_shape=jax.ShapeDtypeStruct((2, ROWS_OUT, FAC), F32),
-        in_specs=[vector] * 7 + [hbm],
+        in_specs=[vector] * 11 + [hbm],
         out_specs=hbm,
         scratch_shapes=[
             pltpu.VMEM((CHUNKS, WIDTH, 2 * FAC // CHUNKS), BF16),
@@ -315,34 +343,34 @@
 
 def shards(vis_coords, vis_values, tile_index):
     columns, rows, left, right, taper_rows, taper_cols, bell = (jnp.asarray(table) for table in tables())
-    place = lax.axis_index("vis").astype(jnp.int32).reshape(1)
-
-    def swap(array, bit):
-        return lax.ppermute(array, "vis", [(i, i ^ bit) for i in range(4)])
-
-    keep, send, keep_x, send_x, left, taper_rows, taper_cols = gridding(
+    place = (lax.axis_index("x_lo") * 2 + lax.axis_index("core")).astype(jnp.int32).reshape(1)
+
+    def swap(array, axis):
+        return lax.ppermute(array, axis, [(0, 1), (1, 0)])
+
+    keep, send, left, taper_rows, taper_cols = gridding(
         place,
         [
             tile_index, by_visibility_row(vis_coords), by_visibility_row(vis_values),
             columns, rows, bell, left, taper_rows, taper_cols,
         ],
     )
-    got_x = swap(send_x, 1)
-    got = swap(send, 1)
-    give = (keep_x.astype(F32) + got_x.astype(F32)).astype(BF16)
-    arrived = swap(give, 2)
-    total = (keep.astype(F32) + got.astype(F32) + arrived.astype(F32)).astype(BF16)
-    outgoing = total.reshape(NBLK * NBLK, QUARTER, LANES)
-    own = lax.all_to_all(outgoing, "grid", split_axis=0, concat_axis=0, tiled=True)
-    own = own.reshape(NBLK, ROWS, LANES)
-    by_x = swap(own, 2)
-    by_core = swap(own, 1)
-    by_both = swap(by_x, 1)
-    return facet((own, by_core, by_x, by_both), left, taper_rows, taper_cols, right)[None]
+    total = (keep.astype(F32) + swap(send, "core").astype(F32)).astype(BF16)
+    outgoing = total.reshape(NBLK * NBLK * 2, QUARTER, LANES)
+    arrived = lax.all_to_all(outgoing, ("grid", "x_lo"), split_axis=0, concat_axis=0, tiled=True)
+    halves = [half.reshape(NBLK // 2, ROWS, LANES) for half in pair_sum(arrived.reshape(NBLK * NBLK, 2, QUARTER, LANES))]
+    by_core = [swap(half, "core") for half in halves]
+    by_x = [swap(half, "x_lo") for half in halves]
+    by_both = [swap(half, "core") for half in by_x]
+    quarters = [*halves, *by_core, *by_x, *by_both]
+    return facet(quarters, left, taper_rows, taper_cols, right)[None]
 
 
 def solution(mesh):
-    placed = (P("grid", "vis", None, None), P("grid", "vis", None, None), P("grid", "vis"))
+    shape = (mesh.shape["grid"], 2, 2)
+    split = jax.sharding.Mesh(mesh.devices.reshape(shape), ("grid", "x_lo", "core"))
+    vis = ("x_lo", "core")
+    placed = (P("grid", vis, None, None), P("grid", vis, None, None), P("grid", vis))
     return jax.shard_map(
-        shards, mesh=mesh, in_specs=placed, out_specs=P("grid", None, "vis", None), check_vma=False
+        shards, mesh=split, in_specs=placed, out_specs=P("grid", None, vis, None), check_vma=False
     )

time: 65.7 us -> 63.3 us (0.963)
  waiting for transfers between devices: 10.9 us -> 2.52 us
  blocking collectives: 24.8 us -> 30.9 us
    ppermute x6 -> x7, waiting for transfers between devices: 10.9 us -> 2.52 us  [swap(): return lax.ppermute(array, axis, [(0, 1), (1, 0)])]
    all_to_all x1, blocking collectives: 24.8 us -> 30.9 us  [shards(): lax.all_to_all(outgoing, ('grid', 'x_lo'), split_axis=0, concat_axis=0, t...]
    ppermute x6 -> x7, starting transfers between devices: 12.3 us -> 12.1 us  [swap(): return lax.ppermute(array, axis, [(0, 1), (1, 0)])]
    pallas_call x1 -> x2, Pallas kernels: 12.7 us -> 12.7 us  [the longest x1 12.6 us: gridding(): pl.pallas_call(gridding_kernel, out_shape=[half] * 2 + [jax.ShapeDtypeStr...]
  transfers between devices with their start and end apart: 6 -> 7, of which waited for: 5 -> 2; matrix products, arithmetic and copies ran while one was open for 0% -> 0% of each run, Pallas kernels for 0% -> 0%
where the time goes in v2:
time: 63.3 us; the launch traced here: 63.2 us
  blocking collectives  30.9 us (49%)
  Pallas kernels  17.5 us (28%)
  starting transfers between devices  12.1 us (19%)
  waiting for transfers between devices  2.52 us (4%)
    all_to_all x1, blocking collectives, shards(): lax.all_to_all(outgoing, ('grid', 'x_lo'), split_axis=0, concat_axis=0, t...  30.9 us
    pallas_call x1, Pallas kernels, gridding(): pl.pallas_call(gridding_kernel, out_shape=[half] * 2 + [jax.ShapeDtypeStr...  12.6 us
    ppermute x7, starting transfers between devices, swap(): return lax.ppermute(array, axis, [(0, 1), (1, 0)])  12.1 us
    pallas_call x1, Pallas kernels, facet(): pl.pallas_call(facet_kernel, out_shape=jax.ShapeDtypeStruct((2, ROWS_OUT,...  4.79 us
    ppermute x7, waiting for transfers between devices, swap(): return lax.ppermute(array, axis, [(0, 1), (1, 0)])  2.52 us
  transfers between devices with their start and end apart: 7, of which 2 were waited for; matrix products, arithmetic and copies ran while one was open for 0% of the time, Pallas kernels for 0%

profile of v2, /device:TPU:1, one launch (start us, length us, event | category | flops | bytes accessed | tf_op | source)
XLA Modules:
  0.0 63.2 jit_solution(5698703058305403793)
XLA Ops:
  0.0 12.6 %gridding.1 = (bf16[8,256,128]{2,1,0:T(8,128)(2,1)S(1)}, bf16[8,256,128]{2,1,0:T(8,128)(2,1)S(1)}, bf16[512,512]{1,0:T(8,128)(2,1)S(1)}, f32[256,128]{1,0:T(8,128)S(1)}, f32[1,1024]{1,0:T(1,128)S(1)}) custom-call(s32[1]{0:T(128)} %bitcast.place_ref, s32[1,64]{1,0:T(1,128)} %tiles_hbm.1, f32[512,128]{1,0:T(8,128)} %bitcast.24, f32[512,128]{1,0:T(8,128)} %bitcast.25, ...), custom_call_target="tpu_custom_call" | custom-call | tf_op jit(solution)/shard_map/gridding/pallas_call | solution.py:220
  12.6 3.3 %collective-permute-start = (bf16[8,256,128]{2,1,0:T(8,128)(2,1)S(1)}, bf16[8,256,128]{2,1,0:T(8,128)(2,1)S(1)}, u32[]{:S(2)}, u32[]{:S(2)}) collective-permute-start(bf16[8,256,128]{2,1,0:T(8,128)(2,1)S(1)} %get-tuple-element.13), channel_id=1, source_target_pairs={{0,1},{1,0},{2,3},{3,2},{4,5},{5,4},{6,7},{7,6},{8,9},{9,8},{10,11... | collective-permute-start | bytes 1572872 | tf_op jit(solution)/shard_map/ppermute | solution.py:349
  16.0 1.5 %collective-permute-done = bf16[8,256,128]{2,1,0:T(8,128)(2,1)S(1)} collective-permute-done((bf16[8,256,128]{2,1,0:T(8,128)(2,1)S(1)}, bf16[8,256,128]{2,1,0:T(8,128)(2,1)S(1)}, u32[]{:S(2)}, u32[]{:S(2)}) %collective-permute-start) | collective-permute-done | bytes 524320 | tf_op jit(solution)/shard_map/ppermute | solution.py:349
  17.5 0.1 add_convert_fusion
  17.6 30.9 %all_to_all.5 = bf16[128,16,128]{2,1,0:T(8,128)(2,1)S(1)} all-to-all(bf16[128,16,128]{2,1,0:T(8,128)(2,1)S(1)} %bitcast.23), channel_id=1, replica_groups=mesh['grid'=64,'x_lo'=2,'core'=2] {'grid','x_lo'}, dimensions={0} | all-to-all | bytes 1048576 | tf_op jit(solution)/shard_map/all_to_all | solution.py:360
  48.5 0.1 pair_sum.1
  48.6 0.1 collective-permute-start.4
  48.7 1.5 %collective-permute-start.3 = (bf16[4,128,128]{2,1,0:T(8,128)(2,1)S(1)}, bf16[4,128,128]{2,1,0:T(8,128)(2,1)S(1)}, u32[]{:S(2)}, u32[]{:S(2)}) collective-permute-start(bf16[4,128,128]{2,1,0:T(8,128)(2,1)S(1)} %bitcast.17), channel_id=1, source_target_pairs={{0,2},{2,0},{1,3},{3,1},{4,6},{6,4},{5,7},{7,5},{8,10},{10,8},{9,1... | collective-permute-start | bytes 393224 | tf_op jit(solution)/shard_map/ppermute | solution.py:349
  50.2 2.9 %collective-permute-start.2 = (bf16[4,128,128]{2,1,0:T(8,128)(2,1)S(1)}, bf16[4,128,128]{2,1,0:T(8,128)(2,1)S(1)}, u32[]{:S(2)}, u32[]{:S(2)}) collective-permute-start(bf16[4,128,128]{2,1,0:T(8,128)(2,1)S(1)} %bitcast.21), channel_id=1, source_target_pairs={{0,1},{1,0},{2,3},{3,2},{4,5},{5,4},{6,7},{7,6},{8,9},{9,8},{10,11... | collective-permute-start | bytes 393224 | tf_op jit(solution)/shard_map/ppermute | solution.py:349
  53.1 0.0 collective-permute-start.1
  53.1 0.0 collective-permute-done.4.refs_5_
  53.1 2.9 %collective-permute-start.6 = (bf16[4,128,128]{2,1,0:T(8,128)(2,1)S(1)}, bf16[4,128,128]{2,1,0:T(8,128)(2,1)S(1)}, u32[]{:S(2)}, u32[]{:S(2)}) collective-permute-start(bf16[4,128,128]{2,1,0:T(8,128)(2,1)S(1)} %collective-permute-done.4.refs_5_), channel_id=1, source_target_pairs={{0,1},{1,0},{2,3},{3,2},{4,5},{5,4},{6,7},{7,6},{8,9},{9,8},{10,11... | collective-permute-start | bytes 393224 | tf_op jit(solution)/shard_map/ppermute | solution.py:349
  56.0 0.0 collective-permute-done.3.refs_4_
  56.0 1.4 %collective-permute-start.5 = (bf16[4,128,128]{2,1,0:T(8,128)(2,1)S(1)}, bf16[4,128,128]{2,1,0:T(8,128)(2,1)S(1)}, u32[]{:S(2)}, u32[]{:S(2)}) collective-permute-start(bf16[4,128,128]{2,1,0:T(8,128)(2,1)S(1)} %collective-permute-done.3.refs_4_), channel_id=1, source_target_pairs={{0,1},{1,0},{2,3},{3,2},{4,5},{5,4},{6,7},{7,6},{8,9},{9,8},{10,11... | collective-permute-start | bytes 393224 | tf_op jit(solution)/shard_map/ppermute | solution.py:349
  57.4 0.0 collective-permute-done.2.refs_3_
  57.4 0.0 collective-permute-done.1.refs_2_
  57.4 0.0 collective-permute-done.6.refs_7_
  57.5 1.0 %collective-permute-done.5.refs_6_ = bf16[4,128,128]{2,1,0:T(8,128)(2,1)S(1)} collective-permute-done((bf16[4,128,128]{2,1,0:T(8,128)(2,1)S(1)}, bf16[4,128,128]{2,1,0:T(8,128)(2,1)S(1)}, u32[]{:S(2)}, u32[]{:S(2)}) %collective-permute-start.5) | collective-permute-done | bytes 131104 | tf_op jit(solution)/shard_map/ppermute | solution.py:349
  58.4 4.8 %facet.1 = f32[2,256,1024]{2,1,0:T(8,128)} custom-call(bf16[4,128,128]{2,1,0:T(8,128)(2,1)S(1)} %bitcast.19, bf16[4,128,128]{2,1,0:T(8,128)(2,1)S(1)} %bitcast.22, bf16[4,128,128]{2,1,0:T(8,128)(2,1)S(1)} %collective-permute-done.1.refs_2_, bf16[4,128,128]{2,1,0:T(8,128)(2,1)S(1)} %collective-permute-done.2.refs_3_, ...), custom_call_target="tpu_custom_call" | custom-call | tf_op jit(solution)/shard_map/facet/pallas_call | solution.py:324
Async XLA Ops:
  12.6 4.9 %collective-permute-start = (bf16[8,256,128]{2,1,0:T(8,128)(2,1)S(1)}, bf16[8,256,128]{2,1,0:T(8,128)(2,1)S(1)}, u32[]{:S(2)}, u32[]{:S(2)}) collective-permute-start(bf16[8,256,128]{2,1,0:T(8,128)(2,1)S(1)} %get-tuple-element.13), channel_id=1, source_target_pairs={{0,1},{1,0},{2,3},{3,2},{4,5},{5,4},{6,7},{7,6},{8,9},{9,8},{10,11... | collective-permute-start | bytes 1572872 | tf_op jit(solution)/shard_map/ppermute | solution.py:349
  48.6 4.5 %collective-permute-start.4 = (bf16[4,128,128]{2,1,0:T(8,128)(2,1)S(1)}, bf16[4,128,128]{2,1,0:T(8,128)(2,1)S(1)}, u32[]{:S(2)}, u32[]{:S(2)}) collective-permute-start(bf16[4,128,128]{2,1,0:T(8,128)(2,1)S(1)} %bitcast.20), channel_id=1, source_target_pairs={{0,2},{2,0},{1,3},{3,1},{4,6},{6,4},{5,7},{7,5},{8,10},{10,8},{9,1... | collective-permute-start | bytes 393224 | tf_op jit(solution)/shard_map/ppermute | solution.py:349
  48.7 7.3 %collective-permute-start.3 = (bf16[4,128,128]{2,1,0:T(8,128)(2,1)S(1)}, bf16[4,128,128]{2,1,0:T(8,128)(2,1)S(1)}, u32[]{:S(2)}, u32[]{:S(2)}) collective-permute-start(bf16[4,128,128]{2,1,0:T(8,128)(2,1)S(1)} %bitcast.17), channel_id=1, source_target_pairs={{0,2},{2,0},{1,3},{3,1},{4,6},{6,4},{5,7},{7,5},{8,10},{10,8},{9,1... | collective-permute-start | bytes 393224 | tf_op jit(solution)/shard_map/ppermute | solution.py:349
  50.2 7.3 %collective-permute-start.2 = (bf16[4,128,128]{2,1,0:T(8,128)(2,1)S(1)}, bf16[4,128,128]{2,1,0:T(8,128)(2,1)S(1)}, u32[]{:S(2)}, u32[]{:S(2)}) collective-permute-start(bf16[4,128,128]{2,1,0:T(8,128)(2,1)S(1)} %bitcast.21), channel_id=1, source_target_pairs={{0,1},{1,0},{2,3},{3,2},{4,5},{5,4},{6,7},{7,6},{8,9},{9,8},{10,11... | collective-permute-start | bytes 393224 | tf_op jit(solution)/shard_map/ppermute | solution.py:349
  53.1 4.4 %collective-permute-start.1 = (bf16[4,128,128]{2,1,0:T(8,128)(2,1)S(1)}, bf16[4,128,128]{2,1,0:T(8,128)(2,1)S(1)}, u32[]{:S(2)}, u32[]{:S(2)}) collective-permute-start(bf16[4,128,128]{2,1,0:T(8,128)(2,1)S(1)} %bitcast.18), channel_id=1, source_target_pairs={{0,1},{1,0},{2,3},{3,2},{4,5},{5,4},{6,7},{7,6},{8,9},{9,8},{10,11... | collective-permute-start | bytes 393224 | tf_op jit(solution)/shard_map/ppermute | solution.py:349
  53.1 4.3 %collective-permute-start.6 = (bf16[4,128,128]{2,1,0:T(8,128)(2,1)S(1)}, bf16[4,128,128]{2,1,0:T(8,128)(2,1)S(1)}, u32[]{:S(2)}, u32[]{:S(2)}) collective-permute-start(bf16[4,128,128]{2,1,0:T(8,128)(2,1)S(1)} %collective-permute-done.4.refs_5_), channel_id=1, source_target_pairs={{0,1},{1,0},{2,3},{3,2},{4,5},{5,4},{6,7},{7,6},{8,9},{9,8},{10,11... | collective-permute-start | bytes 393224 | tf_op jit(solution)/shard_map/ppermute | solution.py:349
  56.0 2.4 %collective-permute-start.5 = (bf16[4,128,128]{2,1,0:T(8,128)(2,1)S(1)}, bf16[4,128,128]{2,1,0:T(8,128)(2,1)S(1)}, u32[]{:S(2)}, u32[]{:S(2)}) collective-permute-start(bf16[4,128,128]{2,1,0:T(8,128)(2,1)S(1)} %collective-permute-done.3.refs_4_), channel_id=1, source_target_pairs={{0,1},{1,0},{2,3},{3,2},{4,5},{5,4},{6,7},{7,6},{8,9},{9,8},{10,11... | collective-permute-start | bytes 393224 | tf_op jit(solution)/shard_map/ppermute | solution.py:349

commit v3 on v2

v3 whole, which is shorter than its diff:
```python
import functools
import math

import jax
import jax.numpy as jnp
import ml_dtypes
import numpy as np
from jax import lax
from jax.experimental import pallas as pl
from jax.experimental.pallas import tpu as pltpu
from jax.sharding import PartitionSpec as P

SUB = 512
FAC = 1024
CONTRIB = 64
TILE = 64
BLK = 512
BLOCKS = 64
GROUP = 16
CHUNKS = FAC // 2 // 128
NBLK = 8
LANES = 128
QUARTER = 16
ROWS = NBLK * QUARTER
HALF = 2 * ROWS
ROWS_OUT = FAC // 4
WIDTH = 2 * SUB
BF16 = jnp.bfloat16
F32 = jnp.float32


def angles(first, second, length):
    return (first[:, None] * second[None, :] % length) * (2.0 * math.pi / length)


def as_bf16(table):
    return np.ascontiguousarray(table.astype(np.float32)).astype(ml_dtypes.bfloat16)


@functools.lru_cache(maxsize=None)
def tables():
    spectrum = np.arange(SUB)
    turn = angles(spectrum, np.arange(SUB // 2), SUB)
    turn = turn.reshape(NBLK // 2, 2, TILE // 2, 2, NBLK // 2, CONTRIB // 2, 2).transpose(3, 0, 1, 2, 4, 6, 5)
    turn = np.stack([turn[0], turn[1][:, ::-1]])
    cos, sin = np.cos(turn), np.sin(turn)
    columns = np.empty((2, NBLK // 2, 2, 2, TILE // 2, NBLK // 2, 2, 2, CONTRIB // 2))
    columns[:, :, :, 0, :, :, 0] = cos
    columns[:, :, :, 1, :, :, 0] = sin
    columns[:, :, :, 0, :, :, 1] = -sin
    columns[:, :, :, 1, :, :, 1] = cos
    columns = as_bf16(columns.reshape(2, SUB, SUB))
    turn = angles(spectrum, np.arange(SUB // 4), SUB).reshape(ROWS, 4, SUB // 4).transpose(1, 0, 2)
    rows = as_bf16(np.concatenate([np.cos(turn), np.sin(turn)], 2))
    turn = angles(np.arange(FAC), spectrum, FAC).reshape(4, ROWS_OUT, NBLK, QUARTER, 4)
    left = np.empty((4, 2, ROWS_OUT, 4, NBLK, QUARTER))
    for g in range(4):
        for j in range(4):
            left[g, 0, :, j] = np.cos(turn[g, ..., g ^ j])
            left[g, 1, :, j] = np.sin(turn[g, ..., g ^ j])
    left = as_bf16(left.reshape(4, 2 * ROWS_OUT, SUB))
    turn = angles(spectrum, np.arange(FAC // 2), FAC).reshape(NBLK // 2, 2, CONTRIB // 2, 2, CHUNKS, LANES)
    turn = turn.transpose(3, 4, 0, 1, 2, 5)
    cos, sin = np.cos(turn), np.sin(turn)
    right = np.empty((2, CHUNKS, NBLK // 2, 2, 2, CONTRIB // 2, 2, LANES))
    right[:, :, :, 0, :, :, 0] = cos
    right[:, :, :, 1, :, :, 0] = -sin
    right[:, :, :, 0, :, :, 1] = sin
    right[:, :, :, 1, :, :, 1] = cos
    right = as_bf16(right.reshape(2, CHUNKS, SUB, 2 * LANES))
    sines = np.sin(math.pi * (np.arange(FAC) + 0.5) / FAC)
    taper = 0.25 + 0.75 * sines * sines
    taper_rows = np.broadcast_to(taper.reshape(4, ROWS_OUT, 1), (4, ROWS_OUT, LANES)).astype(np.float32)
    taper_cols = (taper / SUB).reshape(1, FAC).astype(np.float32)
    pixel = np.arange(TILE)
    bell = (1.0 - 2.0 * (pixel % 2)) * np.exp(-(pixel * pixel) / 256.0)
    across = bell.reshape(TILE // 2, 2).T
    across = np.stack([across, across[::-1]])[:, :, None, :].repeat(2, 2).reshape(2, 1, LANES)
    bell = (bell[:, None] * across / SUB).astype(np.float32)
    return columns, rows, left, right, np.ascontiguousarray(taper_rows), taper_cols, bell


SINE = [math.pi ** (2 * k + 1) * (-1) ** k / math.factorial(2 * k + 1) for k in range(7)]


def gridding_kernel(
    place_ref, tiles_hbm, coords_hbm, values_hbm, columns_hbm, rows_hbm, bell_hbm, left_hbm, taper_rows_hbm, taper_cols_hbm,
    keep_ref, send_ref, left_ref, taper_rows_ref, taper_cols_ref,
    tile_ref, coords, values, step8, slope, height, acc, grid16, halves, stacked, columns, rows, bell_ref,
    sems,
):
    place = place_ref[0]
    first = [(coords_hbm, coords), (values_hbm, values), (tiles_hbm, tile_ref)]
    later = [(columns_hbm, columns), (rows_hbm, rows), (bell_hbm, bell_ref)]
    last = [(left_hbm.at[place], left_ref), (taper_rows_hbm.at[place], taper_rows_ref), (taper_cols_hbm, taper_cols_ref)]
    copies = [pltpu.make_async_copy(*ends, sems.at[i]) for i, ends in enumerate(first + later + last)]
    for copy in copies:
        copy.start()
    acc[...] = jnp.zeros_like(acc)
    for copy in copies[: len(first)]:
        copy.wait()

    @pl.loop(0, BLOCKS * 8 // 64)
    def _(chunk):
        at = pl.ds(pl.multiple_of(chunk * 64, 64), 64)
        c = coords[at, :]
        r = jnp.round(c)
        c = jnp.where(c == r, c + (c * 2.0**-23 + 1e-20), c)
        f = c - r
        square = f * f
        sine = jnp.full_like(f, SINE[6])
        for k in range(5, -1, -1):
            sine = sine * square + SINE[k]
        half = r * 0.5
        odd = half - jnp.floor(half)
        sine = sine * f * ((1.0 - 4.0 * odd) * (1.0 / math.pi))
        coords[at, :] = c
        step8[at, :] = jnp.exp(c * (1.0 / 16.0))
        slope[at, :] = c * (1.0 / 128.0)
        height[at, :] = sine * jnp.exp(c * c * (-1.0 / 256.0))

    row_of = lax.broadcasted_iota(jnp.int32, (8, LANES), 0).astype(F32)

    def spread(ref, row, count=8):
        return jnp.broadcast_to(ref[pl.ds(row, 1), :], (count, LANES))

    rises = [row_of + 8.0 * a for a in range(8)]

    def taps(row, rises, ratio):
        c = spread(coords, row)
        w = spread(height, row) * jnp.exp(rises[0] * spread(slope, row))
        found = []
        for rise in rises:
            found.append(w * pl.reciprocal(rise - c, approx=True))
            w = w * ratio
        return jnp.concatenate(found, 0).astype(BF16)

    def patch_of(b):
        odd = (tile_ref[0, b] % 2).astype(F32)
        halves_v = [row_of * 2.0 + odd, row_of * 2.0 + (1.0 - odd)]
        rises_v = [[first + 16.0 * a for a in range(4)] for first in halves_v]
        u, v = [], [[] for _ in range(4)]
        for t in range(4):
            row = b * 8 + t * 2
            u.append(taps(row, rises, spread(step8, row)))
            ratio = spread(step8, row + 1)
            ratio = ratio * ratio
            found = [taps(row + 1, some, ratio) for some in rises_v]
            for part in range(2):
                value = spread(values, row + part, TILE // 2).astype(BF16)
                for half in range(2):
                    v[half * 2 + part].append(found[half] * value)
        u = jnp.concatenate(u, 1)
        v = jnp.concatenate([jnp.concatenate(piece, 1) for piece in v], 0)
        return lax.dot_general(u, v, (((1,), (1,)), ((), ())), preferred_element_type=F32)

    def deposit(b, patch):
        tile = tile_ref[0, b]
        at = (
            pl.ds(pl.multiple_of((tile // NBLK) * TILE, TILE), TILE),
            pl.ds(pl.multiple_of((tile % NBLK) * LANES, LANES), LANES),
        )
        acc[at] = acc[at] + patch

    @pl.loop(0, BLOCKS // GROUP)
    def _(group):
        held = None
        for i in range(GROUP):
            patch = patch_of(group * GROUP + i)
            if held is not None:
                deposit(group * GROUP + i - 1, held)
            held = patch
        deposit(group * GROUP + GROUP - 1, held)

    for copy in copies[len(first) :]:
        copy.wait()

    lane = lax.broadcasted_iota(jnp.int32, (1, LANES), 1)
    left_lane = lane < CONTRIB
    sign = jnp.where(left_lane, 1.0, -1.0)
    sign16 = jnp.broadcast_to(sign, (QUARTER, LANES)).astype(BF16)
    step = SUB // 4

    @pl.loop(0, NBLK)
    def _(a):
        at = pl.ds(pl.multiple_of(a * TILE, TILE), TILE)
        for e in range(NBLK // 2):
            even = acc[at, 2 * e * LANES : (2 * e + 1) * LANES] * bell_ref[0]
            odd = acc[at, (2 * e + 1) * LANES : (2 * e + 2) * LANES] * bell_ref[1]
            lanes = slice(e * LANES, (e + 1) * LANES)
            grid16[0, at, lanes] = jnp.where(left_lane, even, odd).astype(BF16)
            grid16[1, at, lanes] = jnp.where(left_lane, odd, even).astype(BF16)

    @pl.loop(0, SUB // 256)
    def _(n):
        at = pl.ds(pl.multiple_of(n * 256, 256), 256)
        for h in range(2):
            halves[h, :, at] = jnp.dot(grid16[h], columns[h, :, at], preferred_element_type=F32)

    @pl.loop(0, step // QUARTER)
    def _(m):
        first = pl.multiple_of(m * QUARTER, QUARTER)
        for i in range(NBLK // 2):
            lanes = slice(i * LANES, (i + 1) * LANES)
            low, high = [], []
            for q in range(4):
                some = halves[0, pl.ds(first + q * step, QUARTER), lanes]
                other = halves[1, pl.ds(first + q * step, QUARTER), lanes]
                low.append(some + other)
                high.append(some - other)
            for image, block in ((low, i), (high, i + NBLK // 2)):
                into = slice(block * LANES, (block + 1) * LANES)
                sum02, diff02 = image[0] + image[2], image[0] - image[2]
                sum13, diff13 = image[1] + image[3], image[1] - image[3]
                turned13 = pltpu.roll(diff13, CONTRIB, 1) * sign
                for v, x in enumerate((sum02 + sum13, diff02 + turned13, sum02 - sum13, diff02 - turned13)):
                    x = x.astype(BF16)
                    stacked[v, pl.ds(first, QUARTER), into] = x
                    stacked[v, pl.ds(first + step, QUARTER), into] = pltpu.roll(x, CONTRIB, 1) * sign16

    core = place % 2

    @pl.loop(0, WIDTH // 256)
    def _(n):
        at = pl.ds(pl.multiple_of(n * 256, 256), 256)
        for which, out in ((core, keep_ref), (1 - core, send_ref)):
            for x_lo in range(2):
                v = which + 2 * x_lo
                spectra = jnp.dot(rows[v], stacked[v, :, at], preferred_element_type=F32).astype(BF16)
                for i in range(2):
                    for ra in range(NBLK):
                        first = (ra * 2 + x_lo) * QUARTER
                        block = spectra[ra * QUARTER : (ra + 1) * QUARTER, i * LANES : (i + 1) * LANES]
                        out[n * 2 + i, first : first + QUARTER] = block


def gridding(place, arrays):
    hbm = pl.BlockSpec(memory_space=pltpu.HBM)
    vector = pl.BlockSpec(memory_space=pltpu.VMEM)
    half = jax.ShapeDtypeStruct((NBLK, HALF, LANES), BF16)
    plane = pltpu.VMEM((BLOCKS * 8, LANES), F32)
    return pl.pallas_call(
        gridding_kernel,
        out_shape=[half] * 2
        + [
            jax.ShapeDtypeStruct((2 * ROWS_OUT, SUB), BF16),
            jax.ShapeDtypeStruct((ROWS_OUT, LANES), F32),
            jax.ShapeDtypeStruct((1, FAC), F32),
        ],
        in_specs=[pl.BlockSpec(memory_space=pltpu.SMEM)] + [hbm] * len(arrays),
        out_specs=[vector] * 5,
        scratch_shapes=[
            pltpu.SMEM((1, BLOCKS), jnp.int32),
            plane, plane, plane, plane, plane,
            pltpu.VMEM((SUB, WIDTH), F32),
            pltpu.VMEM((2, SUB, SUB), BF16),
            pltpu.VMEM((2, SUB, SUB), F32),
            pltpu.VMEM((4, SUB // 2, WIDTH), BF16),
            pltpu.VMEM((2, SUB, SUB), BF16),
            pltpu.VMEM((4, ROWS, SUB // 2), BF16),
            pltpu.VMEM((2, TILE, LANES), F32),
            pltpu.SemaphoreType.DMA((9,)),
        ],
        compiler_params=pltpu.CompilerParams(vmem_limit_bytes=24 * 1024 * 1024),
        name="gridding",
    )(place, *(stay(array) for array in arrays))


def stay(array):
    return pltpu.with_memory_space_constraint(array, pltpu.HBM)


def pair_sum_kernel(arrived, *halves):
    count = NBLK * NBLK // 2
    for i, half in enumerate(halves):

        @pl.loop(0, count // 8)
        def _(n):
            pairs = arrived[pl.ds(i * count + n * 8, 8)].astype(F32)
            half[pl.ds(n * 8, 8)] = (pairs[:, 0] + pairs[:, 1]).astype(BF16)


def pair_sum(arrived):
    vector = pl.BlockSpec(memory_space=pltpu.VMEM)
    half = jax.ShapeDtypeStruct((NBLK * NBLK // 2, QUARTER, LANES), BF16)
    return pl.pallas_call(
        pair_sum_kernel,
        out_shape=[half] * 2,
        in_specs=[vector],
        out_specs=[vector] * 2,
        compiler_params=pltpu.CompilerParams(vmem_limit_bytes=24 * 1024 * 1024),
        name="pair_sum",
    )(arrived)


def facet_kernel(*refs):
    parts = refs[:8]
    left, taper_rows, taper_cols, right_hbm, out_hbm, right, mixture, image, sems = refs[8:]
    for chunk in range(CHUNKS):
        pltpu.make_async_copy(right_hbm.at[:, chunk], right.at[:, chunk], sems.at[chunk]).start()
    lane = lax.broadcasted_iota(jnp.int32, (1, LANES), 1)
    sign = jnp.where(lane < CONTRIB, -1.0, 1.0)
    even = lane % CONTRIB < CONTRIB // 2
    for half in range(2):

        @pl.loop(0, NBLK // 4)
        def _(n):
            right_side = jnp.concatenate(
                [jnp.concatenate([part[2 * n], part[2 * n + 1]], 1) for part in parts[half::2]], 0
            )
            both = jnp.dot(left[...], right_side, preferred_element_type=F32)
            first, second = (
                both[:ROWS_OUT, lanes] + pltpu.roll(both[ROWS_OUT:, lanes], CONTRIB, 1) * sign
                for lanes in (slice(0, LANES), slice(LANES, 2 * LANES))
            )
            into = pl.ds(pl.multiple_of((half * 2 + n) * LANES, LANES), LANES)
            mixture[0, :, into] = jnp.where(even, first, pltpu.roll(second, CONTRIB // 2, 1)).astype(BF16)
            mixture[1, :, into] = jnp.where(even, pltpu.roll(first, LANES - CONTRIB // 2, 1), second).astype(BF16)

    def departures(chunk):
        copies = []
        for part in range(2):
            for half in range(2):
                first = pl.multiple_of(half * (FAC // 2) + chunk * LANES, LANES)
                into = out_hbm.at[part, :, pl.ds(first, LANES)]
                sem = sems.at[CHUNKS + chunk * 4 + part * 2 + half]
                copies.append(pltpu.make_async_copy(image.at[chunk, part, half], into, sem))
        return copies

    @pl.loop(0, CHUNKS)
    def _(chunk):
        pltpu.make_async_copy(right_hbm.at[:, chunk], right.at[:, chunk], sems.at[chunk]).wait()
        evens = jnp.dot(mixture[0], right[0, chunk], preferred_element_type=F32)
        odds = jnp.dot(mixture[1], right[1, chunk], preferred_element_type=F32)
        weights = [
            taper_rows[...] * taper_cols[:, pl.ds(pl.multiple_of(half * (FAC // 2) + chunk * LANES, LANES), LANES)]
            for half in range(2)
        ]
        for part in range(2):
            lanes = slice(part * LANES, (part + 1) * LANES)
            image[chunk, part, 0] = (evens[:, lanes] + odds[:, lanes]) * weights[0]
            image[chunk, part, 1] = (evens[:, lanes] - odds[:, lanes]) * weights[1]
        for copy in departures(chunk):
            copy.start()

    for chunk in range(CHUNKS):
        for copy in departures(chunk):
            copy.wait()


def facet(quarters, left, taper_rows, taper_cols, right):
    vector = pl.BlockSpec(memory_space=pltpu.VMEM)
    hbm = pl.BlockSpec(memory_space=pltpu.HBM)
    return pl.pallas_call(
        facet_kernel,
        out_shape=jax.ShapeDtypeStruct((2, ROWS_OUT, FAC), F32),
        in_specs=[vector] * 11 + [hbm],
        out_specs=hbm,
        scratch_shapes=[
            pltpu.VMEM((2, CHUNKS, SUB, 2 * LANES), BF16),
            pltpu.VMEM((2, ROWS_OUT, SUB), BF16),
            pltpu.VMEM((CHUNKS, 2, 2, ROWS_OUT, LANES), F32),
            pltpu.SemaphoreType.DMA((5 * CHUNKS,)),
        ],
        compiler_params=pltpu.CompilerParams(vmem_limit_bytes=24 * 1024 * 1024),
        name="facet",
    )(*quarters, left, taper_rows, taper_cols, stay(right))


def by_visibility_row(array):
    return array.reshape(BLOCKS, 2, BLK // LANES, LANES).transpose(0, 2, 1, 3).reshape(BLOCKS * 8, LANES)


def shards(vis_coords, vis_values, tile_index):
    columns, rows, left, right, taper_rows, taper_cols, bell = (jnp.asarray(table) for table in tables())
    place = (lax.axis_index("x_lo") * 2 + lax.axis_index("core")).astype(jnp.int32).reshape(1)

    def swap(array, axis):
        return lax.ppermute(array, axis, [(0, 1), (1, 0)])

    keep, send, left, taper_rows, taper_cols = gridding(
        place,
        [
            tile_index, by_visibility_row(vis_coords), by_visibility_row(vis_values),
            columns, rows, bell, left, taper_rows, taper_cols,
        ],
    )
    total = (keep.astype(F32) + swap(send, "core").astype(F32)).astype(BF16)
    outgoing = total.reshape(NBLK * NBLK * 2, QUARTER, LANES)
    arrived = lax.all_to_all(outgoing, ("grid", "x_lo"), split_axis=0, concat_axis=0, tiled=True)
    halves = [half.reshape(NBLK // 2, ROWS, LANES) for half in pair_sum(arrived.reshape(NBLK * NBLK, 2, QUARTER, LANES))]
    by_core = [swap(half, "core") for half in halves]
    by_x = [swap(half, "x_lo") for half in halves]
    by_both = [swap(half, "core") for half in by_x]
    quarters = [*halves, *by_core, *by_x, *by_both]
    return facet(quarters, left, taper_rows, taper_cols, right)[None]


def solution(mesh):
    shape = (mesh.shape["grid"], 2, 2)
    split = jax.sharding.Mesh(mesh.devices.reshape(shape), ("grid", "x_lo", "core"))
    vis = ("x_lo", "core")
    placed = (P("grid", vis, None, None), P("grid", vis, None, None), P("grid", vis))
    return jax.shard_map(
        shards, mesh=split, in_specs=placed, out_specs=P("grid", None, vis, None), check_vma=False
    )
```

time: 63.3 us -> 59.9 us (0.946)
  Pallas kernels: 17.5 us -> 14.1 us
    pallas_call x1, Pallas kernels: 12.6 us -> 10 us  [gridding(): pl.pallas_call(gridding_kernel, out_shape=[half] * 2 + [jax.ShapeDtypeStr...]
    pallas_call x1, Pallas kernels: 4.79 us -> 3.99 us  [facet(): pl.pallas_call(facet_kernel, out_shape=jax.ShapeDtypeStruct((2, ROWS_OUT,...]
where the time goes in v3:
time: 59.9 us; the launch traced here: 59.8 us
  blocking collectives  30.9 us (52%)
  Pallas kernels  14.1 us (24%)
  starting transfers between devices  12.1 us (20%)
  waiting for transfers between devices  2.52 us (4%)
    all_to_all x1, blocking collectives, shards(): lax.all_to_all(outgoing, ('grid', 'x_lo'), split_axis=0, concat_axis=0, t...  30.9 us
    ppermute x7, starting transfers between devices, swap(): return lax.ppermute(array, axis, [(0, 1), (1, 0)])  12.1 us
    pallas_call x1, Pallas kernels, gridding(): pl.pallas_call(gridding_kernel, out_shape=[half] * 2 + [jax.ShapeDtypeStr...  10 us
    pallas_call x1, Pallas kernels, facet(): pl.pallas_call(facet_kernel, out_shape=jax.ShapeDtypeStruct((2, ROWS_OUT,...  3.99 us
    ppermute x7, waiting for transfers between devices, swap(): return lax.ppermute(array, axis, [(0, 1), (1, 0)])  2.52 us
  transfers between devices with their start and end apart: 7, of which 2 were waited for; matrix products, arithmetic and copies ran while one was open for 0% of the time, Pallas kernels for 0%

profile of v3, /device:TPU:1, one launch (start us, length us, event | category | flops | bytes accessed | tf_op | source)
XLA Modules:
  0.0 59.8 jit_solution(11622031525512792932)
XLA Ops:
  0.0 10.0 %gridding.1 = (bf16[8,256,128]{2,1,0:T(8,128)(2,1)S(1)}, bf16[8,256,128]{2,1,0:T(8,128)(2,1)S(1)}, bf16[512,512]{1,0:T(8,128)(2,1)S(1)}, f32[256,128]{1,0:T(8,128)S(1)}, f32[1,1024]{1,0:T(1,128)S(1)}) custom-call(s32[1]{0:T(128)} %bitcast.place_ref, s32[1,64]{1,0:T(1,128)} %tiles_hbm.1, f32[512,128]{1,0:T(8,128)} %bitcast.24, f32[512,128]{1,0:T(8,128)} %bitcast.25, ...), custom_call_target="tpu_custom_call" | custom-call | tf_op jit(solution)/shard_map/gridding/pallas_call | solution.py:242
  10.0 3.3 %collective-permute-start = (bf16[8,256,128]{2,1,0:T(8,128)(2,1)S(1)}, bf16[8,256,128]{2,1,0:T(8,128)(2,1)S(1)}, u32[]{:S(2)}, u32[]{:S(2)}) collective-permute-start(bf16[8,256,128]{2,1,0:T(8,128)(2,1)S(1)} %get-tuple-element.13), channel_id=1, source_target_pairs={{0,1},{1,0},{2,3},{3,2},{4,5},{5,4},{6,7},{7,6},{8,9},{9,8},{10,11... | collective-permute-start | bytes 1572872 | tf_op jit(solution)/shard_map/ppermute | solution.py:379
  13.4 1.5 %collective-permute-done = bf16[8,256,128]{2,1,0:T(8,128)(2,1)S(1)} collective-permute-done((bf16[8,256,128]{2,1,0:T(8,128)(2,1)S(1)}, bf16[8,256,128]{2,1,0:T(8,128)(2,1)S(1)}, u32[]{:S(2)}, u32[]{:S(2)}) %collective-permute-start) | collective-permute-done | bytes 524320 | tf_op jit(solution)/shard_map/ppermute | solution.py:379
  14.9 0.1 add_convert_fusion
  15.0 30.9 %all_to_all.5 = bf16[128,16,128]{2,1,0:T(8,128)(2,1)S(1)} all-to-all(bf16[128,16,128]{2,1,0:T(8,128)(2,1)S(1)} %bitcast.23), channel_id=1, replica_groups=mesh['grid'=64,'x_lo'=2,'core'=2] {'grid','x_lo'}, dimensions={0} | all-to-all | bytes 1048576 | tf_op jit(solution)/shard_map/all_to_all | solution.py:390
  45.9 0.1 pair_sum.1
  46.0 0.1 collective-permute-start.4
  46.1 1.5 %collective-permute-start.3 = (bf16[4,128,128]{2,1,0:T(8,128)(2,1)S(1)}, bf16[4,128,128]{2,1,0:T(8,128)(2,1)S(1)}, u32[]{:S(2)}, u32[]{:S(2)}) collective-permute-start(bf16[4,128,128]{2,1,0:T(8,128)(2,1)S(1)} %bitcast.17), channel_id=1, source_target_pairs={{0,2},{2,0},{1,3},{3,1},{4,6},{6,4},{5,7},{7,5},{8,10},{10,8},{9,1... | collective-permute-start | bytes 393224 | tf_op jit(solution)/shard_map/ppermute | solution.py:379
  47.6 2.9 %collective-permute-start.2 = (bf16[4,128,128]{2,1,0:T(8,128)(2,1)S(1)}, bf16[4,128,128]{2,1,0:T(8,128)(2,1)S(1)}, u32[]{:S(2)}, u32[]{:S(2)}) collective-permute-start(bf16[4,128,128]{2,1,0:T(8,128)(2,1)S(1)} %bitcast.21), channel_id=1, source_target_pairs={{0,1},{1,0},{2,3},{3,2},{4,5},{5,4},{6,7},{7,6},{8,9},{9,8},{10,11... | collective-permute-start | bytes 393224 | tf_op jit(solution)/shard_map/ppermute | solution.py:379
  50.5 0.0 collective-permute-start.1
  50.5 0.0 collective-permute-done.4.refs_5_
  50.5 2.9 %collective-permute-start.6 = (bf16[4,128,128]{2,1,0:T(8,128)(2,1)S(1)}, bf16[4,128,128]{2,1,0:T(8,128)(2,1)S(1)}, u32[]{:S(2)}, u32[]{:S(2)}) collective-permute-start(bf16[4,128,128]{2,1,0:T(8,128)(2,1)S(1)} %collective-permute-done.4.refs_5_), channel_id=1, source_target_pairs={{0,1},{1,0},{2,3},{3,2},{4,5},{5,4},{6,7},{7,6},{8,9},{9,8},{10,11... | collective-permute-start | bytes 393224 | tf_op jit(solution)/shard_map/ppermute | solution.py:379
  53.4 0.0 collective-permute-done.3.refs_4_
  53.4 1.4 %collective-permute-start.5 = (bf16[4,128,128]{2,1,0:T(8,128)(2,1)S(1)}, bf16[4,128,128]{2,1,0:T(8,128)(2,1)S(1)}, u32[]{:S(2)}, u32[]{:S(2)}) collective-permute-start(bf16[4,128,128]{2,1,0:T(8,128)(2,1)S(1)} %collective-permute-done.3.refs_4_), channel_id=1, source_target_pairs={{0,1},{1,0},{2,3},{3,2},{4,5},{5,4},{6,7},{7,6},{8,9},{9,8},{10,11... | collective-permute-start | bytes 393224 | tf_op jit(solution)/shard_map/ppermute | solution.py:379
  54.8 0.0 collective-permute-done.2.refs_3_
  54.8 0.0 collective-permute-done.1.refs_2_
  54.8 0.0 collective-permute-done.6.refs_7_
  54.8 1.0 %collective-permute-done.5.refs_6_ = bf16[4,128,128]{2,1,0:T(8,128)(2,1)S(1)} collective-permute-done((bf16[4,128,128]{2,1,0:T(8,128)(2,1)S(1)}, bf16[4,128,128]{2,1,0:T(8,128)(2,1)S(1)}, u32[]{:S(2)}, u32[]{:S(2)}) %collective-permute-start.5) | collective-permute-done | bytes 131104 | tf_op jit(solution)/shard_map/ppermute | solution.py:379
  55.8 4.0 %facet.1 = f32[2,256,1024]{2,1,0:T(8,128)} custom-call(bf16[4,128,128]{2,1,0:T(8,128)(2,1)S(1)} %bitcast.19, bf16[4,128,128]{2,1,0:T(8,128)(2,1)S(1)} %bitcast.22, bf16[4,128,128]{2,1,0:T(8,128)(2,1)S(1)} %collective-permute-done.1.refs_2_, bf16[4,128,128]{2,1,0:T(8,128)(2,1)S(1)} %collective-permute-done.2.refs_3_, ...), custom_call_target="tpu_custom_call" | custom-call | tf_op jit(solution)/shard_map/facet/pallas_call | solution.py:354
Async XLA Ops:
  10.0 4.9 %collective-permute-start = (bf16[8,256,128]{2,1,0:T(8,128)(2,1)S(1)}, bf16[8,256,128]{2,1,0:T(8,128)(2,1)S(1)}, u32[]{:S(2)}, u32[]{:S(2)}) collective-permute-start(bf16[8,256,128]{2,1,0:T(8,128)(2,1)S(1)} %get-tuple-element.13), channel_id=1, source_target_pairs={{0,1},{1,0},{2,3},{3,2},{4,5},{5,4},{6,7},{7,6},{8,9},{9,8},{10,11... | collective-permute-start | bytes 1572872 | tf_op jit(solution)/shard_map/ppermute | solution.py:379
  46.0 4.5 %collective-permute-start.4 = (bf16[4,128,128]{2,1,0:T(8,128)(2,1)S(1)}, bf16[4,128,128]{2,1,0:T(8,128)(2,1)S(1)}, u32[]{:S(2)}, u32[]{:S(2)}) collective-permute-start(bf16[4,128,128]{2,1,0:T(8,128)(2,1)S(1)} %bitcast.20), channel_id=1, source_target_pairs={{0,2},{2,0},{1,3},{3,1},{4,6},{6,4},{5,7},{7,5},{8,10},{10,8},{9,1... | collective-permute-start | bytes 393224 | tf_op jit(solution)/shard_map/ppermute | solution.py:379
  46.1 7.3 %collective-permute-start.3 = (bf16[4,128,128]{2,1,0:T(8,128)(2,1)S(1)}, bf16[4,128,128]{2,1,0:T(8,128)(2,1)S(1)}, u32[]{:S(2)}, u32[]{:S(2)}) collective-permute-start(bf16[4,128,128]{2,1,0:T(8,128)(2,1)S(1)} %bitcast.17), channel_id=1, source_target_pairs={{0,2},{2,0},{1,3},{3,1},{4,6},{6,4},{5,7},{7,5},{8,10},{10,8},{9,1... | collective-permute-start | bytes 393224 | tf_op jit(solution)/shard_map/ppermute | solution.py:379
  47.6 7.3 %collective-permute-start.2 = (bf16[4,128,128]{2,1,0:T(8,128)(2,1)S(1)}, bf16[4,128,128]{2,1,0:T(8,128)(2,1)S(1)}, u32[]{:S(2)}, u32[]{:S(2)}) collective-permute-start(bf16[4,128,128]{2,1,0:T(8,128)(2,1)S(1)} %bitcast.21), channel_id=1, source_target_pairs={{0,1},{1,0},{2,3},{3,2},{4,5},{5,4},{6,7},{7,6},{8,9},{9,8},{10,11... | collective-permute-start | bytes 393224 | tf_op jit(solution)/shard_map/ppermute | solution.py:379
  50.5 4.4 %collective-permute-start.1 = (bf16[4,128,128]{2,1,0:T(8,128)(2,1)S(1)}, bf16[4,128,128]{2,1,0:T(8,128)(2,1)S(1)}, u32[]{:S(2)}, u32[]{:S(2)}) collective-permute-start(bf16[4,128,128]{2,1,0:T(8,128)(2,1)S(1)} %bitcast.18), channel_id=1, source_target_pairs={{0,1},{1,0},{2,3},{3,2},{4,5},{5,4},{6,7},{7,6},{8,9},{9,8},{10,11... | collective-permute-start | bytes 393224 | tf_op jit(solution)/shard_map/ppermute | solution.py:379
  50.5 4.3 %collective-permute-start.6 = (bf16[4,128,128]{2,1,0:T(8,128)(2,1)S(1)}, bf16[4,128,128]{2,1,0:T(8,128)(2,1)S(1)}, u32[]{:S(2)}, u32[]{:S(2)}) collective-permute-start(bf16[4,128,128]{2,1,0:T(8,128)(2,1)S(1)} %collective-permute-done.4.refs_5_), channel_id=1, source_target_pairs={{0,1},{1,0},{2,3},{3,2},{4,5},{5,4},{6,7},{7,6},{8,9},{9,8},{10,11... | collective-permute-start | bytes 393224 | tf_op jit(solution)/shard_map/ppermute | solution.py:379
  53.4 2.4 %collective-permute-start.5 = (bf16[4,128,128]{2,1,0:T(8,128)(2,1)S(1)}, bf16[4,128,128]{2,1,0:T(8,128)(2,1)S(1)}, u32[]{:S(2)}, u32[]{:S(2)}) collective-permute-start(bf16[4,128,128]{2,1,0:T(8,128)(2,1)S(1)} %collective-permute-done.3.refs_4_), channel_id=1, source_target_pairs={{0,1},{1,0},{2,3},{3,2},{4,5},{5,4},{6,7},{7,6},{8,9},{9,8},{10,11... | collective-permute-start | bytes 393224 | tf_op jit(solution)/shard_map/ppermute | solution.py:379

commit v4 on v3

--- a/solution.py
+++ b/solution.py
@@ -293,29 +293,56 @@
     )(arrived)
 
 
-def facet_kernel(*refs):
-    parts = refs[:8]
-    left, taper_rows, taper_cols, right_hbm, out_hbm, right, mixture, image, sems = refs[8:]
-    for chunk in range(CHUNKS):
-        pltpu.make_async_copy(right_hbm.at[:, chunk], right.at[:, chunk], sems.at[chunk]).start()
+def mix(parts, left, products, mixture):
     lane = lax.broadcasted_iota(jnp.int32, (1, LANES), 1)
     sign = jnp.where(lane < CONTRIB, -1.0, 1.0)
     even = lane % CONTRIB < CONTRIB // 2
-    for half in range(2):
-
-        @pl.loop(0, NBLK // 4)
-        def _(n):
-            right_side = jnp.concatenate(
-                [jnp.concatenate([part[2 * n], part[2 * n + 1]], 1) for part in parts[half::2]], 0
-            )
-            both = jnp.dot(left[...], right_side, preferred_element_type=F32)
+    for n in range(NBLK // 4):
+        right_side = jnp.concatenate(
+            [jnp.concatenate([part[2 * n], part[2 * n + 1]], 1) for part in parts], 0
+        )
+        products[n] = jnp.dot(left[...], right_side, preferred_element_type=F32)
+
+    for n in range(NBLK // 4):
+        into = slice(n * LANES, (n + 1) * LANES)
+
+        @pl.loop(0, ROWS_OUT // 64)
+        def _(m):
+            at = pl.ds(pl.multiple_of(m * 64, 64), 64)
+            below = pl.ds(pl.multiple_of(ROWS_OUT + m * 64, 64), 64)
             first, second = (
-                both[:ROWS_OUT, lanes] + pltpu.roll(both[ROWS_OUT:, lanes], CONTRIB, 1) * sign
+                products[n, at, lanes] + pltpu.roll(products[n, below, lanes], CONTRIB, 1) * sign
                 for lanes in (slice(0, LANES), slice(LANES, 2 * LANES))
             )
-            into = pl.ds(pl.multiple_of((half * 2 + n) * LANES, LANES), LANES)
-            mixture[0, :, into] = jnp.where(even, first, pltpu.roll(second, CONTRIB // 2, 1)).astype(BF16)
-            mixture[1, :, into] = jnp.where(even, pltpu.roll(first, LANES - CONTRIB // 2, 1), second).astype(BF16)
+            mixture[0, at, into] = jnp.where(even, first, pltpu.roll(second, CONTRIB // 2, 1)).astype(BF16)
+            mixture[1, at, into] = jnp.where(even, pltpu.roll(first, LANES - CONTRIB // 2, 1), second).astype(BF16)
+
+
+def mixture_kernel(own, by_core, by_x, by_both, left, mixture, products):
+    mix((own, by_core, by_x, by_both), left, products, mixture)
+
+
+def mixture_half(quarters, left):
+    vector = pl.BlockSpec(memory_space=pltpu.VMEM)
+    return pl.pallas_call(
+        mixture_kernel,
+        out_shape=jax.ShapeDtypeStruct((2, ROWS_OUT, SUB // 2), BF16),
+        in_specs=[vector] * 5,
+        out_specs=vector,
+        scratch_shapes=[pltpu.VMEM((NBLK // 4, 2 * ROWS_OUT, 2 * LANES), F32)],
+        compiler_params=pltpu.CompilerParams(vmem_limit_bytes=24 * 1024 * 1024),
+        cost_estimate=pl.CostEstimate(flops=2**28, bytes_accessed=2**20, transcendentals=0),
+        name="mixture_half",
+    )(*quarters, left)
+
+
+def facet_kernel(
+    own, by_core, by_x, by_both, half_mixture, left, taper_rows, taper_cols, right_hbm, out_hbm,
+    right, mixture, products, image, sems,
+):
+    for chunk in range(CHUNKS):
+        pltpu.make_async_copy(right_hbm.at[:, chunk], right.at[:, chunk], sems.at[chunk]).start()
+    mix((own, by_core, by_x, by_both), left, products, mixture)
 
     def departures(chunk):
         copies = []
@@ -330,8 +357,12 @@
     @pl.loop(0, CHUNKS)
     def _(chunk):
         pltpu.make_async_copy(right_hbm.at[:, chunk], right.at[:, chunk], sems.at[chunk]).wait()
-        evens = jnp.dot(mixture[0], right[0, chunk], preferred_element_type=F32)
-        odds = jnp.dot(mixture[1], right[1, chunk], preferred_element_type=F32)
+        evens, odds = (
+            jnp.dot(
+                jnp.concatenate([half_mixture[r], mixture[r]], 1), right[r, chunk], preferred_element_type=F32
+            )
+            for r in range(2)
+        )
         weights = [
             taper_rows[...] * taper_cols[:, pl.ds(pl.multiple_of(half * (FAC // 2) + chunk * LANES, LANES), LANES)]
             for half in range(2)
@@ -348,23 +379,24 @@
             copy.wait()
 
 
-def facet(quarters, left, taper_rows, taper_cols, right):
+def facet(quarters, half_mixture, left, taper_rows, taper_cols, right):
     vector = pl.BlockSpec(memory_space=pltpu.VMEM)
     hbm = pl.BlockSpec(memory_space=pltpu.HBM)
     return pl.pallas_call(
         facet_kernel,
         out_shape=jax.ShapeDtypeStruct((2, ROWS_OUT, FAC), F32),
-        in_specs=[vector] * 11 + [hbm],
+        in_specs=[vector] * 8 + [hbm],
         out_specs=hbm,
         scratch_shapes=[
             pltpu.VMEM((2, CHUNKS, SUB, 2 * LANES), BF16),
-            pltpu.VMEM((2, ROWS_OUT, SUB), BF16),
+            pltpu.VMEM((2, ROWS_OUT, SUB // 2), BF16),
+            pltpu.VMEM((NBLK // 4, 2 * ROWS_OUT, 2 * LANES), F32),
             pltpu.VMEM((CHUNKS, 2, 2, ROWS_OUT, LANES), F32),
             pltpu.SemaphoreType.DMA((5 * CHUNKS,)),
         ],
         compiler_params=pltpu.CompilerParams(vmem_limit_bytes=24 * 1024 * 1024),
         name="facet",
-    )(*quarters, left, taper_rows, taper_cols, stay(right))
+    )(*quarters, half_mixture, left, taper_rows, taper_cols, stay(right))
 
 
 def by_visibility_row(array):
@@ -392,8 +424,9 @@
     by_core = [swap(half, "core") for half in halves]
     by_x = [swap(half, "x_lo") for half in halves]
     by_both = [swap(half, "core") for half in by_x]
-    quarters = [*halves, *by_core, *by_x, *by_both]
-    return facet(quarters, left, taper_rows, taper_cols, right)[None]
+    first, second = zip(halves, by_core, by_x, by_both)
+    half_mixture = mixture_half(first, left)
+    return facet(second, half_mixture, left, taper_rows, taper_cols, right)[None]
 
 
 def solution(mesh):

time: 59.9 us -> 60.7 us (1.013)
  Pallas kernels: 14.1 us -> 15.8 us
  waiting for transfers between devices: 2.52 us -> 1.55 us
    pallas_call x0 -> x1, Pallas kernels: none -> 1.73 us  [mixture_half(): pl.pallas_call(mixture_kernel, out_shape=jax.ShapeDtypeStruct((2, ROWS_OU...]
    ppermute x7, waiting for transfers between devices: 2.52 us -> 1.55 us  [swap(): return lax.ppermute(array, axis, [(0, 1), (1, 0)])]
  transfers between devices with their start and end apart: 7 -> 7, of which waited for: 2 -> 1; matrix products, arithmetic and copies ran while one was open for 0% -> 0% of each run, Pallas kernels for 0% -> 3%
where the time goes in v4:
time: 60.7 us; the launch traced here: 60.6 us
  blocking collectives  30.9 us (51%)
  Pallas kernels  15.8 us (26%)
  starting transfers between devices  12.1 us (20%)
  waiting for transfers between devices  1.55 us (3%)
    all_to_all x1, blocking collectives, shards(): lax.all_to_all(outgoing, ('grid', 'x_lo'), split_axis=0, concat_axis=0, t...  30.9 us
    ppermute x7, starting transfers between devices, swap(): return lax.ppermute(array, axis, [(0, 1), (1, 0)])  12.1 us
    pallas_call x1, Pallas kernels, gridding(): pl.pallas_call(gridding_kernel, out_shape=[half] * 2 + [jax.ShapeDtypeStr...  10 us
    pallas_call x1, Pallas kernels, facet(): pl.pallas_call(facet_kernel, out_shape=jax.ShapeDtypeStruct((2, ROWS_OUT,...  3.95 us
    pallas_call x1, Pallas kernels, mixture_half(): pl.pallas_call(mixture_kernel, out_shape=jax.ShapeDtypeStruct((2, ROWS_OU...  1.73 us
    ppermute x7, waiting for transfers between devices, swap(): return lax.ppermute(array, axis, [(0, 1), (1, 0)])  1.55 us
  transfers between devices with their start and end apart: 7, of which 1 were waited for; matrix products, arithmetic and copies ran while one was open for 0% of the time, Pallas kernels for 3%

profile of v4, /device:TPU:1, one launch (start us, length us, event | category | flops | bytes accessed | tf_op | source)
XLA Modules:
  0.0 60.6 jit_solution(17009027671476008157)
XLA Ops:
  0.0 10.0 %gridding.1 = (bf16[8,256,128]{2,1,0:T(8,128)(2,1)S(1)}, bf16[8,256,128]{2,1,0:T(8,128)(2,1)S(1)}, bf16[512,512]{1,0:T(8,128)(2,1)S(1)}, f32[256,128]{1,0:T(8,128)S(1)}, f32[1,1024]{1,0:T(1,128)S(1)}) custom-call(s32[1]{0:T(128)} %bitcast.place_ref, s32[1,64]{1,0:T(1,128)} %tiles_hbm.1, f32[512,128]{1,0:T(8,128)} %bitcast.24, f32[512,128]{1,0:T(8,128)} %bitcast.25, ...), custom_call_target="tpu_custom_call" | custom-call | tf_op jit(solution)/shard_map/gridding/pallas_call | solution.py:242
  10.0 3.3 %collective-permute-start = (bf16[8,256,128]{2,1,0:T(8,128)(2,1)S(1)}, bf16[8,256,128]{2,1,0:T(8,128)(2,1)S(1)}, u32[]{:S(2)}, u32[]{:S(2)}) collective-permute-start(bf16[8,256,128]{2,1,0:T(8,128)(2,1)S(1)} %get-tuple-element.13), channel_id=1, source_target_pairs={{0,1},{1,0},{2,3},{3,2},{4,5},{5,4},{6,7},{7,6},{8,9},{9,8},{10,11... | collective-permute-start | bytes 1572872 | tf_op jit(solution)/shard_map/ppermute | solution.py:411
  13.4 1.5 %collective-permute-done = bf16[8,256,128]{2,1,0:T(8,128)(2,1)S(1)} collective-permute-done((bf16[8,256,128]{2,1,0:T(8,128)(2,1)S(1)}, bf16[8,256,128]{2,1,0:T(8,128)(2,1)S(1)}, u32[]{:S(2)}, u32[]{:S(2)}) %collective-permute-start) | collective-permute-done | bytes 524320 | tf_op jit(solution)/shard_map/ppermute | solution.py:411
  14.9 0.1 add_convert_fusion
  15.0 30.9 %all_to_all.5 = bf16[128,16,128]{2,1,0:T(8,128)(2,1)S(1)} all-to-all(bf16[128,16,128]{2,1,0:T(8,128)(2,1)S(1)} %bitcast.23), channel_id=1, replica_groups=mesh['grid'=64,'x_lo'=2,'core'=2] {'grid','x_lo'}, dimensions={0} | all-to-all | bytes 1048576 | tf_op jit(solution)/shard_map/all_to_all | solution.py:422
  45.9 0.1 pair_sum.1
  46.0 0.1 collective-permute-start.5
  46.1 1.5 %collective-permute-start.2 = (bf16[4,128,128]{2,1,0:T(8,128)(2,1)S(1)}, bf16[4,128,128]{2,1,0:T(8,128)(2,1)S(1)}, u32[]{:S(2)}, u32[]{:S(2)}) collective-permute-start(bf16[4,128,128]{2,1,0:T(8,128)(2,1)S(1)} %bitcast.17), channel_id=1, source_target_pairs={{0,2},{2,0},{1,3},{3,1},{4,6},{6,4},{5,7},{7,5},{8,10},{10,8},{9,1... | collective-permute-start | bytes 393224 | tf_op jit(solution)/shard_map/ppermute | solution.py:411
  47.6 2.9 %collective-permute-start.4 = (bf16[4,128,128]{2,1,0:T(8,128)(2,1)S(1)}, bf16[4,128,128]{2,1,0:T(8,128)(2,1)S(1)}, u32[]{:S(2)}, u32[]{:S(2)}) collective-permute-start(bf16[4,128,128]{2,1,0:T(8,128)(2,1)S(1)} %bitcast.21), channel_id=1, source_target_pairs={{0,1},{1,0},{2,3},{3,2},{4,5},{5,4},{6,7},{7,6},{8,9},{9,8},{10,11... | collective-permute-start | bytes 393224 | tf_op jit(solution)/shard_map/ppermute | solution.py:411
  50.5 0.0 collective-permute-done.5.by_x
  50.5 2.9 %collective-permute-start.6 = (bf16[4,128,128]{2,1,0:T(8,128)(2,1)S(1)}, bf16[4,128,128]{2,1,0:T(8,128)(2,1)S(1)}, u32[]{:S(2)}, u32[]{:S(2)}) collective-permute-start(bf16[4,128,128]{2,1,0:T(8,128)(2,1)S(1)} %collective-permute-done.5.by_x), channel_id=1, source_target_pairs={{0,1},{1,0},{2,3},{3,2},{4,5},{5,4},{6,7},{7,6},{8,9},{9,8},{10,11... | collective-permute-start | bytes 393224 | tf_op jit(solution)/shard_map/ppermute | solution.py:411
  53.4 0.0 collective-permute-start.1
  53.4 0.0 collective-permute-done.2.by_x
  53.4 1.4 %collective-permute-start.3 = (bf16[4,128,128]{2,1,0:T(8,128)(2,1)S(1)}, bf16[4,128,128]{2,1,0:T(8,128)(2,1)S(1)}, u32[]{:S(2)}, u32[]{:S(2)}) collective-permute-start(bf16[4,128,128]{2,1,0:T(8,128)(2,1)S(1)} %collective-permute-done.2.by_x), channel_id=1, source_target_pairs={{0,1},{1,0},{2,3},{3,2},{4,5},{5,4},{6,7},{7,6},{8,9},{9,8},{10,11... | collective-permute-start | bytes 393224 | tf_op jit(solution)/shard_map/ppermute | solution.py:411
  54.8 0.0 collective-permute-done.4.by_core
  54.8 0.0 collective-permute-done.6.by_both
  54.8 1.7 %mixture_half.1.half_mixture = bf16[2,256,256]{2,1,0:T(8,128)(2,1)S(1)} custom-call(bf16[4,128,128]{2,1,0:T(8,128)(2,1)S(1)} %bitcast.22, bf16[4,128,128]{2,1,0:T(8,128)(2,1)S(1)} %collective-permute-done.4.by_core, bf16[4,128,128]{2,1,0:T(8,128)(2,1)S(1)} %collective-permute-done.5.by_x, bf16[4,128,128]{2,1,0:T(8,128)(2,1)S(1)} %collective-permute-done.6.by_both, ...), custom_call_target="tpu_custom_call" | custom-call | flops 268435456 | bytes 1048576 | tf_op jit(solution)/shard_map/mixture_half/pallas_call | solution.py:327
  56.6 0.0 collective-permute-done.1.by_core
  56.6 0.0 collective-permute-done.3.by_both
  56.6 3.9 %facet.1 = f32[2,256,1024]{2,1,0:T(8,128)} custom-call(bf16[4,128,128]{2,1,0:T(8,128)(2,1)S(1)} %bitcast.19, bf16[4,128,128]{2,1,0:T(8,128)(2,1)S(1)} %collective-permute-done.1.by_core, bf16[4,128,128]{2,1,0:T(8,128)(2,1)S(1)} %collective-permute-done.2.by_x, bf16[4,128,128]{2,1,0:T(8,128)(2,1)S(1)} %collective-permute-done.3.by_both, ...), custom_call_target="tpu_custom_call" | custom-call | tf_op jit(solution)/shard_map/facet/pallas_call | solution.py:385
Async XLA Ops:
  10.0 4.9 %collective-permute-start = (bf16[8,256,128]{2,1,0:T(8,128)(2,1)S(1)}, bf16[8,256,128]{2,1,0:T(8,128)(2,1)S(1)}, u32[]{:S(2)}, u32[]{:S(2)}) collective-permute-start(bf16[8,256,128]{2,1,0:T(8,128)(2,1)S(1)} %get-tuple-element.13), channel_id=1, source_target_pairs={{0,1},{1,0},{2,3},{3,2},{4,5},{5,4},{6,7},{7,6},{8,9},{9,8},{10,11... | collective-permute-start | bytes 1572872 | tf_op jit(solution)/shard_map/ppermute | solution.py:411
  46.0 4.5 %collective-permute-start.5 = (bf16[4,128,128]{2,1,0:T(8,128)(2,1)S(1)}, bf16[4,128,128]{2,1,0:T(8,128)(2,1)S(1)}, u32[]{:S(2)}, u32[]{:S(2)}) collective-permute-start(bf16[4,128,128]{2,1,0:T(8,128)(2,1)S(1)} %bitcast.20), channel_id=1, source_target_pairs={{0,2},{2,0},{1,3},{3,1},{4,6},{6,4},{5,7},{7,5},{8,10},{10,8},{9,1... | collective-permute-start | bytes 393224 | tf_op jit(solution)/shard_map/ppermute | solution.py:411
  46.1 7.3 %collective-permute-start.2 = (bf16[4,128,128]{2,1,0:T(8,128)(2,1)S(1)}, bf16[4,128,128]{2,1,0:T(8,128)(2,1)S(1)}, u32[]{:S(2)}, u32[]{:S(2)}) collective-permute-start(bf16[4,128,128]{2,1,0:T(8,128)(2,1)S(1)} %bitcast.17), channel_id=1, source_target_pairs={{0,2},{2,0},{1,3},{3,1},{4,6},{6,4},{5,7},{7,5},{8,10},{10,8},{9,1... | collective-permute-start | bytes 393224 | tf_op jit(solution)/shard_map/ppermute | solution.py:411
  47.6 7.3 %collective-permute-start.4 = (bf16[4,128,128]{2,1,0:T(8,128)(2,1)S(1)}, bf16[4,128,128]{2,1,0:T(8,128)(2,1)S(1)}, u32[]{:S(2)}, u32[]{:S(2)}) collective-permute-start(bf16[4,128,128]{2,1,0:T(8,128)(2,1)S(1)} %bitcast.21), channel_id=1, source_target_pairs={{0,1},{1,0},{2,3},{3,2},{4,5},{5,4},{6,7},{7,6},{8,9},{9,8},{10,11... | collective-permute-start | bytes 393224 | tf_op jit(solution)/shard_map/ppermute | solution.py:411
  50.5 4.3 %collective-permute-start.6 = (bf16[4,128,128]{2,1,0:T(8,128)(2,1)S(1)}, bf16[4,128,128]{2,1,0:T(8,128)(2,1)S(1)}, u32[]{:S(2)}, u32[]{:S(2)}) collective-permute-start(bf16[4,128,128]{2,1,0:T(8,128)(2,1)S(1)} %collective-permute-done.5.by_x), channel_id=1, source_target_pairs={{0,1},{1,0},{2,3},{3,2},{4,5},{5,4},{6,7},{7,6},{8,9},{9,8},{10,11... | collective-permute-start | bytes 393224 | tf_op jit(solution)/shard_map/ppermute | solution.py:411
  53.4 3.1 %collective-permute-start.1 = (bf16[4,128,128]{2,1,0:T(8,128)(2,1)S(1)}, bf16[4,128,128]{2,1,0:T(8,128)(2,1)S(1)}, u32[]{:S(2)}, u32[]{:S(2)}) collective-permute-start(bf16[4,128,128]{2,1,0:T(8,128)(2,1)S(1)} %bitcast.18), channel_id=1, source_target_pairs={{0,1},{1,0},{2,3},{3,2},{4,5},{5,4},{6,7},{7,6},{8,9},{9,8},{10,11... | collective-permute-start | bytes 393224 | tf_op jit(solution)/shard_map/ppermute | solution.py:411
  53.4 3.2 %collective-permute-start.3 = (bf16[4,128,128]{2,1,0:T(8,128)(2,1)S(1)}, bf16[4,128,128]{2,1,0:T(8,128)(2,1)S(1)}, u32[]{:S(2)}, u32[]{:S(2)}) collective-permute-start(bf16[4,128,128]{2,1,0:T(8,128)(2,1)S(1)} %collective-permute-done.2.by_x), channel_id=1, source_target_pairs={{0,1},{1,0},{2,3},{3,2},{4,5},{5,4},{6,7},{7,6},{8,9},{9,8},{10,11... | collective-permute-start | bytes 393224 | tf_op jit(solution)/shard_map/ppermute | solution.py:411

commit v5 on v4

--- a/solution.py
+++ b/solution.py
@@ -68,6 +68,14 @@
     right[:, :, :, 0, :, :, 1] = sin
     right[:, :, :, 1, :, :, 1] = cos
     right = as_bf16(right.reshape(2, CHUNKS, SUB, 2 * LANES))
+    fold = np.zeros((2, 2, 2, 2, CONTRIB // 2, 2, 2, 2, CONTRIB // 2))
+    j = np.arange(CONTRIB // 2)
+    for sb in range(2):
+        for r in range(2):
+            for part in range(2):
+                fold[0, sb, part, r, j, r, part, sb, j] = 1.0
+                fold[1, sb, part, r, j, r, 1 - part, sb, j] = 1.0 - 2.0 * part
+    fold = as_bf16(fold.reshape(SUB, 2 * LANES))
     sines = np.sin(math.pi * (np.arange(FAC) + 0.5) / FAC)
     taper = 0.25 + 0.75 * sines * sines
     taper_rows = np.broadcast_to(taper.reshape(4, ROWS_OUT, 1), (4, ROWS_OUT, LANES)).astype(np.float32)
@@ -77,22 +85,23 @@
     across = bell.reshape(TILE // 2, 2).T
     across = np.stack([across, across[::-1]])[:, :, None, :].repeat(2, 2).reshape(2, 1, LANES)
     bell = (bell[:, None] * across / SUB).astype(np.float32)
-    return columns, rows, left, right, np.ascontiguousarray(taper_rows), taper_cols, bell
+    return columns, rows, left, right, fold, np.ascontiguousarray(taper_rows), taper_cols, bell
 
 
 SINE = [math.pi ** (2 * k + 1) * (-1) ** k / math.factorial(2 * k + 1) for k in range(7)]
 
 
 def gridding_kernel(
-    place_ref, tiles_hbm, coords_hbm, values_hbm, columns_hbm, rows_hbm, bell_hbm, left_hbm, taper_rows_hbm, taper_cols_hbm,
-    keep_ref, send_ref, left_ref, taper_rows_ref, taper_cols_ref,
+    place_ref, tiles_hbm, coords_hbm, values_hbm, columns_hbm, rows_hbm, bell_hbm, left_hbm, taper_rows_hbm, taper_cols_hbm, right_hbm, fold_hbm,
+    keep_ref, send_ref, left_ref, taper_rows_ref, taper_cols_ref, right_ref, fold_ref,
     tile_ref, coords, values, step8, slope, height, acc, grid16, halves, stacked, columns, rows, bell_ref,
     sems,
 ):
     place = place_ref[0]
     first = [(coords_hbm, coords), (values_hbm, values), (tiles_hbm, tile_ref)]
     later = [(columns_hbm, columns), (rows_hbm, rows), (bell_hbm, bell_ref)]
-    last = [(left_hbm.at[place], left_ref), (taper_rows_hbm.at[place], taper_rows_ref), (taper_cols_hbm, taper_cols_ref)]
+    last = [(left_hbm.at[place], left_ref), (taper_rows_hbm.at[place], taper_rows_ref)]
+    last += [(taper_cols_hbm, taper_cols_ref), (right_hbm, right_ref), (fold_hbm, fold_ref)]
     copies = [pltpu.make_async_copy(*ends, sems.at[i]) for i, ends in enumerate(first + later + last)]
     for copy in copies:
         copy.start()
@@ -246,9 +255,11 @@
             jax.ShapeDtypeStruct((2 * ROWS_OUT, SUB), BF16),
             jax.ShapeDtypeStruct((ROWS_OUT, LANES), F32),
             jax.ShapeDtypeStruct((1, FAC), F32),
+            jax.ShapeDtypeStruct((2, CHUNKS, SUB, 2 * LANES), BF16),
+            jax.ShapeDtypeStruct((SUB, 2 * LANES), BF16),
         ],
         in_specs=[pl.BlockSpec(memory_space=pltpu.SMEM)] + [hbm] * len(arrays),
-        out_specs=[vector] * 5,
+        out_specs=[vector] * 7,
         scratch_shapes=[
             pltpu.SMEM((1, BLOCKS), jnp.int32),
             plane, plane, plane, plane, plane,
@@ -259,7 +270,7 @@
             pltpu.VMEM((2, SUB, SUB), BF16),
             pltpu.VMEM((4, ROWS, SUB // 2), BF16),
             pltpu.VMEM((2, TILE, LANES), F32),
-            pltpu.SemaphoreType.DMA((9,)),
+            pltpu.SemaphoreType.DMA((11,)),
         ],
         compiler_params=pltpu.CompilerParams(vmem_limit_bytes=24 * 1024 * 1024),
         name="gridding",
@@ -293,56 +304,45 @@
     )(arrived)
 
 
-def mix(parts, left, products, mixture):
-    lane = lax.broadcasted_iota(jnp.int32, (1, LANES), 1)
-    sign = jnp.where(lane < CONTRIB, -1.0, 1.0)
-    even = lane % CONTRIB < CONTRIB // 2
+def mix(parts, left, fold, products, mixture):
     for n in range(NBLK // 4):
         right_side = jnp.concatenate(
             [jnp.concatenate([part[2 * n], part[2 * n + 1]], 1) for part in parts], 0
         )
-        products[n] = jnp.dot(left[...], right_side, preferred_element_type=F32)
-
+        both = jnp.dot(left[...], right_side, preferred_element_type=F32).astype(BF16)
+        at = slice(n * ROWS_OUT, (n + 1) * ROWS_OUT)
+        products[at, : 2 * LANES] = both[:ROWS_OUT]
+        products[at, 2 * LANES :] = both[ROWS_OUT:]
+    mixed = jnp.dot(products[...], fold[...], preferred_element_type=F32).astype(BF16)
     for n in range(NBLK // 4):
-        into = slice(n * LANES, (n + 1) * LANES)
-
-        @pl.loop(0, ROWS_OUT // 64)
-        def _(m):
-            at = pl.ds(pl.multiple_of(m * 64, 64), 64)
-            below = pl.ds(pl.multiple_of(ROWS_OUT + m * 64, 64), 64)
-            first, second = (
-                products[n, at, lanes] + pltpu.roll(products[n, below, lanes], CONTRIB, 1) * sign
-                for lanes in (slice(0, LANES), slice(LANES, 2 * LANES))
-            )
-            mixture[0, at, into] = jnp.where(even, first, pltpu.roll(second, CONTRIB // 2, 1)).astype(BF16)
-            mixture[1, at, into] = jnp.where(even, pltpu.roll(first, LANES - CONTRIB // 2, 1), second).astype(BF16)
-
-
-def mixture_kernel(own, by_core, by_x, by_both, left, mixture, products):
-    mix((own, by_core, by_x, by_both), left, products, mixture)
-
-
-def mixture_half(quarters, left):
+        at = slice(n * ROWS_OUT, (n + 1) * ROWS_OUT)
+        for r in range(2):
+            mixture[r, :, n * LANES : (n + 1) * LANES] = mixed[at, r * LANES : (r + 1) * LANES]
+
+
+def mixture_kernel(own, by_core, by_x, by_both, left, fold, mixture, products):
+    mix((own, by_core, by_x, by_both), left, fold, products, mixture)
+
+
+def mixture_half(quarters, left, fold):
     vector = pl.BlockSpec(memory_space=pltpu.VMEM)
     return pl.pallas_call(
         mixture_kernel,
         out_shape=jax.ShapeDtypeStruct((2, ROWS_OUT, SUB // 2), BF16),
-        in_specs=[vector] * 5,
+        in_specs=[vector] * 6,
         out_specs=vector,
-        scratch_shapes=[pltpu.VMEM((NBLK // 4, 2 * ROWS_OUT, 2 * LANES), F32)],
+        scratch_shapes=[pltpu.VMEM((NBLK // 4 * ROWS_OUT, 4 * LANES), BF16)],
         compiler_params=pltpu.CompilerParams(vmem_limit_bytes=24 * 1024 * 1024),
         cost_estimate=pl.CostEstimate(flops=2**28, bytes_accessed=2**20, transcendentals=0),
         name="mixture_half",
-    )(*quarters, left)
+    )(*quarters, left, fold)
 
 
 def facet_kernel(
-    own, by_core, by_x, by_both, half_mixture, left, taper_rows, taper_cols, right_hbm, out_hbm,
-    right, mixture, products, image, sems,
+    own, by_core, by_x, by_both, half_mixture, left, fold, taper_rows, taper_cols, right, out_hbm,
+    mixture, products, image, sems,
 ):
-    for chunk in range(CHUNKS):
-        pltpu.make_async_copy(right_hbm.at[:, chunk], right.at[:, chunk], sems.at[chunk]).start()
-    mix((own, by_core, by_x, by_both), left, products, mixture)
+    mix((own, by_core, by_x, by_both), left, fold, products, mixture)
 
     def departures(chunk):
         copies = []
@@ -350,13 +350,12 @@
             for half in range(2):
                 first = pl.multiple_of(half * (FAC // 2) + chunk * LANES, LANES)
                 into = out_hbm.at[part, :, pl.ds(first, LANES)]
-                sem = sems.at[CHUNKS + chunk * 4 + part * 2 + half]
+                sem = sems.at[chunk * 4 + part * 2 + half]
                 copies.append(pltpu.make_async_copy(image.at[chunk, part, half], into, sem))
         return copies
 
     @pl.loop(0, CHUNKS)
     def _(chunk):
-        pltpu.make_async_copy(right_hbm.at[:, chunk], right.at[:, chunk], sems.at[chunk]).wait()
         evens, odds = (
             jnp.dot(
                 jnp.concatenate([half_mixture[r], mixture[r]], 1), right[r, chunk], preferred_element_type=F32
@@ -379,24 +378,23 @@
             copy.wait()
 
 
-def facet(quarters, half_mixture, left, taper_rows, taper_cols, right):
+def facet(quarters, half_mixture, left, fold, taper_rows, taper_cols, right):
     vector = pl.BlockSpec(memory_space=pltpu.VMEM)
     hbm = pl.BlockSpec(memory_space=pltpu.HBM)
     return pl.pallas_call(
         facet_kernel,
         out_shape=jax.ShapeDtypeStruct((2, ROWS_OUT, FAC), F32),
-        in_specs=[vector] * 8 + [hbm],
+        in_specs=[vector] * 10,
         out_specs=hbm,
         scratch_shapes=[
-            pltpu.VMEM((2, CHUNKS, SUB, 2 * LANES), BF16),
             pltpu.VMEM((2, ROWS_OUT, SUB // 2), BF16),
-            pltpu.VMEM((NBLK // 4, 2 * ROWS_OUT, 2 * LANES), F32),
+            pltpu.VMEM((NBLK // 4 * ROWS_OUT, 4 * LANES), BF16),
             pltpu.VMEM((CHUNKS, 2, 2, ROWS_OUT, LANES), F32),
-            pltpu.SemaphoreType.DMA((5 * CHUNKS,)),
+            pltpu.SemaphoreType.DMA((4 * CHUNKS,)),
         ],
         compiler_params=pltpu.CompilerParams(vmem_limit_bytes=24 * 1024 * 1024),
         name="facet",
-    )(*quarters, half_mixture, left, taper_rows, taper_cols, stay(right))
+    )(*quarters, half_mixture, left, fold, taper_rows, taper_cols, right)
 
 
 def by_visibility_row(array):
@@ -404,17 +402,17 @@
 
 
 def shards(vis_coords, vis_values, tile_index):
-    columns, rows, left, right, taper_rows, taper_cols, bell = (jnp.asarray(table) for table in tables())
+    columns, rows, left, right, fold, taper_rows, taper_cols, bell = (jnp.asarray(table) for table in tables())
     place = (lax.axis_index("x_lo") * 2 + lax.axis_index("core")).astype(jnp.int32).reshape(1)
 
     def swap(array, axis):
         return lax.ppermute(array, axis, [(0, 1), (1, 0)])
 
-    keep, send, left, taper_rows, taper_cols = gridding(
+    keep, send, left, taper_rows, taper_cols, right, fold = gridding(
         place,
         [
             tile_index, by_visibility_row(vis_coords), by_visibility_row(vis_values),
-            columns, rows, bell, left, taper_rows, taper_cols,
+            columns, rows, bell, left, taper_rows, taper_cols, right, fold,
         ],
     )
     total = (keep.astype(F32) + swap(send, "core").astype(F32)).astype(BF16)
@@ -425,8 +423,8 @@
     by_x = [swap(half, "x_lo") for half in halves]
     by_both = [swap(half, "core") for half in by_x]
     first, second = zip(halves, by_core, by_x, by_both)
-    half_mixture = mixture_half(first, left)
-    return facet(second, half_mixture, left, taper_rows, taper_cols, right)[None]
+    half_mixture = mixture_half(first, left, fold)
+    return facet(second, half_mixture, left, fold, taper_rows, taper_cols, right)[None]
 
 
 def solution(mesh):

time: 60.7 us -> 58.9 us (0.970)
  Pallas kernels: 15.8 us -> 13.8 us
    pallas_call x1, Pallas kernels: 3.95 us -> 2.93 us  [facet(): pl.pallas_call(facet_kernel, out_shape=jax.ShapeDtypeStruct((2, ROWS_OUT,...]
    pallas_call x1, Pallas kernels: 1.73 us -> 0.76 us  [mixture_half(): pl.pallas_call(mixture_kernel, out_shape=jax.ShapeDtypeStruct((2, ROWS_OU...]
  transfers between devices with their start and end apart: 7 -> 7, of which waited for: 1 -> 2; matrix products, arithmetic and copies ran while one was open for 0% -> 0% of each run, Pallas kernels for 3% -> 1%
where the time goes in v5:
time: 58.9 us; the launch traced here: 58.8 us
  blocking collectives  30.9 us (52%)
  Pallas kernels  13.8 us (23%)
  starting transfers between devices  12.1 us (21%)
  waiting for transfers between devices  1.75 us (3%)
    all_to_all x1, blocking collectives, shards(): lax.all_to_all(outgoing, ('grid', 'x_lo'), split_axis=0, concat_axis=0, t...  30.9 us
    ppermute x7, starting transfers between devices, swap(): return lax.ppermute(array, axis, [(0, 1), (1, 0)])  12.1 us
    pallas_call x1, Pallas kernels, gridding(): pl.pallas_call(gridding_kernel, out_shape=[half] * 2 + [jax.ShapeDtypeStr...  10 us
    pallas_call x1, Pallas kernels, facet(): pl.pallas_call(facet_kernel, out_shape=jax.ShapeDtypeStruct((2, ROWS_OUT,...  2.93 us
    ppermute x7, waiting for transfers between devices, swap(): return lax.ppermute(array, axis, [(0, 1), (1, 0)])  1.75 us
  transfers between devices with their start and end apart: 7, of which 2 were waited for; matrix products, arithmetic and copies ran while one was open for 0% of the time, Pallas kernels for 1%

profile of v5, /device:TPU:1, one launch (start us, length us, event | category | flops | bytes accessed | tf_op | source)
XLA Modules:
  0.0 58.8 jit_solution(7819579519597523709)
XLA Ops:
  0.0 10.0 %gridding.1 = (bf16[8,256,128]{2,1,0:T(8,128)(2,1)S(1)}, bf16[8,256,128]{2,1,0:T(8,128)(2,1)S(1)}, bf16[512,512]{1,0:T(8,128)(2,1)S(1)}, f32[256,128]{1,0:T(8,12...) custom-call(s32[1]{0:T(128)} %bitcast.place_ref, ...), custom_call_target="tpu_custom_call" | custom-call | tf_op jit(solution)/shard_map/gridding/pallas_call | solution.py:251
  10.0 3.3 %collective-permute-start = (bf16[8,256,128]{2,1,0:T(8,128)(2,1)S(1)}, bf16[8,256,128]{2,1,0:T(8,128)(2,1)S(1)}, u32[]{:S(2)}, u32[]{:S(2)}) collective-permute-start(bf16[8,256,128]{2,1,0:T(8,128)(2,1)S(1)} %get-tuple-element.15), channel_id=1, source_target_pairs={{0,1},{1,0},{2,3},{3,2},{4,5},{5,4},{6,7},{7,6},{8,9},{9,8},{10,11... | collective-permute-start | bytes 1572872 | tf_op jit(solution)/shard_map/ppermute | solution.py:409
  13.4 1.5 %collective-permute-done = bf16[8,256,128]{2,1,0:T(8,128)(2,1)S(1)} collective-permute-done((bf16[8,256,128]{2,1,0:T(8,128)(2,1)S(1)}, bf16[8,256,128]{2,1,0:T(8,128)(2,1)S(1)}, u32[]{:S(2)}, u32[]{:S(2)}) %collective-permute-start) | collective-permute-done | bytes 524320 | tf_op jit(solution)/shard_map/ppermute | solution.py:409
  14.9 0.1 add_convert_fusion
  15.1 30.9 %all_to_all.5 = bf16[128,16,128]{2,1,0:T(8,128)(2,1)S(1)} all-to-all(bf16[128,16,128]{2,1,0:T(8,128)(2,1)S(1)} %bitcast.23), channel_id=1, replica_groups=mesh['grid'=64,'x_lo'=2,'core'=2] {'grid','x_lo'}, dimensions={0} | all-to-all | bytes 1048576 | tf_op jit(solution)/shard_map/all_to_all | solution.py:420
  46.0 0.1 pair_sum.1
  46.1 0.1 collective-permute-start.5
  46.2 1.5 %collective-permute-start.2 = (bf16[4,128,128]{2,1,0:T(8,128)(2,1)S(1)}, bf16[4,128,128]{2,1,0:T(8,128)(2,1)S(1)}, u32[]{:S(2)}, u32[]{:S(2)}) collective-permute-start(bf16[4,128,128]{2,1,0:T(8,128)(2,1)S(1)} %bitcast.17), channel_id=1, source_target_pairs={{0,2},{2,0},{1,3},{3,1},{4,6},{6,4},{5,7},{7,5},{8,10},{10,8},{9,1... | collective-permute-start | bytes 393224 | tf_op jit(solution)/shard_map/ppermute | solution.py:409
  47.6 2.9 %collective-permute-start.4 = (bf16[4,128,128]{2,1,0:T(8,128)(2,1)S(1)}, bf16[4,128,128]{2,1,0:T(8,128)(2,1)S(1)}, u32[]{:S(2)}, u32[]{:S(2)}) collective-permute-start(bf16[4,128,128]{2,1,0:T(8,128)(2,1)S(1)} %bitcast.21), channel_id=1, source_target_pairs={{0,1},{1,0},{2,3},{3,2},{4,5},{5,4},{6,7},{7,6},{8,9},{9,8},{10,11... | collective-permute-start | bytes 393224 | tf_op jit(solution)/shard_map/ppermute | solution.py:409
  50.5 0.0 collective-permute-done.5.by_x
  50.5 2.9 %collective-permute-start.6 = (bf16[4,128,128]{2,1,0:T(8,128)(2,1)S(1)}, bf16[4,128,128]{2,1,0:T(8,128)(2,1)S(1)}, u32[]{:S(2)}, u32[]{:S(2)}) collective-permute-start(bf16[4,128,128]{2,1,0:T(8,128)(2,1)S(1)} %collective-permute-done.5.by_x), channel_id=1, source_target_pairs={{0,1},{1,0},{2,3},{3,2},{4,5},{5,4},{6,7},{7,6},{8,9},{9,8},{10,11... | collective-permute-start | bytes 393224 | tf_op jit(solution)/shard_map/ppermute | solution.py:409
  53.5 0.0 collective-permute-start.1
  53.5 0.0 collective-permute-done.2.by_x
  53.5 1.4 %collective-permute-start.3 = (bf16[4,128,128]{2,1,0:T(8,128)(2,1)S(1)}, bf16[4,128,128]{2,1,0:T(8,128)(2,1)S(1)}, u32[]{:S(2)}, u32[]{:S(2)}) collective-permute-start(bf16[4,128,128]{2,1,0:T(8,128)(2,1)S(1)} %collective-permute-done.2.by_x), channel_id=1, source_target_pairs={{0,1},{1,0},{2,3},{3,2},{4,5},{5,4},{6,7},{7,6},{8,9},{9,8},{10,11... | collective-permute-start | bytes 393224 | tf_op jit(solution)/shard_map/ppermute | solution.py:409
  54.9 0.0 collective-permute-done.4.by_core
  54.9 0.0 collective-permute-done.6.by_both
  54.9 0.8 %mixture_half.1.half_mixture = bf16[2,256,256]{2,1,0:T(8,128)(2,1)S(1)} custom-call(bf16[4,128,128]{2,1,0:T(8,128)(2,1)S(1)} %bitcast.22, bf16[4,128,128]{2,1,0:T(8,128)(2,1)S(1)} %collective-permute-done.4.by_core, bf16[4,128,128]{2,1,0:T(8,128)(2,1)S(1)} %collective-permute-done.5.by_x, bf16[4,128,128]{2,1,0:T(8,128)(2,1)S(1)} %collective-permute-done.6.by_both, ...), custom_call_target="tpu_custom_call" | custom-call | flops 268435456 | bytes 1048576 | tf_op jit(solution)/shard_map/mixture_half/pallas_call | solution.py:329
  55.6 0.0 collective-permute-done.1.by_core
  55.6 0.2 collective-permute-done.3.by_both
  55.9 2.9 %facet.1 = f32[2,256,1024]{2,1,0:T(8,128)} custom-call(bf16[4,128,128]{2,1,0:T(8,128)(2,1)S(1)} %bitcast.19, bf16[4,128,128]{2,1,0:T(8,128)(2,1)S(1)} %collective-permute-done.1.by_core, bf16[4,128,128]{2,1,0:T(8,128)(2,1)S(1)} %collective-permute-done.2.by_x, bf16[4,128,128]{2,1,0:T(8,128)(2,1)S(1)} %collective-permute-done.3.by_both, ...), custom_call_target="tpu_custom_call" | custom-call | tf_op jit(solution)/shard_map/facet/pallas_call | solution.py:384
Async XLA Ops:
  10.0 4.9 %collective-permute-start = (bf16[8,256,128]{2,1,0:T(8,128)(2,1)S(1)}, bf16[8,256,128]{2,1,0:T(8,128)(2,1)S(1)}, u32[]{:S(2)}, u32[]{:S(2)}) collective-permute-start(bf16[8,256,128]{2,1,0:T(8,128)(2,1)S(1)} %get-tuple-element.15), channel_id=1, source_target_pairs={{0,1},{1,0},{2,3},{3,2},{4,5},{5,4},{6,7},{7,6},{8,9},{9,8},{10,11... | collective-permute-start | bytes 1572872 | tf_op jit(solution)/shard_map/ppermute | solution.py:409
  46.1 4.5 %collective-permute-start.5 = (bf16[4,128,128]{2,1,0:T(8,128)(2,1)S(1)}, bf16[4,128,128]{2,1,0:T(8,128)(2,1)S(1)}, u32[]{:S(2)}, u32[]{:S(2)}) collective-permute-start(bf16[4,128,128]{2,1,0:T(8,128)(2,1)S(1)} %bitcast.20), channel_id=1, source_target_pairs={{0,2},{2,0},{1,3},{3,1},{4,6},{6,4},{5,7},{7,5},{8,10},{10,8},{9,1... | collective-permute-start | bytes 393224 | tf_op jit(solution)/shard_map/ppermute | solution.py:409
  46.2 7.3 %collective-permute-start.2 = (bf16[4,128,128]{2,1,0:T(8,128)(2,1)S(1)}, bf16[4,128,128]{2,1,0:T(8,128)(2,1)S(1)}, u32[]{:S(2)}, u32[]{:S(2)}) collective-permute-start(bf16[4,128,128]{2,1,0:T(8,128)(2,1)S(1)} %bitcast.17), channel_id=1, source_target_pairs={{0,2},{2,0},{1,3},{3,1},{4,6},{6,4},{5,7},{7,5},{8,10},{10,8},{9,1... | collective-permute-start | bytes 393224 | tf_op jit(solution)/shard_map/ppermute | solution.py:409
  47.6 7.3 %collective-permute-start.4 = (bf16[4,128,128]{2,1,0:T(8,128)(2,1)S(1)}, bf16[4,128,128]{2,1,0:T(8,128)(2,1)S(1)}, u32[]{:S(2)}, u32[]{:S(2)}) collective-permute-start(bf16[4,128,128]{2,1,0:T(8,128)(2,1)S(1)} %bitcast.21), channel_id=1, source_target_pairs={{0,1},{1,0},{2,3},{3,2},{4,5},{5,4},{6,7},{7,6},{8,9},{9,8},{10,11... | collective-permute-start | bytes 393224 | tf_op jit(solution)/shard_map/ppermute | solution.py:409
  50.5 4.3 %collective-permute-start.6 = (bf16[4,128,128]{2,1,0:T(8,128)(2,1)S(1)}, bf16[4,128,128]{2,1,0:T(8,128)(2,1)S(1)}, u32[]{:S(2)}, u32[]{:S(2)}) collective-permute-start(bf16[4,128,128]{2,1,0:T(8,128)(2,1)S(1)} %collective-permute-done.5.by_x), channel_id=1, source_target_pairs={{0,1},{1,0},{2,3},{3,2},{4,5},{5,4},{6,7},{7,6},{8,9},{9,8},{10,11... | collective-permute-start | bytes 393224 | tf_op jit(solution)/shard_map/ppermute | solution.py:409
  53.5 2.2 %collective-permute-start.1 = (bf16[4,128,128]{2,1,0:T(8,128)(2,1)S(1)}, bf16[4,128,128]{2,1,0:T(8,128)(2,1)S(1)}, u32[]{:S(2)}, u32[]{:S(2)}) collective-permute-start(bf16[4,128,128]{2,1,0:T(8,128)(2,1)S(1)} %bitcast.18), channel_id=1, source_target_pairs={{0,1},{1,0},{2,3},{3,2},{4,5},{5,4},{6,7},{7,6},{8,9},{9,8},{10,11... | collective-permute-start | bytes 393224 | tf_op jit(solution)/shard_map/ppermute | solution.py:409
  53.5 2.4 %collective-permute-start.3 = (bf16[4,128,128]{2,1,0:T(8,128)(2,1)S(1)}, bf16[4,128,128]{2,1,0:T(8,128)(2,1)S(1)}, u32[]{:S(2)}, u32[]{:S(2)}) collective-permute-start(bf16[4,128,128]{2,1,0:T(8,128)(2,1)S(1)} %collective-permute-done.2.by_x), channel_id=1, source_target_pairs={{0,1},{1,0},{2,3},{3,2},{4,5},{5,4},{6,7},{7,6},{8,9},{9,8},{10,11... | collective-permute-start | bytes 393224 | tf_op jit(solution)/shard_map/ppermute | solution.py:409

commit v6 on v5

--- a/solution.py
+++ b/solution.py
@@ -16,7 +16,7 @@
 TILE = 64
 BLK = 512
 BLOCKS = 64
-GROUP = 16
+GROUP = 32
 CHUNKS = FAC // 2 // 128
 NBLK = 8
 LANES = 128
@@ -76,6 +76,12 @@
                 fold[0, sb, part, r, j, r, part, sb, j] = 1.0
                 fold[1, sb, part, r, j, r, 1 - part, sb, j] = 1.0 - 2.0 * part
     fold = as_bf16(fold.reshape(SUB, 2 * LANES))
+    spin = np.zeros((2, 2, CONTRIB, 2, 2, CONTRIB))
+    j = np.arange(CONTRIB)
+    for block in range(2):
+        spin[block, 0, j, block, 1, j] = -1.0
+        spin[block, 1, j, block, 0, j] = 1.0
+    spin = as_bf16(spin.reshape(2 * LANES, 2 * LANES))
     sines = np.sin(math.pi * (np.arange(FAC) + 0.5) / FAC)
     taper = 0.25 + 0.75 * sines * sines
     taper_rows = np.broadcast_to(taper.reshape(4, ROWS_OUT, 1), (4, ROWS_OUT, LANES)).astype(np.float32)
@@ -85,21 +91,22 @@
     across = bell.reshape(TILE // 2, 2).T
     across = np.stack([across, across[::-1]])[:, :, None, :].repeat(2, 2).reshape(2, 1, LANES)
     bell = (bell[:, None] * across / SUB).astype(np.float32)
-    return columns, rows, left, right, fold, np.ascontiguousarray(taper_rows), taper_cols, bell
+    return columns, rows, left, right, fold, np.ascontiguousarray(taper_rows), taper_cols, bell, spin
 
 
 SINE = [math.pi ** (2 * k + 1) * (-1) ** k / math.factorial(2 * k + 1) for k in range(7)]
 
 
 def gridding_kernel(
-    place_ref, tiles_hbm, coords_hbm, values_hbm, columns_hbm, rows_hbm, bell_hbm, left_hbm, taper_rows_hbm, taper_cols_hbm, right_hbm, fold_hbm,
+    place_ref, tiles_hbm, coords_hbm, values_hbm, columns_hbm, rows_hbm, bell_hbm, left_hbm, taper_rows_hbm, taper_cols_hbm,
+    right_hbm, fold_hbm, spin_hbm,
     keep_ref, send_ref, left_ref, taper_rows_ref, taper_cols_ref, right_ref, fold_ref,
     tile_ref, coords, values, step8, slope, height, acc, grid16, halves, stacked, columns, rows, bell_ref,
-    sems,
+    spin, apart, sems,
 ):
     place = place_ref[0]
     first = [(coords_hbm, coords), (values_hbm, values), (tiles_hbm, tile_ref)]
-    later = [(columns_hbm, columns), (rows_hbm, rows), (bell_hbm, bell_ref)]
+    later = [(columns_hbm, columns), (rows_hbm, rows), (bell_hbm, bell_ref), (spin_hbm, spin)]
     last = [(left_hbm.at[place], left_ref), (taper_rows_hbm.at[place], taper_rows_ref)]
     last += [(taper_cols_hbm, taper_cols_ref), (right_hbm, right_ref), (fold_hbm, fold_ref)]
     copies = [pltpu.make_async_copy(*ends, sems.at[i]) for i, ends in enumerate(first + later + last)]
@@ -186,8 +193,6 @@
 
     lane = lax.broadcasted_iota(jnp.int32, (1, LANES), 1)
     left_lane = lane < CONTRIB
-    sign = jnp.where(left_lane, 1.0, -1.0)
-    sign16 = jnp.broadcast_to(sign, (QUARTER, LANES)).astype(BF16)
     step = SUB // 4
 
     @pl.loop(0, NBLK)
@@ -221,11 +226,24 @@
                 into = slice(block * LANES, (block + 1) * LANES)
                 sum02, diff02 = image[0] + image[2], image[0] - image[2]
                 sum13, diff13 = image[1] + image[3], image[1] - image[3]
-                turned13 = pltpu.roll(diff13, CONTRIB, 1) * sign
-                for v, x in enumerate((sum02 + sum13, diff02 + turned13, sum02 - sum13, diff02 - turned13)):
-                    x = x.astype(BF16)
-                    stacked[v, pl.ds(first, QUARTER), into] = x
-                    stacked[v, pl.ds(first + step, QUARTER), into] = pltpu.roll(x, CONTRIB, 1) * sign16
+                for i, x in enumerate((sum02 + sum13, sum02 - sum13, diff02, diff13)):
+                    apart[i, pl.ds(first, QUARTER), into] = x.astype(BF16)
+
+    @pl.loop(0, WIDTH // 256)
+    def _(n):
+        at = pl.ds(pl.multiple_of(n * 256, 256), 256)
+        pieces = [apart[i, :, at] for i in range(4)]
+        turned = jnp.dot(jnp.concatenate(pieces, 0), spin[...], preferred_element_type=F32)
+        turned = [turned[i * step : (i + 1) * step] for i in range(4)]
+        stacked[0, :step, at] = pieces[0]
+        stacked[0, step:, at] = turned[0].astype(BF16)
+        stacked[2, :step, at] = pieces[1]
+        stacked[2, step:, at] = turned[1].astype(BF16)
+        diff02, diff13 = pieces[2].astype(F32), pieces[3].astype(F32)
+        stacked[1, :step, at] = (diff02 + turned[3]).astype(BF16)
+        stacked[1, step:, at] = (turned[2] - diff13).astype(BF16)
+        stacked[3, :step, at] = (diff02 - turned[3]).astype(BF16)
+        stacked[3, step:, at] = (turned[2] + diff13).astype(BF16)
 
     core = place % 2
 
@@ -270,7 +288,9 @@
             pltpu.VMEM((2, SUB, SUB), BF16),
             pltpu.VMEM((4, ROWS, SUB // 2), BF16),
             pltpu.VMEM((2, TILE, LANES), F32),
-            pltpu.SemaphoreType.DMA((11,)),
+            pltpu.VMEM((2 * LANES, 2 * LANES), BF16),
+            pltpu.VMEM((4, SUB // 4, WIDTH), BF16),
+            pltpu.SemaphoreType.DMA((12,)),
         ],
         compiler_params=pltpu.CompilerParams(vmem_limit_bytes=24 * 1024 * 1024),
         name="gridding",
@@ -402,7 +422,7 @@
 
 
 def shards(vis_coords, vis_values, tile_index):
-    columns, rows, left, right, fold, taper_rows, taper_cols, bell = (jnp.asarray(table) for table in tables())
+    columns, rows, left, right, fold, taper_rows, taper_cols, bell, spin = (jnp.asarray(table) for table in tables())
     place = (lax.axis_index("x_lo") * 2 + lax.axis_index("core")).astype(jnp.int32).reshape(1)
 
     def swap(array, axis):
@@ -412,7 +432,7 @@
         place,
         [
             tile_index, by_visibility_row(vis_coords), by_visibility_row(vis_values),
-            columns, rows, bell, left, taper_rows, taper_cols, right, fold,
+            columns, rows, bell, left, taper_rows, taper_cols, right, fold, spin,
         ],
     )
     total = (keep.astype(F32) + swap(send, "core").astype(F32)).astype(BF16)

time: 58.9 us -> 58.4 us (level)
  no operation moved by 1% of the time
where the time goes in v6:
time: 58.4 us; the launch traced here: 58.3 us
  blocking collectives  30.9 us (53%)
  Pallas kernels  13.3 us (23%)
  starting transfers between devices  12.1 us (21%)
  waiting for transfers between devices  1.75 us (3%)
    all_to_all x1, blocking collectives, shards(): lax.all_to_all(outgoing, ('grid', 'x_lo'), split_axis=0, concat_axis=0, t...  30.9 us
    ppermute x7, starting transfers between devices, swap(): return lax.ppermute(array, axis, [(0, 1), (1, 0)])  12.1 us
    pallas_call x1, Pallas kernels, gridding(): pl.pallas_call(gridding_kernel, out_shape=[half] * 2 + [jax.ShapeDtypeStr...  9.51 us
    pallas_call x1, Pallas kernels, facet(): pl.pallas_call(facet_kernel, out_shape=jax.ShapeDtypeStruct((2, ROWS_OUT,...  2.93 us
    ppermute x7, waiting for transfers between devices, swap(): return lax.ppermute(array, axis, [(0, 1), (1, 0)])  1.75 us
  transfers between devices with their start and end apart: 7, of which 2 were waited for; matrix products, arithmetic and copies ran while one was open for 0% of the time, Pallas kernels for 1%

profile of v6, /device:TPU:1, one launch (start us, length us, event | category | flops | bytes accessed | tf_op | source)
XLA Modules:
  0.0 58.3 jit_solution(2490835674920825987)
XLA Ops:
  0.0 9.5 %gridding.1 = (bf16[8,256,128]{2,1,0:T(8,128)(2,1)S(1)}, bf16[8,256,128]{2,1,0:T(8,128)(2,1)S(1)}, bf16[512,512]{1,0:T(8,128)(2,1)S(1)}, f32[256,128]{1,0:T(8,12...) custom-call(s32[1]{0:T(128)} %bitcast.place_ref, ...), custom_call_target="tpu_custom_call" | custom-call | tf_op jit(solution)/shard_map/gridding/pallas_call | solution.py:269
  9.5 3.3 %collective-permute-start = (bf16[8,256,128]{2,1,0:T(8,128)(2,1)S(1)}, bf16[8,256,128]{2,1,0:T(8,128)(2,1)S(1)}, u32[]{:S(2)}, u32[]{:S(2)}) collective-permute-start(bf16[8,256,128]{2,1,0:T(8,128)(2,1)S(1)} %get-tuple-element.15), channel_id=1, source_target_pairs={{0,1},{1,0},{2,3},{3,2},{4,5},{5,4},{6,7},{7,6},{8,9},{9,8},{10,11... | collective-permute-start | bytes 1572872 | tf_op jit(solution)/shard_map/ppermute | solution.py:429
  12.8 1.5 %collective-permute-done = bf16[8,256,128]{2,1,0:T(8,128)(2,1)S(1)} collective-permute-done((bf16[8,256,128]{2,1,0:T(8,128)(2,1)S(1)}, bf16[8,256,128]{2,1,0:T(8,128)(2,1)S(1)}, u32[]{:S(2)}, u32[]{:S(2)}) %collective-permute-start) | collective-permute-done | bytes 524320 | tf_op jit(solution)/shard_map/ppermute | solution.py:429
  14.4 0.1 add_convert_fusion
  14.5 30.9 %all_to_all.5 = bf16[128,16,128]{2,1,0:T(8,128)(2,1)S(1)} all-to-all(bf16[128,16,128]{2,1,0:T(8,128)(2,1)S(1)} %bitcast.23), channel_id=1, replica_groups=mesh['grid'=64,'x_lo'=2,'core'=2] {'grid','x_lo'}, dimensions={0} | all-to-all | bytes 1048576 | tf_op jit(solution)/shard_map/all_to_all | solution.py:440
  45.4 0.1 pair_sum.1
  45.5 0.1 collective-permute-start.5
  45.6 1.5 %collective-permute-start.2 = (bf16[4,128,128]{2,1,0:T(8,128)(2,1)S(1)}, bf16[4,128,128]{2,1,0:T(8,128)(2,1)S(1)}, u32[]{:S(2)}, u32[]{:S(2)}) collective-permute-start(bf16[4,128,128]{2,1,0:T(8,128)(2,1)S(1)} %bitcast.17), channel_id=1, source_target_pairs={{0,2},{2,0},{1,3},{3,1},{4,6},{6,4},{5,7},{7,5},{8,10},{10,8},{9,1... | collective-permute-start | bytes 393224 | tf_op jit(solution)/shard_map/ppermute | solution.py:429
  47.1 2.9 %collective-permute-start.4 = (bf16[4,128,128]{2,1,0:T(8,128)(2,1)S(1)}, bf16[4,128,128]{2,1,0:T(8,128)(2,1)S(1)}, u32[]{:S(2)}, u32[]{:S(2)}) collective-permute-start(bf16[4,128,128]{2,1,0:T(8,128)(2,1)S(1)} %bitcast.21), channel_id=1, source_target_pairs={{0,1},{1,0},{2,3},{3,2},{4,5},{5,4},{6,7},{7,6},{8,9},{9,8},{10,11... | collective-permute-start | bytes 393224 | tf_op jit(solution)/shard_map/ppermute | solution.py:429
  50.0 0.0 collective-permute-done.5.by_x
  50.0 2.9 %collective-permute-start.6 = (bf16[4,128,128]{2,1,0:T(8,128)(2,1)S(1)}, bf16[4,128,128]{2,1,0:T(8,128)(2,1)S(1)}, u32[]{:S(2)}, u32[]{:S(2)}) collective-permute-start(bf16[4,128,128]{2,1,0:T(8,128)(2,1)S(1)} %collective-permute-done.5.by_x), channel_id=1, source_target_pairs={{0,1},{1,0},{2,3},{3,2},{4,5},{5,4},{6,7},{7,6},{8,9},{9,8},{10,11... | collective-permute-start | bytes 393224 | tf_op jit(solution)/shard_map/ppermute | solution.py:429
  52.9 0.0 collective-permute-start.1
  52.9 0.0 collective-permute-done.2.by_x
  52.9 1.4 %collective-permute-start.3 = (bf16[4,128,128]{2,1,0:T(8,128)(2,1)S(1)}, bf16[4,128,128]{2,1,0:T(8,128)(2,1)S(1)}, u32[]{:S(2)}, u32[]{:S(2)}) collective-permute-start(bf16[4,128,128]{2,1,0:T(8,128)(2,1)S(1)} %collective-permute-done.2.by_x), channel_id=1, source_target_pairs={{0,1},{1,0},{2,3},{3,2},{4,5},{5,4},{6,7},{7,6},{8,9},{9,8},{10,11... | collective-permute-start | bytes 393224 | tf_op jit(solution)/shard_map/ppermute | solution.py:429
  54.3 0.0 collective-permute-done.4.by_core
  54.3 0.0 collective-permute-done.6.by_both
  54.3 0.8 %mixture_half.1.half_mixture = bf16[2,256,256]{2,1,0:T(8,128)(2,1)S(1)} custom-call(bf16[4,128,128]{2,1,0:T(8,128)(2,1)S(1)} %bitcast.22, bf16[4,128,128]{2,1,0:T(8,128)(2,1)S(1)} %collective-permute-done.4.by_core, bf16[4,128,128]{2,1,0:T(8,128)(2,1)S(1)} %collective-permute-done.5.by_x, bf16[4,128,128]{2,1,0:T(8,128)(2,1)S(1)} %collective-permute-done.6.by_both, ...), custom_call_target="tpu_custom_call" | custom-call | flops 268435456 | bytes 1048576 | tf_op jit(solution)/shard_map/mixture_half/pallas_call | solution.py:349
  55.1 0.0 collective-permute-done.1.by_core
  55.1 0.2 collective-permute-done.3.by_both
  55.3 2.9 %facet.1 = f32[2,256,1024]{2,1,0:T(8,128)} custom-call(bf16[4,128,128]{2,1,0:T(8,128)(2,1)S(1)} %bitcast.19, bf16[4,128,128]{2,1,0:T(8,128)(2,1)S(1)} %collective-permute-done.1.by_core, bf16[4,128,128]{2,1,0:T(8,128)(2,1)S(1)} %collective-permute-done.2.by_x, bf16[4,128,128]{2,1,0:T(8,128)(2,1)S(1)} %collective-permute-done.3.by_both, ...), custom_call_target="tpu_custom_call" | custom-call | tf_op jit(solution)/shard_map/facet/pallas_call | solution.py:404
Async XLA Ops:
  9.5 4.9 %collective-permute-start = (bf16[8,256,128]{2,1,0:T(8,128)(2,1)S(1)}, bf16[8,256,128]{2,1,0:T(8,128)(2,1)S(1)}, u32[]{:S(2)}, u32[]{:S(2)}) collective-permute-start(bf16[8,256,128]{2,1,0:T(8,128)(2,1)S(1)} %get-tuple-element.15), channel_id=1, source_target_pairs={{0,1},{1,0},{2,3},{3,2},{4,5},{5,4},{6,7},{7,6},{8,9},{9,8},{10,11... | collective-permute-start | bytes 1572872 | tf_op jit(solution)/shard_map/ppermute | solution.py:429
  45.5 4.5 %collective-permute-start.5 = (bf16[4,128,128]{2,1,0:T(8,128)(2,1)S(1)}, bf16[4,128,128]{2,1,0:T(8,128)(2,1)S(1)}, u32[]{:S(2)}, u32[]{:S(2)}) collective-permute-start(bf16[4,128,128]{2,1,0:T(8,128)(2,1)S(1)} %bitcast.20), channel_id=1, source_target_pairs={{0,2},{2,0},{1,3},{3,1},{4,6},{6,4},{5,7},{7,5},{8,10},{10,8},{9,1... | collective-permute-start | bytes 393224 | tf_op jit(solution)/shard_map/ppermute | solution.py:429
  45.6 7.3 %collective-permute-start.2 = (bf16[4,128,128]{2,1,0:T(8,128)(2,1)S(1)}, bf16[4,128,128]{2,1,0:T(8,128)(2,1)S(1)}, u32[]{:S(2)}, u32[]{:S(2)}) collective-permute-start(bf16[4,128,128]{2,1,0:T(8,128)(2,1)S(1)} %bitcast.17), channel_id=1, source_target_pairs={{0,2},{2,0},{1,3},{3,1},{4,6},{6,4},{5,7},{7,5},{8,10},{10,8},{9,1... | collective-permute-start | bytes 393224 | tf_op jit(solution)/shard_map/ppermute | solution.py:429
  47.1 7.3 %collective-permute-start.4 = (bf16[4,128,128]{2,1,0:T(8,128)(2,1)S(1)}, bf16[4,128,128]{2,1,0:T(8,128)(2,1)S(1)}, u32[]{:S(2)}, u32[]{:S(2)}) collective-permute-start(bf16[4,128,128]{2,1,0:T(8,128)(2,1)S(1)} %bitcast.21), channel_id=1, source_target_pairs={{0,1},{1,0},{2,3},{3,2},{4,5},{5,4},{6,7},{7,6},{8,9},{9,8},{10,11... | collective-permute-start | bytes 393224 | tf_op jit(solution)/shard_map/ppermute | solution.py:429
  50.0 4.3 %collective-permute-start.6 = (bf16[4,128,128]{2,1,0:T(8,128)(2,1)S(1)}, bf16[4,128,128]{2,1,0:T(8,128)(2,1)S(1)}, u32[]{:S(2)}, u32[]{:S(2)}) collective-permute-start(bf16[4,128,128]{2,1,0:T(8,128)(2,1)S(1)} %collective-permute-done.5.by_x), channel_id=1, source_target_pairs={{0,1},{1,0},{2,3},{3,2},{4,5},{5,4},{6,7},{7,6},{8,9},{9,8},{10,11... | collective-permute-start | bytes 393224 | tf_op jit(solution)/shard_map/ppermute | solution.py:429
  52.9 2.2 %collective-permute-start.1 = (bf16[4,128,128]{2,1,0:T(8,128)(2,1)S(1)}, bf16[4,128,128]{2,1,0:T(8,128)(2,1)S(1)}, u32[]{:S(2)}, u32[]{:S(2)}) collective-permute-start(bf16[4,128,128]{2,1,0:T(8,128)(2,1)S(1)} %bitcast.18), channel_id=1, source_target_pairs={{0,1},{1,0},{2,3},{3,2},{4,5},{5,4},{6,7},{7,6},{8,9},{9,8},{10,11... | collective-permute-start | bytes 393224 | tf_op jit(solution)/shard_map/ppermute | solution.py:429
  52.9 2.4 %collective-permute-start.3 = (bf16[4,128,128]{2,1,0:T(8,128)(2,1)S(1)}, bf16[4,128,128]{2,1,0:T(8,128)(2,1)S(1)}, u32[]{:S(2)}, u32[]{:S(2)}) collective-permute-start(bf16[4,128,128]{2,1,0:T(8,128)(2,1)S(1)} %collective-permute-done.2.by_x), channel_id=1, source_target_pairs={{0,1},{1,0},{2,3},{3,2},{4,5},{5,4},{6,7},{7,6},{8,9},{9,8},{10,11... | collective-permute-start | bytes 393224 | tf_op jit(solution)/shard_map/ppermute | solution.py:429

commit v7 on v6

--- a/solution.py
+++ b/solution.py
@@ -100,8 +100,8 @@
 def gridding_kernel(
     place_ref, tiles_hbm, coords_hbm, values_hbm, columns_hbm, rows_hbm, bell_hbm, left_hbm, taper_rows_hbm, taper_cols_hbm,
     right_hbm, fold_hbm, spin_hbm,
-    keep_ref, send_ref, left_ref, taper_rows_ref, taper_cols_ref, right_ref, fold_ref,
-    tile_ref, coords, values, step8, slope, height, acc, grid16, halves, stacked, columns, rows, bell_ref,
+    send_ref, rows, stacked, left_ref, taper_rows_ref, taper_cols_ref, right_ref, fold_ref,
+    tile_ref, coords, values, step8, slope, height, acc, grid16, halves, columns, bell_ref,
     spin, apart, sems,
 ):
     place = place_ref[0]
@@ -245,20 +245,38 @@
         stacked[3, :step, at] = (diff02 - turned[3]).astype(BF16)
         stacked[3, step:, at] = (turned[2] + diff13).astype(BF16)
 
-    core = place % 2
-
+    facet_rows(1 - place % 2, rows, stacked, send_ref)
+
+
+def facet_rows(core, rows, stacked, out):
     @pl.loop(0, WIDTH // 256)
     def _(n):
         at = pl.ds(pl.multiple_of(n * 256, 256), 256)
-        for which, out in ((core, keep_ref), (1 - core, send_ref)):
-            for x_lo in range(2):
-                v = which + 2 * x_lo
-                spectra = jnp.dot(rows[v], stacked[v, :, at], preferred_element_type=F32).astype(BF16)
-                for i in range(2):
-                    for ra in range(NBLK):
-                        first = (ra * 2 + x_lo) * QUARTER
-                        block = spectra[ra * QUARTER : (ra + 1) * QUARTER, i * LANES : (i + 1) * LANES]
-                        out[n * 2 + i, first : first + QUARTER] = block
+        for x_lo in range(2):
+            v = core + 2 * x_lo
+            spectra = jnp.dot(rows[v], stacked[v, :, at], preferred_element_type=F32).astype(BF16)
+            for i in range(2):
+                for ra in range(NBLK):
+                    first = (ra * 2 + x_lo) * QUARTER
+                    block = spectra[ra * QUARTER : (ra + 1) * QUARTER, i * LANES : (i + 1) * LANES]
+                    out[n * 2 + i, first : first + QUARTER] = block
+
+
+def keep_kernel(place_ref, rows, stacked, out):
+    facet_rows(place_ref[0] % 2, rows, stacked, out)
+
+
+def keep_half(place, rows, stacked):
+    vector = pl.BlockSpec(memory_space=pltpu.VMEM)
+    return pl.pallas_call(
+        keep_kernel,
+        out_shape=jax.ShapeDtypeStruct((NBLK, HALF, LANES), BF16),
+        in_specs=[pl.BlockSpec(memory_space=pltpu.SMEM), vector, vector],
+        out_specs=vector,
+        compiler_params=pltpu.CompilerParams(vmem_limit_bytes=24 * 1024 * 1024),
+        cost_estimate=pl.CostEstimate(flops=2**27, bytes_accessed=2**20, transcendentals=0),
+        name="keep_half",
+    )(place, rows, stacked)
 
 
 def gridding(place, arrays):
@@ -268,8 +286,10 @@
     plane = pltpu.VMEM((BLOCKS * 8, LANES), F32)
     return pl.pallas_call(
         gridding_kernel,
-        out_shape=[half] * 2
+        out_shape=[half]
         + [
+            jax.ShapeDtypeStruct((4, ROWS, SUB // 2), BF16),
+            jax.ShapeDtypeStruct((4, SUB // 2, WIDTH), BF16),
             jax.ShapeDtypeStruct((2 * ROWS_OUT, SUB), BF16),
             jax.ShapeDtypeStruct((ROWS_OUT, LANES), F32),
             jax.ShapeDtypeStruct((1, FAC), F32),
@@ -277,16 +297,14 @@
             jax.ShapeDtypeStruct((SUB, 2 * LANES), BF16),
         ],
         in_specs=[pl.BlockSpec(memory_space=pltpu.SMEM)] + [hbm] * len(arrays),
-        out_specs=[vector] * 7,
+        out_specs=[vector] * 8,
         scratch_shapes=[
             pltpu.SMEM((1, BLOCKS), jnp.int32),
             plane, plane, plane, plane, plane,
             pltpu.VMEM((SUB, WIDTH), F32),
             pltpu.VMEM((2, SUB, SUB), BF16),
             pltpu.VMEM((2, SUB, SUB), F32),
-            pltpu.VMEM((4, SUB // 2, WIDTH), BF16),
             pltpu.VMEM((2, SUB, SUB), BF16),
-            pltpu.VMEM((4, ROWS, SUB // 2), BF16),
             pltpu.VMEM((2, TILE, LANES), F32),
             pltpu.VMEM((2 * LANES, 2 * LANES), BF16),
             pltpu.VMEM((4, SUB // 4, WIDTH), BF16),
@@ -428,14 +446,16 @@
     def swap(array, axis):
         return lax.ppermute(array, axis, [(0, 1), (1, 0)])
 
-    keep, send, left, taper_rows, taper_cols, right, fold = gridding(
+    send, rows, stacked, left, taper_rows, taper_cols, right, fold = gridding(
         place,
         [
             tile_index, by_visibility_row(vis_coords), by_visibility_row(vis_values),
             columns, rows, bell, left, taper_rows, taper_cols, right, fold, spin,
         ],
     )
-    total = (keep.astype(F32) + swap(send, "core").astype(F32)).astype(BF16)
+    got = swap(send, "core")
+    keep = keep_half(place, rows, stacked)
+    total = (keep.astype(F32) + got.astype(F32)).astype(BF16)
     outgoing = total.reshape(NBLK * NBLK * 2, QUARTER, LANES)
     arrived = lax.all_to_all(outgoing, ("grid", "x_lo"), split_axis=0, concat_axis=0, tiled=True)
     halves = [half.reshape(NBLK // 2, ROWS, LANES) for half in pair_sum(arrived.reshape(NBLK * NBLK, 2, QUARTER, LANES))]

time: 58.4 us -> 58.2 us (level)
  waiting for transfers between devices: 1.75 us -> 0.95 us
  Pallas kernels: 13.3 us -> 13.9 us
    ppermute x7, waiting for transfers between devices: 1.75 us -> 0.95 us  [swap(): return lax.ppermute(array, axis, [(0, 1), (1, 0)])]
    pallas_call x1 -> x2, Pallas kernels: 9.51 us -> 10.1 us  [the longest x1 9.31 us: gridding(): pl.pallas_call(gridding_kernel, out_shape=[half] + [jax.ShapeDtypeStruct(...]
  transfers between devices with their start and end apart: 7 -> 7, of which waited for: 2 -> 2; matrix products, arithmetic and copies ran while one was open for 0% -> 0% of each run, Pallas kernels for 1% -> 3%
where the time goes in v7:
time: 58.2 us; the launch traced here: 58.1 us
  blocking collectives  30.9 us (53%)
  Pallas kernels  13.9 us (24%)
  starting transfers between devices  12.1 us (21%)
  waiting for transfers between devices  0.95 us (2%)
    all_to_all x1, blocking collectives, shards(): lax.all_to_all(outgoing, ('grid', 'x_lo'), split_axis=0, concat_axis=0, t...  30.9 us
    ppermute x7, starting transfers between devices, swap(): return lax.ppermute(array, axis, [(0, 1), (1, 0)])  12.1 us
    pallas_call x1, Pallas kernels, gridding(): pl.pallas_call(gridding_kernel, out_shape=[half] + [jax.ShapeDtypeStruct(...  9.31 us
    pallas_call x1, Pallas kernels, facet(): pl.pallas_call(facet_kernel, out_shape=jax.ShapeDtypeStruct((2, ROWS_OUT,...  2.94 us
  transfers between devices with their start and end apart: 7, of which 2 were waited for; matrix products, arithmetic and copies ran while one was open for 0% of the time, Pallas kernels for 3%

profile of v7, /device:TPU:1, one launch (start us, length us, event | category | flops | bytes accessed | tf_op | source)
XLA Modules:
  0.0 58.1 jit_solution(4220111579340754462)
XLA Ops:
  0.0 9.3 %gridding.1 = (bf16[8,256,128]{2,1,0:T(8,128)(2,1)S(1)}, bf16[4,128,256]{2,1,0:T(8,128)(2,1)S(1)}, bf16[4,256,1024]{2,1,0:T(8,128)(2,1)S(1)}, bf16[512,512]{1,0:...) custom-call(s32[1]{0:T(128)} %bitcast.place_ref, ...), custom_call_target="tpu_custom_call" | custom-call | tf_op jit(solution)/shard_map/gridding/pallas_call | solution.py:287
  9.3 3.3 %collective-permute-start = (bf16[8,256,128]{2,1,0:T(8,128)(2,1)S(1)}, bf16[8,256,128]{2,1,0:T(8,128)(2,1)S(1)}, u32[]{:S(2)}, u32[]{:S(2)}) collective-permute-start(bf16[8,256,128]{2,1,0:T(8,128)(2,1)S(1)} %get-tuple-element.17), channel_id=1, source_target_pairs={{0,1},{1,0},{2,3},{3,2},{4,5},{5,4},{6,7},{7,6},{8,9},{9,8},{10,11... | collective-permute-start | bytes 1572872 | tf_op jit(solution)/shard_map/ppermute | solution.py:447
  12.7 0.8 %keep_half.1 = bf16[8,256,128]{2,1,0:T(8,128)(2,1)S(1)} custom-call(s32[1]{0:T(128)} %bitcast.place_ref, bf16[4,128,256]{2,1,0:T(8,128)(2,1)S(1)} %get-tuple-element.15.rows, bf16[4,256,1024]{2,1,0:T(8,128)(2,1)S(1)} %get-tuple-element.16.stacked), custom_call_target="tpu_custom_call" | custom-call | flops 134217728 | bytes 1048576 | tf_op jit(solution)/shard_map/keep_half/pallas_call | solution.py:271
  13.5 0.7 %collective-permute-done = bf16[8,256,128]{2,1,0:T(8,128)(2,1)S(1)} collective-permute-done((bf16[8,256,128]{2,1,0:T(8,128)(2,1)S(1)}, bf16[8,256,128]{2,1,0:T(8,128)(2,1)S(1)}, u32[]{:S(2)}, u32[]{:S(2)}) %collective-permute-start) | collective-permute-done | bytes 524320 | tf_op jit(solution)/shard_map/ppermute | solution.py:447
  14.2 0.1 add_convert_fusion
  14.3 30.9 %all_to_all.5 = bf16[128,16,128]{2,1,0:T(8,128)(2,1)S(1)} all-to-all(bf16[128,16,128]{2,1,0:T(8,128)(2,1)S(1)} %bitcast.23), channel_id=1, replica_groups=mesh['grid'=64,'x_lo'=2,'core'=2] {'grid','x_lo'}, dimensions={0} | all-to-all | bytes 1048576 | tf_op jit(solution)/shard_map/all_to_all | solution.py:460
  45.2 0.1 pair_sum.1
  45.3 0.1 collective-permute-start.5
  45.4 1.5 %collective-permute-start.2 = (bf16[4,128,128]{2,1,0:T(8,128)(2,1)S(1)}, bf16[4,128,128]{2,1,0:T(8,128)(2,1)S(1)}, u32[]{:S(2)}, u32[]{:S(2)}) collective-permute-start(bf16[4,128,128]{2,1,0:T(8,128)(2,1)S(1)} %bitcast.17), channel_id=1, source_target_pairs={{0,2},{2,0},{1,3},{3,1},{4,6},{6,4},{5,7},{7,5},{8,10},{10,8},{9,1... | collective-permute-start | bytes 393224 | tf_op jit(solution)/shard_map/ppermute | solution.py:447
  46.9 2.9 %collective-permute-start.4 = (bf16[4,128,128]{2,1,0:T(8,128)(2,1)S(1)}, bf16[4,128,128]{2,1,0:T(8,128)(2,1)S(1)}, u32[]{:S(2)}, u32[]{:S(2)}) collective-permute-start(bf16[4,128,128]{2,1,0:T(8,128)(2,1)S(1)} %bitcast.21), channel_id=1, source_target_pairs={{0,1},{1,0},{2,3},{3,2},{4,5},{5,4},{6,7},{7,6},{8,9},{9,8},{10,11... | collective-permute-start | bytes 393224 | tf_op jit(solution)/shard_map/ppermute | solution.py:447
  49.8 0.0 collective-permute-done.5.by_x
  49.8 2.9 %collective-permute-start.6 = (bf16[4,128,128]{2,1,0:T(8,128)(2,1)S(1)}, bf16[4,128,128]{2,1,0:T(8,128)(2,1)S(1)}, u32[]{:S(2)}, u32[]{:S(2)}) collective-permute-start(bf16[4,128,128]{2,1,0:T(8,128)(2,1)S(1)} %collective-permute-done.5.by_x), channel_id=1, source_target_pairs={{0,1},{1,0},{2,3},{3,2},{4,5},{5,4},{6,7},{7,6},{8,9},{9,8},{10,11... | collective-permute-start | bytes 393224 | tf_op jit(solution)/shard_map/ppermute | solution.py:447
  52.7 0.0 collective-permute-start.1
  52.7 0.0 collective-permute-done.2.by_x
  52.7 1.4 %collective-permute-start.3 = (bf16[4,128,128]{2,1,0:T(8,128)(2,1)S(1)}, bf16[4,128,128]{2,1,0:T(8,128)(2,1)S(1)}, u32[]{:S(2)}, u32[]{:S(2)}) collective-permute-start(bf16[4,128,128]{2,1,0:T(8,128)(2,1)S(1)} %collective-permute-done.2.by_x), channel_id=1, source_target_pairs={{0,1},{1,0},{2,3},{3,2},{4,5},{5,4},{6,7},{7,6},{8,9},{9,8},{10,11... | collective-permute-start | bytes 393224 | tf_op jit(solution)/shard_map/ppermute | solution.py:447
  54.1 0.0 collective-permute-done.4.by_core
  54.1 0.0 collective-permute-done.6.by_both
  54.1 0.8 %mixture_half.1.half_mixture = bf16[2,256,256]{2,1,0:T(8,128)(2,1)S(1)} custom-call(bf16[4,128,128]{2,1,0:T(8,128)(2,1)S(1)} %bitcast.22, bf16[4,128,128]{2,1,0:T(8,128)(2,1)S(1)} %collective-permute-done.4.by_core, bf16[4,128,128]{2,1,0:T(8,128)(2,1)S(1)} %collective-permute-done.5.by_x, bf16[4,128,128]{2,1,0:T(8,128)(2,1)S(1)} %collective-permute-done.6.by_both, ...), custom_call_target="tpu_custom_call" | custom-call | flops 268435456 | bytes 1048576 | tf_op jit(solution)/shard_map/mixture_half/pallas_call | solution.py:367
  54.9 0.0 collective-permute-done.1.by_core
  54.9 0.2 collective-permute-done.3.by_both
  55.1 2.9 %facet.1 = f32[2,256,1024]{2,1,0:T(8,128)} custom-call(bf16[4,128,128]{2,1,0:T(8,128)(2,1)S(1)} %bitcast.19, bf16[4,128,128]{2,1,0:T(8,128)(2,1)S(1)} %collective-permute-done.1.by_core, bf16[4,128,128]{2,1,0:T(8,128)(2,1)S(1)} %collective-permute-done.2.by_x, bf16[4,128,128]{2,1,0:T(8,128)(2,1)S(1)} %collective-permute-done.3.by_both, ...), custom_call_target="tpu_custom_call" | custom-call | tf_op jit(solution)/shard_map/facet/pallas_call | solution.py:422
Async XLA Ops:
  9.3 4.9 %collective-permute-start = (bf16[8,256,128]{2,1,0:T(8,128)(2,1)S(1)}, bf16[8,256,128]{2,1,0:T(8,128)(2,1)S(1)}, u32[]{:S(2)}, u32[]{:S(2)}) collective-permute-start(bf16[8,256,128]{2,1,0:T(8,128)(2,1)S(1)} %get-tuple-element.17), channel_id=1, source_target_pairs={{0,1},{1,0},{2,3},{3,2},{4,5},{5,4},{6,7},{7,6},{8,9},{9,8},{10,11... | collective-permute-start | bytes 1572872 | tf_op jit(solution)/shard_map/ppermute | solution.py:447
  45.3 4.5 %collective-permute-start.5 = (bf16[4,128,128]{2,1,0:T(8,128)(2,1)S(1)}, bf16[4,128,128]{2,1,0:T(8,128)(2,1)S(1)}, u32[]{:S(2)}, u32[]{:S(2)}) collective-permute-start(bf16[4,128,128]{2,1,0:T(8,128)(2,1)S(1)} %bitcast.20), channel_id=1, source_target_pairs={{0,2},{2,0},{1,3},{3,1},{4,6},{6,4},{5,7},{7,5},{8,10},{10,8},{9,1... | collective-permute-start | bytes 393224 | tf_op jit(solution)/shard_map/ppermute | solution.py:447
  45.4 7.3 %collective-permute-start.2 = (bf16[4,128,128]{2,1,0:T(8,128)(2,1)S(1)}, bf16[4,128,128]{2,1,0:T(8,128)(2,1)S(1)}, u32[]{:S(2)}, u32[]{:S(2)}) collective-permute-start(bf16[4,128,128]{2,1,0:T(8,128)(2,1)S(1)} %bitcast.17), channel_id=1, source_target_pairs={{0,2},{2,0},{1,3},{3,1},{4,6},{6,4},{5,7},{7,5},{8,10},{10,8},{9,1... | collective-permute-start | bytes 393224 | tf_op jit(solution)/shard_map/ppermute | solution.py:447
  46.9 7.3 %collective-permute-start.4 = (bf16[4,128,128]{2,1,0:T(8,128)(2,1)S(1)}, bf16[4,128,128]{2,1,0:T(8,128)(2,1)S(1)}, u32[]{:S(2)}, u32[]{:S(2)}) collective-permute-start(bf16[4,128,128]{2,1,0:T(8,128)(2,1)S(1)} %bitcast.21), channel_id=1, source_target_pairs={{0,1},{1,0},{2,3},{3,2},{4,5},{5,4},{6,7},{7,6},{8,9},{9,8},{10,11... | collective-permute-start | bytes 393224 | tf_op jit(solution)/shard_map/ppermute | solution.py:447
  49.8 4.3 %collective-permute-start.6 = (bf16[4,128,128]{2,1,0:T(8,128)(2,1)S(1)}, bf16[4,128,128]{2,1,0:T(8,128)(2,1)S(1)}, u32[]{:S(2)}, u32[]{:S(2)}) collective-permute-start(bf16[4,128,128]{2,1,0:T(8,128)(2,1)S(1)} %collective-permute-done.5.by_x), channel_id=1, source_target_pairs={{0,1},{1,0},{2,3},{3,2},{4,5},{5,4},{6,7},{7,6},{8,9},{9,8},{10,11... | collective-permute-start | bytes 393224 | tf_op jit(solution)/shard_map/ppermute | solution.py:447
  52.7 2.2 %collective-permute-start.1 = (bf16[4,128,128]{2,1,0:T(8,128)(2,1)S(1)}, bf16[4,128,128]{2,1,0:T(8,128)(2,1)S(1)}, u32[]{:S(2)}, u32[]{:S(2)}) collective-permute-start(bf16[4,128,128]{2,1,0:T(8,128)(2,1)S(1)} %bitcast.18), channel_id=1, source_target_pairs={{0,1},{1,0},{2,3},{3,2},{4,5},{5,4},{6,7},{7,6},{8,9},{9,8},{10,11... | collective-permute-start | bytes 393224 | tf_op jit(solution)/shard_map/ppermute | solution.py:447
  52.7 2.4 %collective-permute-start.3 = (bf16[4,128,128]{2,1,0:T(8,128)(2,1)S(1)}, bf16[4,128,128]{2,1,0:T(8,128)(2,1)S(1)}, u32[]{:S(2)}, u32[]{:S(2)}) collective-permute-start(bf16[4,128,128]{2,1,0:T(8,128)(2,1)S(1)} %collective-permute-done.2.by_x), channel_id=1, source_target_pairs={{0,1},{1,0},{2,3},{3,2},{4,5},{5,4},{6,7},{7,6},{8,9},{9,8},{10,11... | collective-permute-start | bytes 393224 | tf_op jit(solution)/shard_map/ppermute | solution.py:447

commit v8 on v7

--- a/solution.py
+++ b/solution.py
@@ -110,15 +110,17 @@
     last = [(left_hbm.at[place], left_ref), (taper_rows_hbm.at[place], taper_rows_ref)]
     last += [(taper_cols_hbm, taper_cols_ref), (right_hbm, right_ref), (fold_hbm, fold_ref)]
     copies = [pltpu.make_async_copy(*ends, sems.at[i]) for i, ends in enumerate(first + later + last)]
-    for copy in copies:
+    for copy in copies[: len(first)]:
         copy.start()
     acc[...] = jnp.zeros_like(acc)
     for copy in copies[: len(first)]:
         copy.wait()
-
-    @pl.loop(0, BLOCKS * 8 // 64)
+    for copy in copies[len(first) :]:
+        copy.start()
+
+    @pl.loop(0, BLOCKS * 8 // 128)
     def _(chunk):
-        at = pl.ds(pl.multiple_of(chunk * 64, 64), 64)
+        at = pl.ds(pl.multiple_of(chunk * 128, 128), 128)
         c = coords[at, :]
         r = jnp.round(c)
         c = jnp.where(c == r, c + (c * 2.0**-23 + 1e-20), c)

time: 58.2 us -> 58.2 us (level)
  no operation moved by 1% of the time
where the time goes in v8:
time: 58.2 us; the launch traced here: 58 us
  blocking collectives  30.9 us (53%)
  Pallas kernels  13.9 us (24%)
  starting transfers between devices  12.1 us (21%)
  waiting for transfers between devices  0.95 us (2%)
    all_to_all x1, blocking collectives, shards(): lax.all_to_all(outgoing, ('grid', 'x_lo'), split_axis=0, concat_axis=0, t...  30.9 us
    ppermute x7, starting transfers between devices, swap(): return lax.ppermute(array, axis, [(0, 1), (1, 0)])  12.1 us
    pallas_call x1, Pallas kernels, gridding(): pl.pallas_call(gridding_kernel, out_shape=[half] + [jax.ShapeDtypeStruct(...  9.31 us
    pallas_call x1, Pallas kernels, facet(): pl.pallas_call(facet_kernel, out_shape=jax.ShapeDtypeStruct((2, ROWS_OUT,...  2.94 us
  transfers between devices with their start and end apart: 7, of which 2 were waited for; matrix products, arithmetic and copies ran while one was open for 0% of the time, Pallas kernels for 3%

profile of v8, /device:TPU:1, one launch (start us, length us, event | category | flops | bytes accessed | tf_op | source)
XLA Modules:
  0.0 58.0 jit_solution(394487792722180623)
XLA Ops:
  0.0 9.3 %gridding.1 = (bf16[8,256,128]{2,1,0:T(8,128)(2,1)S(1)}, bf16[4,128,256]{2,1,0:T(8,128)(2,1)S(1)}, bf16[4,256,1024]{2,1,0:T(8,128)(2,1)S(1)}, bf16[512,512]{1,0:...) custom-call(s32[1]{0:T(128)} %bitcast.place_ref, ...), custom_call_target="tpu_custom_call" | custom-call | tf_op jit(solution)/shard_map/gridding/pallas_call | solution.py:289
  9.3 3.3 %collective-permute-start = (bf16[8,256,128]{2,1,0:T(8,128)(2,1)S(1)}, bf16[8,256,128]{2,1,0:T(8,128)(2,1)S(1)}, u32[]{:S(2)}, u32[]{:S(2)}) collective-permute-start(bf16[8,256,128]{2,1,0:T(8,128)(2,1)S(1)} %get-tuple-element.17), channel_id=1, source_target_pairs={{0,1},{1,0},{2,3},{3,2},{4,5},{5,4},{6,7},{7,6},{8,9},{9,8},{10,11... | collective-permute-start | bytes 1572872 | tf_op jit(solution)/shard_map/ppermute | solution.py:449
  12.6 0.8 %keep_half.1 = bf16[8,256,128]{2,1,0:T(8,128)(2,1)S(1)} custom-call(s32[1]{0:T(128)} %bitcast.place_ref, bf16[4,128,256]{2,1,0:T(8,128)(2,1)S(1)} %get-tuple-element.15.rows, bf16[4,256,1024]{2,1,0:T(8,128)(2,1)S(1)} %get-tuple-element.16.stacked), custom_call_target="tpu_custom_call" | custom-call | flops 134217728 | bytes 1048576 | tf_op jit(solution)/shard_map/keep_half/pallas_call | solution.py:273
  13.4 0.7 %collective-permute-done = bf16[8,256,128]{2,1,0:T(8,128)(2,1)S(1)} collective-permute-done((bf16[8,256,128]{2,1,0:T(8,128)(2,1)S(1)}, bf16[8,256,128]{2,1,0:T(8,128)(2,1)S(1)}, u32[]{:S(2)}, u32[]{:S(2)}) %collective-permute-start) | collective-permute-done | bytes 524320 | tf_op jit(solution)/shard_map/ppermute | solution.py:449
  14.2 0.1 add_convert_fusion
  14.3 30.9 %all_to_all.5 = bf16[128,16,128]{2,1,0:T(8,128)(2,1)S(1)} all-to-all(bf16[128,16,128]{2,1,0:T(8,128)(2,1)S(1)} %bitcast.23), channel_id=1, replica_groups=mesh['grid'=64,'x_lo'=2,'core'=2] {'grid','x_lo'}, dimensions={0} | all-to-all | bytes 1048576 | tf_op jit(solution)/shard_map/all_to_all | solution.py:462
  45.2 0.1 pair_sum.1
  45.3 0.1 collective-permute-start.5
  45.4 1.5 %collective-permute-start.2 = (bf16[4,128,128]{2,1,0:T(8,128)(2,1)S(1)}, bf16[4,128,128]{2,1,0:T(8,128)(2,1)S(1)}, u32[]{:S(2)}, u32[]{:S(2)}) collective-permute-start(bf16[4,128,128]{2,1,0:T(8,128)(2,1)S(1)} %bitcast.17), channel_id=1, source_target_pairs={{0,2},{2,0},{1,3},{3,1},{4,6},{6,4},{5,7},{7,5},{8,10},{10,8},{9,1... | collective-permute-start | bytes 393224 | tf_op jit(solution)/shard_map/ppermute | solution.py:449
  46.9 2.9 %collective-permute-start.4 = (bf16[4,128,128]{2,1,0:T(8,128)(2,1)S(1)}, bf16[4,128,128]{2,1,0:T(8,128)(2,1)S(1)}, u32[]{:S(2)}, u32[]{:S(2)}) collective-permute-start(bf16[4,128,128]{2,1,0:T(8,128)(2,1)S(1)} %bitcast.21), channel_id=1, source_target_pairs={{0,1},{1,0},{2,3},{3,2},{4,5},{5,4},{6,7},{7,6},{8,9},{9,8},{10,11... | collective-permute-start | bytes 393224 | tf_op jit(solution)/shard_map/ppermute | solution.py:449
  49.8 0.0 collective-permute-done.5.by_x
  49.8 2.9 %collective-permute-start.6 = (bf16[4,128,128]{2,1,0:T(8,128)(2,1)S(1)}, bf16[4,128,128]{2,1,0:T(8,128)(2,1)S(1)}, u32[]{:S(2)}, u32[]{:S(2)}) collective-permute-start(bf16[4,128,128]{2,1,0:T(8,128)(2,1)S(1)} %collective-permute-done.5.by_x), channel_id=1, source_target_pairs={{0,1},{1,0},{2,3},{3,2},{4,5},{5,4},{6,7},{7,6},{8,9},{9,8},{10,11... | collective-permute-start | bytes 393224 | tf_op jit(solution)/shard_map/ppermute | solution.py:449
  52.7 0.0 collective-permute-start.1
  52.7 0.0 collective-permute-done.2.by_x
  52.7 1.4 %collective-permute-start.3 = (bf16[4,128,128]{2,1,0:T(8,128)(2,1)S(1)}, bf16[4,128,128]{2,1,0:T(8,128)(2,1)S(1)}, u32[]{:S(2)}, u32[]{:S(2)}) collective-permute-start(bf16[4,128,128]{2,1,0:T(8,128)(2,1)S(1)} %collective-permute-done.2.by_x), channel_id=1, source_target_pairs={{0,1},{1,0},{2,3},{3,2},{4,5},{5,4},{6,7},{7,6},{8,9},{9,8},{10,11... | collective-permute-start | bytes 393224 | tf_op jit(solution)/shard_map/ppermute | solution.py:449
  54.1 0.0 collective-permute-done.4.by_core
  54.1 0.0 collective-permute-done.6.by_both
  54.1 0.8 %mixture_half.1.half_mixture = bf16[2,256,256]{2,1,0:T(8,128)(2,1)S(1)} custom-call(bf16[4,128,128]{2,1,0:T(8,128)(2,1)S(1)} %bitcast.22, bf16[4,128,128]{2,1,0:T(8,128)(2,1)S(1)} %collective-permute-done.4.by_core, bf16[4,128,128]{2,1,0:T(8,128)(2,1)S(1)} %collective-permute-done.5.by_x, bf16[4,128,128]{2,1,0:T(8,128)(2,1)S(1)} %collective-permute-done.6.by_both, ...), custom_call_target="tpu_custom_call" | custom-call | flops 268435456 | bytes 1048576 | tf_op jit(solution)/shard_map/mixture_half/pallas_call | solution.py:369
  54.9 0.0 collective-permute-done.1.by_core
  54.9 0.2 collective-permute-done.3.by_both
  55.1 2.9 %facet.1 = f32[2,256,1024]{2,1,0:T(8,128)} custom-call(bf16[4,128,128]{2,1,0:T(8,128)(2,1)S(1)} %bitcast.19, bf16[4,128,128]{2,1,0:T(8,128)(2,1)S(1)} %collective-permute-done.1.by_core, bf16[4,128,128]{2,1,0:T(8,128)(2,1)S(1)} %collective-permute-done.2.by_x, bf16[4,128,128]{2,1,0:T(8,128)(2,1)S(1)} %collective-permute-done.3.by_both, ...), custom_call_target="tpu_custom_call" | custom-call | tf_op jit(solution)/shard_map/facet/pallas_call | solution.py:424
Async XLA Ops:
  9.3 4.8 %collective-permute-start = (bf16[8,256,128]{2,1,0:T(8,128)(2,1)S(1)}, bf16[8,256,128]{2,1,0:T(8,128)(2,1)S(1)}, u32[]{:S(2)}, u32[]{:S(2)}) collective-permute-start(bf16[8,256,128]{2,1,0:T(8,128)(2,1)S(1)} %get-tuple-element.17), channel_id=1, source_target_pairs={{0,1},{1,0},{2,3},{3,2},{4,5},{5,4},{6,7},{7,6},{8,9},{9,8},{10,11... | collective-permute-start | bytes 1572872 | tf_op jit(solution)/shard_map/ppermute | solution.py:449
  45.3 4.5 %collective-permute-start.5 = (bf16[4,128,128]{2,1,0:T(8,128)(2,1)S(1)}, bf16[4,128,128]{2,1,0:T(8,128)(2,1)S(1)}, u32[]{:S(2)}, u32[]{:S(2)}) collective-permute-start(bf16[4,128,128]{2,1,0:T(8,128)(2,1)S(1)} %bitcast.20), channel_id=1, source_target_pairs={{0,2},{2,0},{1,3},{3,1},{4,6},{6,4},{5,7},{7,5},{8,10},{10,8},{9,1... | collective-permute-start | bytes 393224 | tf_op jit(solution)/shard_map/ppermute | solution.py:449
  45.4 7.3 %collective-permute-start.2 = (bf16[4,128,128]{2,1,0:T(8,128)(2,1)S(1)}, bf16[4,128,128]{2,1,0:T(8,128)(2,1)S(1)}, u32[]{:S(2)}, u32[]{:S(2)}) collective-permute-start(bf16[4,128,128]{2,1,0:T(8,128)(2,1)S(1)} %bitcast.17), channel_id=1, source_target_pairs={{0,2},{2,0},{1,3},{3,1},{4,6},{6,4},{5,7},{7,5},{8,10},{10,8},{9,1... | collective-permute-start | bytes 393224 | tf_op jit(solution)/shard_map/ppermute | solution.py:449
  46.9 7.3 %collective-permute-start.4 = (bf16[4,128,128]{2,1,0:T(8,128)(2,1)S(1)}, bf16[4,128,128]{2,1,0:T(8,128)(2,1)S(1)}, u32[]{:S(2)}, u32[]{:S(2)}) collective-permute-start(bf16[4,128,128]{2,1,0:T(8,128)(2,1)S(1)} %bitcast.21), channel_id=1, source_target_pairs={{0,1},{1,0},{2,3},{3,2},{4,5},{5,4},{6,7},{7,6},{8,9},{9,8},{10,11... | collective-permute-start | bytes 393224 | tf_op jit(solution)/shard_map/ppermute | solution.py:449
  49.8 4.3 %collective-permute-start.6 = (bf16[4,128,128]{2,1,0:T(8,128)(2,1)S(1)}, bf16[4,128,128]{2,1,0:T(8,128)(2,1)S(1)}, u32[]{:S(2)}, u32[]{:S(2)}) collective-permute-start(bf16[4,128,128]{2,1,0:T(8,128)(2,1)S(1)} %collective-permute-done.5.by_x), channel_id=1, source_target_pairs={{0,1},{1,0},{2,3},{3,2},{4,5},{5,4},{6,7},{7,6},{8,9},{9,8},{10,11... | collective-permute-start | bytes 393224 | tf_op jit(solution)/shard_map/ppermute | solution.py:449
  52.7 2.2 %collective-permute-start.1 = (bf16[4,128,128]{2,1,0:T(8,128)(2,1)S(1)}, bf16[4,128,128]{2,1,0:T(8,128)(2,1)S(1)}, u32[]{:S(2)}, u32[]{:S(2)}) collective-permute-start(bf16[4,128,128]{2,1,0:T(8,128)(2,1)S(1)} %bitcast.18), channel_id=1, source_target_pairs={{0,1},{1,0},{2,3},{3,2},{4,5},{5,4},{6,7},{7,6},{8,9},{9,8},{10,11... | collective-permute-start | bytes 393224 | tf_op jit(solution)/shard_map/ppermute | solution.py:449
  52.7 2.4 %collective-permute-start.3 = (bf16[4,128,128]{2,1,0:T(8,128)(2,1)S(1)}, bf16[4,128,128]{2,1,0:T(8,128)(2,1)S(1)}, u32[]{:S(2)}, u32[]{:S(2)}) collective-permute-start(bf16[4,128,128]{2,1,0:T(8,128)(2,1)S(1)} %collective-permute-done.2.by_x), channel_id=1, source_target_pairs={{0,1},{1,0},{2,3},{3,2},{4,5},{5,4},{6,7},{7,6},{8,9},{9,8},{10,11... | collective-permute-start | bytes 393224 | tf_op jit(solution)/shard_map/ppermute | solution.py:449

commit v9 on v8

--- a/solution.py
+++ b/solution.py
@@ -321,24 +321,27 @@
     return pltpu.with_memory_space_constraint(array, pltpu.HBM)
 
 
-def pair_sum_kernel(arrived, *halves):
+def pair_sum_kernel(arrived, whole, *halves):
     count = NBLK * NBLK // 2
     for i, half in enumerate(halves):
 
         @pl.loop(0, count // 8)
         def _(n):
             pairs = arrived[pl.ds(i * count + n * 8, 8)].astype(F32)
-            half[pl.ds(n * 8, 8)] = (pairs[:, 0] + pairs[:, 1]).astype(BF16)
+            total = (pairs[:, 0] + pairs[:, 1]).astype(BF16)
+            whole[pl.ds(i * count + n * 8, 8)] = total
+            half[pl.ds(n * 8, 8)] = total
 
 
 def pair_sum(arrived):
     vector = pl.BlockSpec(memory_space=pltpu.VMEM)
     half = jax.ShapeDtypeStruct((NBLK * NBLK // 2, QUARTER, LANES), BF16)
+    whole = jax.ShapeDtypeStruct((NBLK * NBLK, QUARTER, LANES), BF16)
     return pl.pallas_call(
         pair_sum_kernel,
-        out_shape=[half] * 2,
+        out_shape=[whole, half, half],
         in_specs=[vector],
-        out_specs=[vector] * 2,
+        out_specs=[vector] * 3,
         compiler_params=pltpu.CompilerParams(vmem_limit_bytes=24 * 1024 * 1024),
         name="pair_sum",
     )(arrived)
@@ -361,7 +364,8 @@
 
 
 def mixture_kernel(own, by_core, by_x, by_both, left, fold, mixture, products):
-    mix((own, by_core, by_x, by_both), left, fold, products, mixture)
+    first = pl.ds(0, NBLK // 2)
+    mix((own.at[first], by_core.at[first], by_x, by_both), left, fold, products, mixture)
 
 
 def mixture_half(quarters, left, fold):
@@ -382,7 +386,8 @@
     own, by_core, by_x, by_both, half_mixture, left, fold, taper_rows, taper_cols, right, out_hbm,
     mixture, products, image, sems,
 ):
-    mix((own, by_core, by_x, by_both), left, fold, products, mixture)
+    second = pl.ds(NBLK // 2, NBLK // 2)
+    mix((own.at[second], by_core.at[second], by_x, by_both), left, fold, products, mixture)
 
     def departures(chunk):
         copies = []
@@ -460,11 +465,12 @@
     total = (keep.astype(F32) + got.astype(F32)).astype(BF16)
     outgoing = total.reshape(NBLK * NBLK * 2, QUARTER, LANES)
     arrived = lax.all_to_all(outgoing, ("grid", "x_lo"), split_axis=0, concat_axis=0, tiled=True)
-    halves = [half.reshape(NBLK // 2, ROWS, LANES) for half in pair_sum(arrived.reshape(NBLK * NBLK, 2, QUARTER, LANES))]
-    by_core = [swap(half, "core") for half in halves]
-    by_x = [swap(half, "x_lo") for half in halves]
+    own, *halves = pair_sum(arrived.reshape(NBLK * NBLK, 2, QUARTER, LANES))
+    own = own.reshape(NBLK, ROWS, LANES)
+    by_x = [swap(half.reshape(NBLK // 2, ROWS, LANES), "x_lo") for half in halves]
+    by_core = swap(own, "core")
     by_both = [swap(half, "core") for half in by_x]
-    first, second = zip(halves, by_core, by_x, by_both)
+    first, second = ((own, by_core, *pair) for pair in zip(by_x, by_both))
     half_mixture = mixture_half(first, left, fold)
     return facet(second, half_mixture, left, fold, taper_rows, taper_cols, right)[None]
 

time: 58.2 us -> 59.6 us (1.024)
  starting transfers between devices: 12.1 us -> 13.5 us
    ppermute x7 -> x6, starting transfers between devices: 12.1 us -> 13.5 us  [swap(): return lax.ppermute(array, axis, [(0, 1), (1, 0)])]
  transfers between devices with their start and end apart: 7 -> 6, of which waited for: 2 -> 2; matrix products, arithmetic and copies ran while one was open for 0% -> 0% of each run, Pallas kernels for 3% -> 3%
where the time goes in v9:
time: 59.6 us; the launch traced here: 59.4 us
  blocking collectives  30.9 us (52%)
  Pallas kernels  13.9 us (23%)
  starting transfers between devices  13.5 us (23%)
  waiting for transfers between devices  0.95 us (2%)
    all_to_all x1, blocking collectives, shards(): lax.all_to_all(outgoing, ('grid', 'x_lo'), split_axis=0, concat_axis=0, t...  30.9 us
    ppermute x6, starting transfers between devices, swap(): return lax.ppermute(array, axis, [(0, 1), (1, 0)])  13.5 us
    pallas_call x1, Pallas kernels, gridding(): pl.pallas_call(gridding_kernel, out_shape=[half] + [jax.ShapeDtypeStruct(...  9.29 us
    pallas_call x1, Pallas kernels, facet(): pl.pallas_call(facet_kernel, out_shape=jax.ShapeDtypeStruct((2, ROWS_OUT,...  2.94 us
  transfers between devices with their start and end apart: 6, of which 2 were waited for; matrix products, arithmetic and copies ran while one was open for 0% of the time, Pallas kernels for 3%

profile of v9, /device:TPU:1, one launch (start us, length us, event | category | flops | bytes accessed | tf_op | source)
XLA Modules:
  0.0 59.4 jit_solution(2392836046698222543)
XLA Ops:
  0.0 9.3 %gridding.1 = (bf16[8,256,128]{2,1,0:T(8,128)(2,1)S(1)}, bf16[4,128,256]{2,1,0:T(8,128)(2,1)S(1)}, bf16[4,256,1024]{2,1,0:T(8,128)(2,1)S(1)}, bf16[512,512]{1,0:...) custom-call(s32[1]{0:T(128)} %bitcast.place_ref, ...), custom_call_target="tpu_custom_call" | custom-call | tf_op jit(solution)/shard_map/gridding/pallas_call | solution.py:289
  9.3 3.3 %collective-permute-start = (bf16[8,256,128]{2,1,0:T(8,128)(2,1)S(1)}, bf16[8,256,128]{2,1,0:T(8,128)(2,1)S(1)}, u32[]{:S(2)}, u32[]{:S(2)}) collective-permute-start(bf16[8,256,128]{2,1,0:T(8,128)(2,1)S(1)} %get-tuple-element.18), channel_id=1, source_target_pairs={{0,1},{1,0},{2,3},{3,2},{4,5},{5,4},{6,7},{7,6},{8,9},{9,8},{10,11... | collective-permute-start | bytes 1572872 | tf_op jit(solution)/shard_map/ppermute | solution.py:454
  12.6 0.8 %keep_half.1 = bf16[8,256,128]{2,1,0:T(8,128)(2,1)S(1)} custom-call(s32[1]{0:T(128)} %bitcast.place_ref, bf16[4,128,256]{2,1,0:T(8,128)(2,1)S(1)} %get-tuple-element.16.rows, bf16[4,256,1024]{2,1,0:T(8,128)(2,1)S(1)} %get-tuple-element.17.stacked), custom_call_target="tpu_custom_call" | custom-call | flops 134217728 | bytes 1048576 | tf_op jit(solution)/shard_map/keep_half/pallas_call | solution.py:273
  13.4 0.7 %collective-permute-done = bf16[8,256,128]{2,1,0:T(8,128)(2,1)S(1)} collective-permute-done((bf16[8,256,128]{2,1,0:T(8,128)(2,1)S(1)}, bf16[8,256,128]{2,1,0:T(8,128)(2,1)S(1)}, u32[]{:S(2)}, u32[]{:S(2)}) %collective-permute-start) | collective-permute-done | bytes 524320 | tf_op jit(solution)/shard_map/ppermute | solution.py:454
  14.2 0.1 add_convert_fusion
  14.3 30.9 %all_to_all.5 = bf16[128,16,128]{2,1,0:T(8,128)(2,1)S(1)} all-to-all(bf16[128,16,128]{2,1,0:T(8,128)(2,1)S(1)} %bitcast.23), channel_id=1, replica_groups=mesh['grid'=64,'x_lo'=2,'core'=2] {'grid','x_lo'}, dimensions={0} | all-to-all | bytes 1048576 | tf_op jit(solution)/shard_map/all_to_all | solution.py:467
  45.2 0.1 pair_sum.1
  45.3 0.1 collective-permute-start.4
  45.4 2.8 %collective-permute-start.1 = (bf16[8,128,128]{2,1,0:T(8,128)(2,1)S(1)}, bf16[8,128,128]{2,1,0:T(8,128)(2,1)S(1)}, u32[]{:S(2)}, u32[]{:S(2)}) collective-permute-start(bf16[8,128,128]{2,1,0:T(8,128)(2,1)S(1)} %bitcast.18), channel_id=1, source_target_pairs={{0,1},{1,0},{2,3},{3,2},{4,5},{5,4},{6,7},{7,6},{8,9},{9,8},{10,11... | collective-permute-start | bytes 786440 | tf_op jit(solution)/shard_map/ppermute | solution.py:454
  48.2 1.2 %collective-permute-start.2 = (bf16[4,128,128]{2,1,0:T(8,128)(2,1)S(1)}, bf16[4,128,128]{2,1,0:T(8,128)(2,1)S(1)}, u32[]{:S(2)}, u32[]{:S(2)}) collective-permute-start(bf16[4,128,128]{2,1,0:T(8,128)(2,1)S(1)} %bitcast.21), channel_id=1, source_target_pairs={{0,2},{2,0},{1,3},{3,1},{4,6},{6,4},{5,7},{7,5},{8,10},{10,8},{9,1... | collective-permute-start | bytes 393224 | tf_op jit(solution)/shard_map/ppermute | solution.py:454
  49.5 0.0 collective-permute-done.4.by_x
  49.5 4.6 %collective-permute-start.5 = (bf16[4,128,128]{2,1,0:T(8,128)(2,1)S(1)}, bf16[4,128,128]{2,1,0:T(8,128)(2,1)S(1)}, u32[]{:S(2)}, u32[]{:S(2)}) collective-permute-start(bf16[4,128,128]{2,1,0:T(8,128)(2,1)S(1)} %collective-permute-done.4.by_x), channel_id=1, source_target_pairs={{0,1},{1,0},{2,3},{3,2},{4,5},{5,4},{6,7},{7,6},{8,9},{9,8},{10,11... | collective-permute-start | bytes 393224 | tf_op jit(solution)/shard_map/ppermute | solution.py:454
  54.1 0.0 collective-permute-done.2.by_x
  54.1 1.5 %collective-permute-start.3 = (bf16[4,128,128]{2,1,0:T(8,128)(2,1)S(1)}, bf16[4,128,128]{2,1,0:T(8,128)(2,1)S(1)}, u32[]{:S(2)}, u32[]{:S(2)}) collective-permute-start(bf16[4,128,128]{2,1,0:T(8,128)(2,1)S(1)} %collective-permute-done.2.by_x), channel_id=1, source_target_pairs={{0,1},{1,0},{2,3},{3,2},{4,5},{5,4},{6,7},{7,6},{8,9},{9,8},{10,11... | collective-permute-start | bytes 393224 | tf_op jit(solution)/shard_map/ppermute | solution.py:454
  55.5 0.0 collective-permute-done.1.by_core
  55.5 0.0 collective-permute-done.5.by_both
  55.5 0.8 %mixture_half.1.half_mixture = bf16[2,256,256]{2,1,0:T(8,128)(2,1)S(1)} custom-call(bf16[8,128,128]{2,1,0:T(8,128)(2,1)S(1)} %bitcast.19, bf16[8,128,128]{2,1,0:T(8,128)(2,1)S(1)} %collective-permute-done.1.by_core, bf16[4,128,128]{2,1,0:T(8,128)(2,1)S(1)} %collective-permute-done.4.by_x, bf16[4,128,128]{2,1,0:T(8,128)(2,1)S(1)} %collective-permute-done.5.by_both, ...), custom_call_target="tpu_custom_call" | custom-call | flops 268435456 | bytes 1048576 | tf_op jit(solution)/shard_map/mixture_half/pallas_call | solution.py:373
  56.3 0.2 collective-permute-done.3.by_both
  56.5 2.9 %facet.1 = f32[2,256,1024]{2,1,0:T(8,128)} custom-call(bf16[8,128,128]{2,1,0:T(8,128)(2,1)S(1)} %bitcast.20, bf16[8,128,128]{2,1,0:T(8,128)(2,1)S(1)} %collective-permute-done.1.by_core, bf16[4,128,128]{2,1,0:T(8,128)(2,1)S(1)} %collective-permute-done.2.by_x, bf16[4,128,128]{2,1,0:T(8,128)(2,1)S(1)} %collective-permute-done.3.by_both, ...), custom_call_target="tpu_custom_call" | custom-call | tf_op jit(solution)/shard_map/facet/pallas_call | solution.py:429
Async XLA Ops:
  9.3 4.9 %collective-permute-start = (bf16[8,256,128]{2,1,0:T(8,128)(2,1)S(1)}, bf16[8,256,128]{2,1,0:T(8,128)(2,1)S(1)}, u32[]{:S(2)}, u32[]{:S(2)}) collective-permute-start(bf16[8,256,128]{2,1,0:T(8,128)(2,1)S(1)} %get-tuple-element.18), channel_id=1, source_target_pairs={{0,1},{1,0},{2,3},{3,2},{4,5},{5,4},{6,7},{7,6},{8,9},{9,8},{10,11... | collective-permute-start | bytes 1572872 | tf_op jit(solution)/shard_map/ppermute | solution.py:454
  45.3 4.2 %collective-permute-start.4 = (bf16[4,128,128]{2,1,0:T(8,128)(2,1)S(1)}, bf16[4,128,128]{2,1,0:T(8,128)(2,1)S(1)}, u32[]{:S(2)}, u32[]{:S(2)}) collective-permute-start(bf16[4,128,128]{2,1,0:T(8,128)(2,1)S(1)} %bitcast.22), channel_id=1, source_target_pairs={{0,2},{2,0},{1,3},{3,1},{4,6},{6,4},{5,7},{7,5},{8,10},{10,8},{9,1... | collective-permute-start | bytes 393224 | tf_op jit(solution)/shard_map/ppermute | solution.py:454
  45.4 10.1 %collective-permute-start.1 = (bf16[8,128,128]{2,1,0:T(8,128)(2,1)S(1)}, bf16[8,128,128]{2,1,0:T(8,128)(2,1)S(1)}, u32[]{:S(2)}, u32[]{:S(2)}) collective-permute-start(bf16[8,128,128]{2,1,0:T(8,128)(2,1)S(1)} %bitcast.18), channel_id=1, source_target_pairs={{0,1},{1,0},{2,3},{3,2},{4,5},{5,4},{6,7},{7,6},{8,9},{9,8},{10,11... | collective-permute-start | bytes 786440 | tf_op jit(solution)/shard_map/ppermute | solution.py:454
  48.2 5.8 %collective-permute-start.2 = (bf16[4,128,128]{2,1,0:T(8,128)(2,1)S(1)}, bf16[4,128,128]{2,1,0:T(8,128)(2,1)S(1)}, u32[]{:S(2)}, u32[]{:S(2)}) collective-permute-start(bf16[4,128,128]{2,1,0:T(8,128)(2,1)S(1)} %bitcast.21), channel_id=1, source_target_pairs={{0,2},{2,0},{1,3},{3,1},{4,6},{6,4},{5,7},{7,5},{8,10},{10,8},{9,1... | collective-permute-start | bytes 393224 | tf_op jit(solution)/shard_map/ppermute | solution.py:454
  49.5 6.0 %collective-permute-start.5 = (bf16[4,128,128]{2,1,0:T(8,128)(2,1)S(1)}, bf16[4,128,128]{2,1,0:T(8,128)(2,1)S(1)}, u32[]{:S(2)}, u32[]{:S(2)}) collective-permute-start(bf16[4,128,128]{2,1,0:T(8,128)(2,1)S(1)} %collective-permute-done.4.by_x), channel_id=1, source_target_pairs={{0,1},{1,0},{2,3},{3,2},{4,5},{5,4},{6,7},{7,6},{8,9},{9,8},{10,11... | collective-permute-start | bytes 393224 | tf_op jit(solution)/shard_map/ppermute | solution.py:454
  54.1 2.4 %collective-permute-start.3 = (bf16[4,128,128]{2,1,0:T(8,128)(2,1)S(1)}, bf16[4,128,128]{2,1,0:T(8,128)(2,1)S(1)}, u32[]{:S(2)}, u32[]{:S(2)}) collective-permute-start(bf16[4,128,128]{2,1,0:T(8,128)(2,1)S(1)} %collective-permute-done.2.by_x), channel_id=1, source_target_pairs={{0,1},{1,0},{2,3},{3,2},{4,5},{5,4},{6,7},{7,6},{8,9},{9,8},{10,11... | collective-permute-start | bytes 393224 | tf_op jit(solution)/shard_map/ppermute | solution.py:454
